TPU v7x, 32 devices: a whole 2x2x4 slice. The times are simulated.
32 devices in a mesh: dp: 8 (over z, y), mod: 4 (over x, core).
Axes of the slice: x: 2, y: 2, z: 4, core: 2. Of those that a mesh axis runs over, the one named last changes fastest.
Arguments:
- embeddings: bfloat16 [4, 2048, 512], P('mod', 'dp'), may hold values from -4 to 4
- pairings: int32 [3, 4], replicated, may hold values from 0 to 3, as said below
- logit_scale: float32 [3], replicated, may hold values from 2 to 6
Outputs:
- gradient: float32 [4, 2048, 512], P('mod', 'dp')
- losses: float32 [4, 2048], P('mod', 'dp')
Inputs may be any that keep to these rules, and one draw needn't show every extreme that they name: Row k of pairings maps each modality to its partner in matching k; each row is an involution without fixed points, and the three rows are the three perfect matchings of the four modalities in some order.
All inputs are finite; a program needn't handle non-finite values.
Results may differ from a plain program's by a relative error of at most 0.0013.
Values may be sent and summed in bfloat16 or wider, within the bound.
No kernel may reach another device: no remote copies, remote signals or barrier semaphores. Data moves between devices by JAX's collectives and lax.ppermute only.
A program may use at most 192 MiB of HBM per device.

v0:
```python
import jax
import jax.numpy as jnp
from jax import lax
from jax.sharding import PartitionSpec as P


def shards(embeddings, pairings, logit_scale):
    row_count = embeddings.shape[1]
    feat_width = embeddings.shape[2]
    mod_index = lax.axis_index("mod")
    anchor = embeddings[0]
    local_set = lax.all_gather(embeddings, "mod", axis=0, tiled=True)
    gradient = jnp.zeros((row_count, feat_width), jnp.float32)
    losses = jnp.zeros((row_count,), jnp.float32)
    for matching in range(3):
        partner_id = pairings[matching][mod_index]
        factor = logit_scale[matching]
        own_rows = lax.dynamic_index_in_dim(local_set, partner_id, 0, keepdims=False)
        partner = lax.all_gather(own_rows, "dp", axis=0, tiled=True)
        scores = factor * lax.dot_general(
            anchor, partner, (((1,), (1,)), ((), ())), preferred_element_type=jnp.float32
        )
        row_max = jnp.max(scores, 1, keepdims=True)
        row_lse = row_max[:, 0] + jnp.log(jnp.sum(jnp.exp(scores - row_max), 1))
        col_max = lax.pmax(jnp.max(scores, 0).astype(jnp.bfloat16), "dp").astype(jnp.float32)
        col_sum = lax.psum(jnp.sum(jnp.exp(scores - col_max[None, :]), 0), "dp")
        col_lse = col_max + jnp.log(col_sum)
        weights = (jnp.exp(scores - row_lse[:, None]) + jnp.exp(scores - col_lse[None, :])).astype(
            jnp.bfloat16
        )
        product = jnp.dot(weights, partner, preferred_element_type=jnp.float32)
        own_float = own_rows.astype(jnp.float32)
        diagonal = factor * jnp.sum(anchor.astype(jnp.float32) * own_float, -1)
        gradient = gradient + factor * (product - 2.0 * own_float)
        losses = losses + (row_lse - diagonal)
    return (gradient[None], losses[None])


def solution(mesh):
    return jax.shard_map(
        shards,
        mesh=mesh,
        in_specs=(P("mod", "dp", None), P(), P()),
        out_specs=(P("mod", "dp", None), P("mod", "dp")),
        check_vma=False,
    )
```

profile of v0, /device:TPU:0, one launch (start us, length us, event | category | flops | bytes accessed | tf_op | source)
XLA Modules:
  0.0 275.8 jit_solution(15326653770826481865)
XLA Ops:
  7.2 0.0 copy-start.3
  7.2 0.0 all-gather.8.cloned.1.call-start
  7.2 0.7 all-gather.8.cloned.1.call-update
  7.9 0.0 all-gather.10.cloned.1.call-start
  8.0 0.8 fusion.51
  8.8 0.6 constant_dynamic-slice_fusion.1
  11.9 0.7 constant_dynamic-slice_fusion.5
  16.0 13.0 %all-gather.8.cloned.1.call-done = bf16[4,256,512]{2,1,0:T(8,128)(2,1)} async-done(((bf16[1,256,512]{2,1,0:T(8,128)(2,1)}), bf16[4,256,512]{2,1,0:T(8,128)(2,1)}) %all-gather.8.cloned.1.call-update) | async-done | bytes 1048592 | tf_op jit(solution)/shard_map/all_gather | solution.py:12
  29.0 2.1 fusion.42
  31.2 0.0 all-gather.10.cloned.1.call-update
  31.2 0.0 all-gather.14.cloned.1.call-start
  31.3 0.7 all-gather.14.cloned.1.call-update
  31.9 0.0 all-gather.12.cloned.1.call-start
  32.0 0.5 all-gather.12.cloned.1.call-update
  32.5 0.6 fusion.52
  33.1 47.5 %all-gather.10.cloned.1.call-done = bf16[1,2048,512]{2,1,0:T(8,128)(2,1)} async-done(((bf16[1,256,512]{2,1,0:T(8,128)(2,1)}), bf16[1,2048,512]{2,1,0:T(8,128)(2,1)}) %all-gather.10.cloned.1.call-update) | async-done | bytes 2097168 | tf_op jit(solution)/shard_map/all_gather | solution.py:19
  80.7 4.4 %fusion.50 = (f32[256]{0:T(256)S(1)}, bf16[2048]{0:T(1024)(128)(2,1)S(1)}, f32[2048,256]{1,0:T(8,128)}) fusion(bf16[1,256,512]{2,1,0:T(8,128)(2,1)S(1)} %copy-done.3, bf16[1,2048,512]{2,1,0:T(8,128)(2,1)} %all-gather.10.cloned.1.call-done, f32[]{:T(128)} %bitcast), kind=kOutput, calls=%fused_computation.63 | convolution fusion | flops 538441472 | bytes 4461572 | tf_op jit(solution)/shard_map/dot_general | solution.py:20
  85.0 46.2 %all-gather.14.cloned.1.call-done = bf16[1,2048,512]{2,1,0:T(8,128)(2,1)} async-done(((bf16[1,256,512]{2,1,0:T(8,128)(2,1)}), bf16[1,2048,512]{2,1,0:T(8,128)(2,1)}) %all-gather.14.cloned.1.call-update) | async-done | bytes 2097168 | tf_op jit(solution)/shard_map/all_gather | solution.py:19
  131.2 3.0 %fusion.48 = (f32[256]{0:T(256)S(1)}, bf16[2048]{0:T(1024)(128)(2,1)S(1)}, f32[2048,256]{1,0:T(8,128)S(1)}) fusion(bf16[1,256,512]{2,1,0:T(8,128)(2,1)S(1)} %copy-done.3, bf16[1,2048,512]{2,1,0:T(8,128)(2,1)} %all-gather.14.cloned.1.call-done, f32[]{:T(128)} %bitcast.9), kind=kOutput, calls=%fused_computation.61 | convolution fusion | flops 538441472 | bytes 4461572 | tf_op jit(solution)/shard_map/dot_general | solution.py:20
  134.1 46.8 %all-gather.12.cloned.1.call-done = bf16[1,2048,512]{2,1,0:T(8,128)(2,1)} async-done(((bf16[1,256,512]{2,1,0:T(8,128)(2,1)}), bf16[1,2048,512]{2,1,0:T(8,128)(2,1)}) %all-gather.12.cloned.1.call-update) | async-done | bytes 2097168 | tf_op jit(solution)/shard_map/all_gather | solution.py:19
  181.0 4.3 %fusion.49 = (f32[256]{0:T(256)S(1)}, bf16[2048]{0:T(1024)(128)(2,1)S(1)}, f32[2048,256]{1,0:T(8,128)}) fusion(bf16[1,256,512]{2,1,0:T(8,128)(2,1)S(1)} %copy-done.3, bf16[1,2048,512]{2,1,0:T(8,128)(2,1)} %all-gather.12.cloned.1.call-done, f32[]{:T(128)} %bitcast.5), kind=kOutput, calls=%fused_computation.62 | convolution fusion | flops 538441472 | bytes 4461572 | tf_op jit(solution)/shard_map/dot_general | solution.py:20
  185.3 34.6 %all-reduce.1 = (bf16[2048]{0:T(1024)(128)(2,1)S(1)}, bf16[2048]{0:T(1024)(128)(2,1)S(1)}, bf16[2048]{0:T(1024)(128)(2,1)S(1)}) all-reduce(bf16[2048]{0:T(1024)(128)(2,1)S(1)} %get-tuple-element.13, bf16[2048]{0:T(1024)(128)(2,1)S(1)} %get-tuple-element.9, ...), channel_id=1, replica_groups=mesh['dp'=8,'mod'=4] {'dp'}, use_global_device_ids=true, to_apply=%region_3.4 | all-reduce | flops 6144 | bytes 24576 | tf_op jit(solution)/shard_map/pmax | solution.py:25
  220.0 0.9 exponential_reduce_fusion.1
  220.9 0.6 copy-done.1
  221.5 0.9 exponential_reduce_fusion.3
  222.5 0.9 exponential_reduce_fusion.5
  223.4 33.1 %all-reduce = (f32[2048]{0:T(1024)S(1)}, f32[2048]{0:T(1024)S(1)}, f32[2048]{0:T(1024)S(1)}) all-reduce(f32[2048]{0:T(1024)S(1)} %get-tuple-element.11, f32[2048]{0:T(1024)S(1)} %get-tuple-element.7, f32[2048]{0:T(1024)S(1)} %get-tuple-element.3), channel_id=1, replica_groups=mesh['dp'=8,'mod'=4] {'dp'}, use_global_device_ids=true, to_apply=%region_5.6 | all-reduce | flops 6144 | bytes 49152 | tf_op jit(solution)/shard_map/psum | solution.py:26
  256.5 2.4 subtract_add_fusion
  259.0 5.0 %fusion.12 = f32[256,512]{1,0:T(8,128)S(1)} fusion(bf16[1,2048,512]{2,1,0:T(8,128)(2,1)} %all-gather.10.cloned.1.call-done, f32[2048,256]{1,0:T(8,128)} %get-tuple-element.36, f32[2048]{0:T(1024)S(1)} %log_add_fusion.2, f32[256]{0:T(256)S(1)} %get-tuple-element.26, bf16[1,256,512]{2,1,0:T(8,128)(2,1)S(1)} %copy-done.6, f32[]{:T(128)} %bitcast), kind=kOutput, calls=%fused_computation.22 | convolution fusion | flops 539492352 | bytes 4989956 | tf_op jit(solution)/shard_map/dot_general | solution.py:31
  264.0 0.0 copy-start.4
  264.0 2.3 fusion.33
  266.4 2.9 %fusion.30 = f32[1,256,512]{2,1,0:T(8,128)} fusion(f32[256,512]{1,0:T(8,128)S(1)} %fusion.33, bf16[1,2048,512]{2,1,0:T(8,128)(2,1)S(1)} %copy-done.8, f32[2048,256]{1,0:T(8,128)S(1)} %get-tuple-element.38, f32[2048]{0:T(1024)S(1)} %log_add_fusion, f32[256]{0:T(256)S(1)} %get-tuple-element.24, bf16[1,256,512]{2,1,0:T(8,128)(2,1)S(1)} %copy-done.4, f32[]{:T(128)} %bitcast.9), kind=kOutput, calls=%fused_computation.28 | convolution fusion | flops 539623424 | bytes 5514244 | tf_op jit(solution)/shard_map/dot_general | solution.py:31
  (23 shorter events, 0.1 us)
Async XLA Ops:
  7.2 73.5 %copy-start.3 = (bf16[1,256,512]{2,1,0:T(8,128)(2,1)S(1)}, bf16[1,256,512]{2,1,0:T(8,128)(2,1)}, u32[]{:S(2)}) copy-start(bf16[1,256,512]{2,1,0:T(8,128)(2,1)} %param.3) | copy-start | bytes 786436
  7.2 25.3 %copy-start.7 = (f32[3]{0:T(128)S(1)}, f32[3]{0:T(128)}, u32[]{:S(2)}) copy-start(f32[3]{0:T(128)} %param.5) | copy-start | bytes 40
  7.2 21.8 %all-gather.8.cloned.1.call-start = ((), (), s32[]{:S(2)}) async-start(), calls=%async_computation | async-start | bytes 1310720 | tf_op jit(solution)/shard_map/all_gather | solution.py:12
  7.9 72.7 %all-gather.10.cloned.1.call-start = ((), (), s32[]{:S(2)}) async-start(), calls=%async_computation.1 | async-start | bytes 2359296 | tf_op jit(solution)/shard_map/all_gather | solution.py:19
  31.2 100.0 %all-gather.14.cloned.1.call-start = ((), (), s32[]{:S(2)}) async-start(), calls=%async_computation.3 | async-start | bytes 2359296 | tf_op jit(solution)/shard_map/all_gather | solution.py:19
  31.9 149.0 %all-gather.12.cloned.1.call-start = ((), (), s32[]{:S(2)}) async-start(), calls=%async_computation.2 | async-start | bytes 2359296 | tf_op jit(solution)/shard_map/all_gather | solution.py:19
  219.9 1.6 copy-start.1
  220.0 2.5 copy-start
  221.5 37.4 %copy-start.6 = (bf16[1,256,512]{2,1,0:T(8,128)(2,1)S(1)}, bf16[1,256,512]{2,1,0:T(8,128)(2,1)}, u32[]{:S(2)}) copy-start(bf16[1,256,512]{2,1,0:T(8,128)(2,1)} %get-tuple-element.29) | copy-start | bytes 786436
  259.0 5.0 %copy-start.2 = (f32[2048,256]{1,0:T(8,128)S(1)}, f32[2048,256]{1,0:T(8,128)}, u32[]{:S(2)}) copy-start(f32[2048,256]{1,0:T(8,128)} %get-tuple-element.37) | copy-start | bytes 6291460
  259.0 5.0 %copy-start.5 = (bf16[1,256,512]{2,1,0:T(8,128)(2,1)S(1)}, bf16[1,256,512]{2,1,0:T(8,128)(2,1)}, u32[]{:S(2)}) copy-start(bf16[1,256,512]{2,1,0:T(8,128)(2,1)} %get-tuple-element.28) | copy-start | bytes 786436
  259.0 5.0 %copy-start.9 = (bf16[1,2048,512]{2,1,0:T(8,128)(2,1)S(1)}, bf16[1,2048,512]{2,1,0:T(8,128)(2,1)}, u32[]{:S(2)}) copy-start(bf16[1,2048,512]{2,1,0:T(8,128)(2,1)} %all-gather.12.cloned.1.call-done) | copy-start | bytes 6291460
  264.0 2.3 copy-start.4
  264.0 2.3 copy-start.8
Sparse Core Ops, SparseCore 0:
  9.6 19.4 all-gather.7
  31.3 49.2 all-gather.9
  83.4 47.7 all-gather.13
  133.2 47.7 all-gather.11
where the time goes:
time: 276 us
  waiting for transfers between devices  155 us (56%)
  blocking collectives  67.7 us (25%)
  matrix products  21.9 us (8%)
  between operations  19.9 us (7%)
  other arithmetic  7.43 us (3%)
  local copies, waits for them, and re-layouts  3.31 us (1%)
    all_gather x3, waiting for transfers between devices, shards(): partner = lax.all_gather(own_rows, 'dp', axis=0, tiled=True)  141 us
    pmax x1, blocking collectives, shards(): lax.pmax(jnp.max(scores, 0).astype(jnp.bfloat16), 'dp').astype(jnp.float32)  34.6 us
    psum x1, blocking collectives, shards(): col_sum = lax.psum(jnp.sum(jnp.exp(scores - col_max[None, :]), 0), 'dp')  33.1 us
    all_gather x1, waiting for transfers between devices, shards(): local_set = lax.all_gather(embeddings, 'mod', axis=0, tiled=True)  13 us
    dot_general x3, matrix products, shards(): lax.dot_general(anchor, partner, (((1,), (1,)), ((), ())), preferred_elem...  11.7 us
    dot_general x3, matrix products, shards(): product = jnp.dot(weights, partner, preferred_element_type=jnp.float32)  10.2 us
  transfers between devices with their start and end apart: 4, of which 4 were waited for; matrix products, arithmetic and copies ran while one was open for 4% of the time, Pallas kernels for 0%

commit v1 on v0

v1 whole, which is shorter than its diff:
```python
import functools
import math

import jax
import jax.numpy as jnp
from jax import lax
from jax.experimental import pallas as pl
from jax.experimental.pallas import tpu as pltpu
from jax.sharding import PartitionSpec as P

LOG2E = math.log2(math.e)
TILE = 256
NT = (((1,), (1,)), ((), ()))


def fold(x):
    return x.reshape(x.shape[0] // 8, 8, x.shape[1])


def scores(rows, cols):
    return lax.dot_general(rows, cols, NT, preferred_element_type=jnp.float32)


def fetch_all(refs, scratch, sems):
    size = refs[0].shape[0]
    copies = []
    for i, ref in enumerate(refs):
        copy = pltpu.make_async_copy(ref, scratch.at[pl.ds(i * size, size)], sems.at[i])
        copy.start()
        copies.append(copy)
    return copies


def col_kernel(n_cols, factor_ref, *refs):
    row_refs, col_refs = refs[:8], refs[8 : 8 + n_cols]
    out_ref, rows, cols, row_sems, col_sems = refs[8 + n_cols :]
    size = row_refs[0].shape[0]
    copies = fetch_all(row_refs, rows, row_sems) + fetch_all(col_refs, cols, col_sems)
    for copy in copies:
        copy.wait()
    chunks = rows.shape[0] // TILE
    per_block = size // TILE

    def body(j, _):
        block = cols[pl.ds(pl.multiple_of(j * TILE, TILE), TILE), :]
        scale = factor_ref[j // (8 * per_block)] * LOG2E

        def group(g, carry):
            top, total = carry
            for i in range(8):
                start = pl.multiple_of(g * (8 * TILE) + i * TILE, TILE)
                s = fold(scores(rows[pl.ds(start, TILE), :], block))
                new = jnp.maximum(top, jnp.max(s, 0))
                shift = new * scale
                total = total * jnp.exp2(top * scale - shift) + jnp.sum(jnp.exp2(s * scale - shift[None]), 0)
                top = new
            return top, total

        carry = (jnp.full((8, TILE), -1e30, jnp.float32), jnp.zeros((8, TILE), jnp.float32))
        if chunks == 8:
            top, total = group(0, carry)
        else:
            top, total = lax.fori_loop(0, chunks // 8, group, carry)
        best = jnp.max(top, 0, keepdims=True)
        total = jnp.sum(total * jnp.exp2((top - best) * scale), 0, keepdims=True)
        out_ref[j] = best * scale + jnp.log2(total)
        return 0

    lax.fori_loop(0, cols.shape[0] // TILE, body, 0)


def col_stats(factors, rows, cols):
    size, width = rows[0].shape
    n_cols = len(cols)
    n_tiles = n_cols * size // TILE
    need = (8 + n_cols) * size * width * 2
    work = 8 * size * n_cols * size
    return pl.pallas_call(
        functools.partial(col_kernel, n_cols),
        out_shape=jax.ShapeDtypeStruct((n_tiles, 1, TILE), jnp.float32),
        in_specs=[pl.BlockSpec(memory_space=pltpu.SMEM)] + [pl.BlockSpec(memory_space=pl.ANY)] * (8 + n_cols),
        out_specs=pl.BlockSpec(memory_space=pltpu.VMEM),
        scratch_shapes=[
            pltpu.VMEM((8 * size, width), jnp.bfloat16),
            pltpu.VMEM((n_cols * size, width), jnp.bfloat16),
            pltpu.SemaphoreType.DMA((8,)),
            pltpu.SemaphoreType.DMA((n_cols,)),
        ],
        compiler_params=pltpu.CompilerParams(vmem_limit_bytes=need + (12 << 20)),
        cost_estimate=pl.CostEstimate(flops=2 * work * width, bytes_accessed=need, transcendentals=work),
        name="col_stats",
    )(factors, *rows, *cols)


def final_kernel(factor_ref, own_ref, pown1, pown2, pown3, lse_ref, *refs):
    col_refs = refs[:24]
    grad_ref, loss_ref, cols, prob, colprob, sems = refs[24:]
    size = col_refs[0].shape[0]
    groups = size // TILE
    copies = fetch_all(col_refs, cols, sems)
    own = own_ref[...]
    own_float = own.astype(jnp.float32)
    grad = jnp.zeros(own.shape, jnp.float32)
    loss = jnp.zeros((own.shape[0], 1), jnp.float32)
    n = own.shape[0]

    def loop(f, carry):
        if groups == 1:
            for i in range(8):
                carry = f(i, carry)
            return carry

        def eight(g, c):
            for i in range(8):
                c = f(g * 8 + i, c)
            return c

        return lax.fori_loop(0, groups, eight, carry)

    for pair, pown_ref in enumerate((pown1, pown2, pown3)):
        slot = pair if groups == 1 else 0
        factor = factor_ref[pair]
        scale = factor * LOG2E
        for copy in copies[8 * pair : 8 * pair + 8]:
            copy.wait()

        def block_of(j):
            return cols[pl.ds(pl.multiple_of((pair * 8 * groups + j) * TILE, TILE), TILE), :]

        def first(j, top):
            s = scores(own, block_of(j))
            prob[slot, j] = s
            return jnp.maximum(top, jnp.maximum(s[:, :128], s[:, 128:]))

        top = loop(first, jnp.full((n, 128), -1e30, jnp.float32))
        best = jnp.max(top, 1, keepdims=True) * scale

        def second(j, total):
            s = prob[slot, j] * scale
            p = jnp.exp2(s - best)
            prob[slot, j] = p
            colprob[slot, j] = jnp.exp2(s - lse_ref[pair * 8 * groups + j])
            return total + p[:, :128] + p[:, 128:]

        total = jnp.sum(loop(second, jnp.zeros((n, 128), jnp.float32)), 1, keepdims=True)
        inverse = 1.0 / total

        def third(j, acc):
            w = (prob[slot, j] * inverse + colprob[slot, j]).astype(jnp.bfloat16)
            return acc + jnp.dot(w, block_of(j), preferred_element_type=jnp.float32)

        product = loop(third, jnp.zeros(own.shape, jnp.float32))
        partner = pown_ref[...].astype(jnp.float32)
        grad = grad + factor * (product - 2.0 * partner)
        diagonal = factor * jnp.sum(own_float * partner, 1, keepdims=True)
        loss = loss + (best * (1.0 / LOG2E) + jnp.log(total) - diagonal)
    grad_ref[...] = grad
    loss_ref[...] = jnp.transpose(jnp.broadcast_to(loss, (n, 128)))[:8, :]


def final(factors, own, pown, lse, cols):
    n, width = own.shape
    size = cols[0].shape[0]
    groups = size // TILE
    slots = 3 if groups == 1 else 1
    need = 24 * size * width * 2 + slots * 8 * groups * n * TILE * 8
    vmem = pl.BlockSpec(memory_space=pltpu.VMEM)
    return pl.pallas_call(
        final_kernel,
        out_shape=(jax.ShapeDtypeStruct((n, width), jnp.float32), jax.ShapeDtypeStruct((8, n), jnp.float32)),
        in_specs=[pl.BlockSpec(memory_space=pltpu.SMEM)] + [vmem] * 5 + [pl.BlockSpec(memory_space=pl.ANY)] * 24,
        out_specs=(vmem, vmem),
        scratch_shapes=[
            pltpu.VMEM((24 * size, width), jnp.bfloat16),
            pltpu.VMEM((slots, 8 * groups, n, TILE), jnp.float32),
            pltpu.VMEM((slots, 8 * groups, n, TILE), jnp.float32),
            pltpu.SemaphoreType.DMA((24,)),
        ],
        compiler_params=pltpu.CompilerParams(vmem_limit_bytes=need + (12 << 20)),
        cost_estimate=pl.CostEstimate(flops=4 * n * 24 * size * width, bytes_accessed=need, transcendentals=2 * n * 24 * size),
        name="weights_and_gradient",
    )(factors, own, *pown, lse, *cols)


def shards(n_dp, embeddings, pairings, logit_scale):
    own = embeddings[0]
    n = own.shape[0]
    group = n_dp // 8
    dp_index = lax.axis_index("dp")
    mod_index = lax.axis_index("mod")

    def send(block, dp_xor, mod_xor):
        pairs = [
            (d * 4 + m, (d ^ (dp_xor * group)) * 4 + (m ^ mod_xor)) for d in range(n_dp) for m in range(4)
        ]
        return lax.ppermute(block, ("dp", "mod"), pairs)

    block = own
    if group > 1:
        members = [[g * group + i for i in range(group)] for g in range(8)]
        block = lax.all_gather(own, "dp", axis=0, tiled=True, axis_index_groups=members)

    e = [[None] * 8 for _ in range(4)]
    e[0][0] = block
    e[2][0] = send(e[0][0], 0, 2)
    e[0][1] = send(e[0][0], 1, 0)
    e[0][2] = send(e[0][0], 2, 0)
    e[0][4] = send(e[0][0], 4, 0)
    e[2][1] = send(e[0][1], 0, 2)
    e[0][3] = send(e[0][2], 1, 0)
    e[0][6] = send(e[0][4], 2, 0)
    e[2][4] = send(e[0][4], 0, 2)
    e[0][5] = send(e[0][4], 1, 0)
    e[2][2] = send(e[2][0], 2, 0)
    e[2][6] = send(e[0][6], 0, 2)
    e[0][7] = send(e[0][6], 1, 0)
    e[2][5] = send(e[0][5], 0, 2)
    e[2][3] = send(e[2][1], 2, 0)
    e[2][7] = send(e[2][6], 1, 0)
    for a in range(8):
        e[1][a] = send(e[0][a], 0, 1)
        e[3][a] = send(e[2][a], 0, 1)

    partner_ids = lax.dynamic_index_in_dim(pairings, mod_index, 1, keepdims=False)
    factors = jnp.stack(
        [jnp.sum(jnp.where(partner_ids == (mod_index ^ m), logit_scale, 0.0)) for m in (1, 2, 3)]
    )
    pown = [e[m][0] for m in (1, 2, 3)]
    if group > 1:
        start = (dp_index % group) * n
        pown = [lax.dynamic_slice_in_dim(x, start, n, 0) for x in pown]
    cols = e[1] + e[2] + e[3]
    lse = col_stats(factors, e[0], cols)
    gradient, losses = final(factors, own, pown, lse, cols)
    return gradient[None], losses[:1]


def solution(mesh):
    return jax.shard_map(
        functools.partial(shards, mesh.shape["dp"]),
        mesh=mesh,
        in_specs=(P("mod", "dp", None), P(), P()),
        out_specs=(P("mod", "dp", None), P("mod", "dp")),
        check_vma=False,
    )
```

time: 276 us -> 105 us (0.38)
  waiting for transfers between devices: 155 us -> 27.6 us
  blocking collectives: 67.7 us -> 0 us
  Pallas kernels: 0 us -> 32.3 us
  starting transfers between devices: 0.16 us -> 24.3 us
  matrix products: 21.9 us -> 0 us
  between operations: 19.9 us -> 0.85 us
  local copies, waits for them, and re-layouts: 3.31 us -> 16.1 us
  other arithmetic: 7.43 us -> 2.87 us
    all_gather x4 -> x0, waiting for transfers between devices: 154 us -> none  [the longest x3 141 us: shards(): partner = lax.all_gather(own_rows, 'dp', axis=0, tiled=True)]
    pmax x1 -> x0, blocking collectives: 34.6 us -> none  [shards(): lax.pmax(jnp.max(scores, 0).astype(jnp.bfloat16), 'dp').astype(jnp.float32)]
    psum x1 -> x0, blocking collectives: 33.1 us -> none  [shards(): col_sum = lax.psum(jnp.sum(jnp.exp(scores - col_max[None, :]), 0), 'dp')]
    pallas_call x0 -> x2, Pallas kernels: none -> 32.3 us  [the longest x1 24 us: col_stats(): pl.pallas_call(functools.partial(col_kernel, n_cols), out_shape=jax.Shape...]
    ppermute x0 -> x31, waiting for transfers between devices: none -> 27.6 us  [send(): return lax.ppermute(block, ('dp', 'mod'), pairs)]
    ppermute x0 -> x31, starting transfers between devices: none -> 24.3 us  [send(): return lax.ppermute(block, ('dp', 'mod'), pairs)]
    dot_general x6 -> x0, matrix products: 21.9 us -> none  [the longest x3 11.7 us: shards(): lax.dot_general(anchor, partner, (((1,), (1,)), ((), ())), preferred_elem...]
    unnamed x20 -> x56, local copies, waits for them, and re-layouts: 0.66 us -> 15.6 us
  transfers between devices with their start and end apart: 4 -> 31, of which waited for: 4 -> 9; matrix products, arithmetic and copies ran while one was open for 4% -> 3% of each run, Pallas kernels for 0% -> 0%
where the time goes in v1:
time: 105 us; the launch traced here: 104 us
  Pallas kernels  32.3 us (31%)
  waiting for transfers between devices  27.6 us (26%)
  starting transfers between devices  24.3 us (23%)
  local copies, waits for them, and re-layouts  16.1 us (15%)
  other arithmetic  2.87 us (3%)
    ppermute x31, waiting for transfers between devices, send(): return lax.ppermute(block, ('dp', 'mod'), pairs)  27.6 us
    ppermute x31, starting transfers between devices, send(): return lax.ppermute(block, ('dp', 'mod'), pairs)  24.3 us
    pallas_call x1, Pallas kernels, col_stats(): pl.pallas_call(functools.partial(col_kernel, n_cols), out_shape=jax.Shape...  24 us
    unnamed x56, local copies, waits for them, and re-layouts  15.6 us
    pallas_call x1, Pallas kernels, final(): pl.pallas_call(final_kernel, out_shape=(jax.ShapeDtypeStruct((n, width),...  8.28 us
  transfers between devices with their start and end apart: 31, of which 9 were waited for; matrix products, arithmetic and copies ran while one was open for 3% of the time, Pallas kernels for 0%

profile of v1, /device:TPU:0, one launch (start us, length us, event | category | flops | bytes accessed | tf_op | source)
XLA Modules:
  0.0 104.0 jit_solution(13390548681076602705)
XLA Ops:
  0.6 4.1 %collective-permute-start.6 = (bf16[256,512]{1,0:T(8,128)(2,1)}, bf16[256,512]{1,0:T(8,128)(2,1)S(1)}, u32[]{:S(2)}, u32[]{:S(2)}) collective-permute-start(bf16[256,512]{1,0:T(8,128)(2,1)} %bitcast.5), channel_id=1, source_target_pairs={{0,16},{1,17},{2,18},{3,19},{4,20},{5,21},{6,22},{7,23},{8,24},{9,... | collective-permute-start | bytes 786440 | tf_op jit(solution)/shard_map/ppermute | solution.py:196
  4.7 1.6 %collective-permute-start.4 = (bf16[256,512]{1,0:T(8,128)(2,1)}, bf16[256,512]{1,0:T(8,128)(2,1)S(1)}, u32[]{:S(2)}, u32[]{:S(2)}) collective-permute-start(bf16[256,512]{1,0:T(8,128)(2,1)} %bitcast.6), channel_id=1, source_target_pairs={{0,8},{1,9},{2,10},{3,11},{4,12},{5,13},{6,14},{7,15},{8,0},{9,1},... | collective-permute-start | bytes 786440 | tf_op jit(solution)/shard_map/ppermute | solution.py:196
  6.3 1.5 %collective-permute-start.3 = (bf16[256,512]{1,0:T(8,128)(2,1)}, bf16[256,512]{1,0:T(8,128)(2,1)S(1)}, u32[]{:S(2)}, u32[]{:S(2)}) collective-permute-start(bf16[256,512]{1,0:T(8,128)(2,1)} %bitcast.7), channel_id=1, source_target_pairs={{0,4},{1,5},{2,6},{3,7},{4,0},{5,1},{6,2},{7,3},{8,12},{9,13},{10,... | collective-permute-start | bytes 786440 | tf_op jit(solution)/shard_map/ppermute | solution.py:196
  7.8 1.5 %collective-permute-start.1 = (bf16[256,512]{1,0:T(8,128)(2,1)}, bf16[256,512]{1,0:T(8,128)(2,1)S(1)}, u32[]{:S(2)}, u32[]{:S(2)}) collective-permute-start(bf16[256,512]{1,0:T(8,128)(2,1)} %bitcast.8), channel_id=1, source_target_pairs={{0,2},{1,3},{2,0},{3,1},{4,6},{5,7},{6,4},{7,5},{8,10},{9,11},{10,... | collective-permute-start | bytes 786440 | tf_op jit(solution)/shard_map/ppermute | solution.py:196
  9.3 7.7 %collective-permute-done.6.refs_4_ = bf16[256,512]{1,0:T(8,128)(2,1)S(1)} collective-permute-done((bf16[256,512]{1,0:T(8,128)(2,1)}, bf16[256,512]{1,0:T(8,128)(2,1)S(1)}, u32[]{:S(2)}, u32[]{:S(2)}) %collective-permute-start.6) | collective-permute-done | bytes 262176 | tf_op jit(solution)/shard_map/ppermute | solution.py:196
  17.0 1.5 %collective-permute-start.20 = (bf16[256,512]{1,0:T(8,128)(2,1)S(1)}, bf16[256,512]{1,0:T(8,128)(2,1)S(1)}, u32[]{:S(2)}, u32[]{:S(2)}) collective-permute-start(bf16[256,512]{1,0:T(8,128)(2,1)S(1)} %collective-permute-done.6.refs_4_), channel_id=1, source_target_pairs={{0,2},{1,3},{2,0},{3,1},{4,6},{5,7},{6,4},{7,5},{8,10},{9,11},{10,... | collective-permute-start | bytes 786440 | tf_op jit(solution)/shard_map/ppermute | solution.py:196
  19.3 1.5 %collective-permute-start.7 = (bf16[256,512]{1,0:T(8,128)(2,1)S(1)}, bf16[256,512]{1,0:T(8,128)(2,1)S(1)}, u32[]{:S(2)}, u32[]{:S(2)}) collective-permute-start(bf16[256,512]{1,0:T(8,128)(2,1)S(1)} %collective-permute-done.6.refs_4_), channel_id=1, source_target_pairs={{0,4},{1,5},{2,6},{3,7},{4,0},{5,1},{6,2},{7,3},{8,12},{9,13},{10,... | collective-permute-start | bytes 786440 | tf_op jit(solution)/shard_map/ppermute | solution.py:196
  20.8 3.6 %collective-permute-done.20.refs_20_.refs_12_ = bf16[256,512]{1,0:T(8,128)(2,1)S(1)} collective-permute-done((bf16[256,512]{1,0:T(8,128)(2,1)S(1)}, bf16[256,512]{1,0:T(8,128)(2,1)S(1)}, u32[]{:S(2)}, u32[]{:S(2)}) %collective-permute-start.20) | collective-permute-done | bytes 262176 | tf_op jit(solution)/shard_map/ppermute | solution.py:196
  24.4 1.3 %collective-permute-start.5 = (bf16[256,512]{1,0:T(8,128)(2,1)S(1)}, bf16[256,512]{1,0:T(8,128)(2,1)S(1)}, u32[]{:S(2)}, u32[]{:S(2)}) collective-permute-start(bf16[256,512]{1,0:T(8,128)(2,1)S(1)} %collective-permute-done.4.refs_2_), channel_id=1, source_target_pairs={{0,4},{1,5},{2,6},{3,7},{4,0},{5,1},{6,2},{7,3},{8,12},{9,13},{10,... | collective-permute-start | bytes 786440 | tf_op jit(solution)/shard_map/ppermute | solution.py:196
  25.7 1.5 %collective-permute-start.17 = (bf16[256,512]{1,0:T(8,128)(2,1)S(1)}, bf16[256,512]{1,0:T(8,128)(2,1)S(1)}, u32[]{:S(2)}, u32[]{:S(2)}) collective-permute-start(bf16[256,512]{1,0:T(8,128)(2,1)S(1)} %collective-permute-done.3.refs_1_), channel_id=1, source_target_pairs={{0,2},{1,3},{2,0},{3,1},{4,6},{5,7},{6,4},{7,5},{8,10},{9,11},{10,... | collective-permute-start | bytes 786440 | tf_op jit(solution)/shard_map/ppermute | solution.py:196
  27.2 1.2 %collective-permute-done.7.refs_5_ = bf16[256,512]{1,0:T(8,128)(2,1)S(1)} collective-permute-done((bf16[256,512]{1,0:T(8,128)(2,1)S(1)}, bf16[256,512]{1,0:T(8,128)(2,1)S(1)}, u32[]{:S(2)}, u32[]{:S(2)}) %collective-permute-start.7) | collective-permute-done | bytes 262176 | tf_op jit(solution)/shard_map/ppermute | solution.py:196
  28.4 1.4 %collective-permute-start.18 = (bf16[256,512]{1,0:T(8,128)(2,1)S(1)}, bf16[256,512]{1,0:T(8,128)(2,1)S(1)}, u32[]{:S(2)}, u32[]{:S(2)}) collective-permute-start(bf16[256,512]{1,0:T(8,128)(2,1)S(1)} %collective-permute-done.1.refs_16_.pown2.refs_8_), channel_id=1, source_target_pairs={{0,8},{1,9},{2,10},{3,11},{4,12},{5,13},{6,14},{7,15},{8,0},{9,1},... | collective-permute-start | bytes 786440 | tf_op jit(solution)/shard_map/ppermute | solution.py:196
  29.8 3.5 %collective-permute-done.5.refs_3_ = bf16[256,512]{1,0:T(8,128)(2,1)S(1)} collective-permute-done((bf16[256,512]{1,0:T(8,128)(2,1)S(1)}, bf16[256,512]{1,0:T(8,128)(2,1)S(1)}, u32[]{:S(2)}, u32[]{:S(2)}) %collective-permute-start.5) | collective-permute-done | bytes 262176 | tf_op jit(solution)/shard_map/ppermute | solution.py:196
  33.3 1.0 collective-permute-start.22
  34.4 1.5 %collective-permute-done.18.refs_18_.refs_10_ = bf16[256,512]{1,0:T(8,128)(2,1)S(1)} collective-permute-done((bf16[256,512]{1,0:T(8,128)(2,1)S(1)}, bf16[256,512]{1,0:T(8,128)(2,1)S(1)}, u32[]{:S(2)}, u32[]{:S(2)}) %collective-permute-start.18) | collective-permute-done | bytes 262176 | tf_op jit(solution)/shard_map/ppermute | solution.py:196
  36.0 1.5 %collective-permute-start.9 = (bf16[256,512]{1,0:T(8,128)(2,1)S(1)}, bf16[256,512]{1,0:T(8,128)(2,1)}, u32[]{:S(2)}, u32[]{:S(2)}) collective-permute-start(bf16[256,512]{1,0:T(8,128)(2,1)S(1)} %collective-permute-done.8.refs_6_), channel_id=1, source_target_pairs={{0,4},{1,5},{2,6},{3,7},{4,0},{5,1},{6,2},{7,3},{8,12},{9,13},{10,... | collective-permute-start | bytes 786440 | tf_op jit(solution)/shard_map/ppermute | solution.py:196
  39.4 3.0 %collective-permute-done.22.refs_22_.refs_14_ = bf16[256,512]{1,0:T(8,128)(2,1)} collective-permute-done((bf16[256,512]{1,0:T(8,128)(2,1)S(1)}, bf16[256,512]{1,0:T(8,128)(2,1)}, u32[]{:S(2)}, u32[]{:S(2)}) %collective-permute-start.22) | collective-permute-done | bytes 262176 | tf_op jit(solution)/shard_map/ppermute | solution.py:196
  43.7 1.4 %collective-permute-start.19 = (bf16[256,512]{1,0:T(8,128)(2,1)S(1)}, bf16[256,512]{1,0:T(8,128)(2,1)}, u32[]{:S(2)}, u32[]{:S(2)}) collective-permute-start(bf16[256,512]{1,0:T(8,128)(2,1)S(1)} %collective-permute-done.17.refs_17_.refs_9_), channel_id=1, source_target_pairs={{0,8},{1,9},{2,10},{3,11},{4,12},{5,13},{6,14},{7,15},{8,0},{9,1},... | collective-permute-start | bytes 786440 | tf_op jit(solution)/shard_map/ppermute | solution.py:196
  45.1 2.7 %collective-permute-done.21.refs_21_.refs_13_ = bf16[256,512]{1,0:T(8,128)(2,1)} collective-permute-done((bf16[256,512]{1,0:T(8,128)(2,1)S(1)}, bf16[256,512]{1,0:T(8,128)(2,1)}, u32[]{:S(2)}, u32[]{:S(2)}) %collective-permute-start.21) | collective-permute-done | bytes 262176 | tf_op jit(solution)/shard_map/ppermute | solution.py:196
  49.1 1.5 %collective-permute-start.23 = (bf16[256,512]{1,0:T(8,128)(2,1)}, bf16[256,512]{1,0:T(8,128)(2,1)}, u32[]{:S(2)}, u32[]{:S(2)}) collective-permute-start(bf16[256,512]{1,0:T(8,128)(2,1)} %collective-permute-done.22.refs_22_.refs_14_), channel_id=1, source_target_pairs={{0,4},{1,5},{2,6},{3,7},{4,0},{5,1},{6,2},{7,3},{8,12},{9,13},{10,... | collective-permute-start | bytes 786440 | tf_op jit(solution)/shard_map/ppermute | solution.py:196
  53.8 4.4 %collective-permute-done.23.refs_23_.refs_15_ = bf16[256,512]{1,0:T(8,128)(2,1)} collective-permute-done((bf16[256,512]{1,0:T(8,128)(2,1)}, bf16[256,512]{1,0:T(8,128)(2,1)}, u32[]{:S(2)}, u32[]{:S(2)}) %collective-permute-start.23) | collective-permute-done | bytes 262176 | tf_op jit(solution)/shard_map/ppermute | solution.py:196
  60.4 2.0 %pad_maximum_fusion.factor_ref = f32[3]{0:T(128)S(1)} fusion(f32[1]{0:T(128)} %bitcast.2, f32[1]{0:T(128)} %bitcast.1, f32[1]{0:T(128)} %bitcast), kind=kLoop, calls=%fused_computation.3 | loop fusion | flops 6 | bytes 24 | tf_op jit(solution)/shard_map/stack | solution.py:225
  63.4 0.9 copy-done.3
  64.3 0.9 copy-done.6
  65.3 0.9 copy-done.9
  66.2 0.9 copy-done.12
  67.2 0.9 copy-done.15
  68.1 0.9 copy-done.18
  69.1 0.9 copy-done.21
  70.0 0.9 copy-done.24
  71.0 24.0 %col_stats.1.lse_ref = f32[24,1,256]{2,1,0:T(1,128)S(1)} custom-call(f32[3]{0:T(128)S(1)} %pad_maximum_fusion.factor_ref, bf16[256,512]{1,0:T(8,128)(2,1)S(1)} %bitcast.10, bf16[256,512]{1,0:T(8,128)(2,1)S(1)} %collective-permute-done.3.refs_1_, bf16[256,512]{1,0:T(8,128)(2,1)S(1)} %collective-permute-done.4.refs_2_, ...), custom_call_target="tpu_custom_call" | custom-call | flops 12884901888 | bytes 8388608 | tf_op jit(solution)/shard_map/col_stats/pallas_call | solution.py:78
  95.1 8.3 %weights_and_gradient.1 = (f32[256,512]{1,0:T(8,128)}, f32[8,256]{1,0:T(8,128)S(1)}) custom-call(f32[3]{0:T(128)S(1)} %pad_maximum_fusion.factor_ref, bf16[256,512]{1,0:T(8,128)(2,1)S(1)} %bitcast.11, bf16[256,512]{1,0:T(8,128)(2,1)S(1)} %collective-permute-done.refs_8_.pown1.refs_0_, bf16[256,512]{1,0:T(8,128)(2,1)S(1)} %collective-permute-done.1.refs_16_.pown2.refs_8_, ...), custom_call_target="tpu_custom_call" | custom-call | flops 3221225472 | bytes 18874368 | tf_op jit(solution)/shard_map/weights_and_gradient/pallas_call | solution.py:168
  (92 shorter events, 12.6 us)
Async XLA Ops:
  0.6 16.3 %collective-permute-start.6 = (bf16[256,512]{1,0:T(8,128)(2,1)}, bf16[256,512]{1,0:T(8,128)(2,1)S(1)}, u32[]{:S(2)}, u32[]{:S(2)}) collective-permute-start(bf16[256,512]{1,0:T(8,128)(2,1)} %bitcast.5), channel_id=1, source_target_pairs={{0,16},{1,17},{2,18},{3,19},{4,20},{5,21},{6,22},{7,23},{8,24},{9,... | collective-permute-start | bytes 786440 | tf_op jit(solution)/shard_map/ppermute | solution.py:196
  4.7 13.8 %collective-permute-start.4 = (bf16[256,512]{1,0:T(8,128)(2,1)}, bf16[256,512]{1,0:T(8,128)(2,1)S(1)}, u32[]{:S(2)}, u32[]{:S(2)}) collective-permute-start(bf16[256,512]{1,0:T(8,128)(2,1)} %bitcast.6), channel_id=1, source_target_pairs={{0,8},{1,9},{2,10},{3,11},{4,12},{5,13},{6,14},{7,15},{8,0},{9,1},... | collective-permute-start | bytes 786440 | tf_op jit(solution)/shard_map/ppermute | solution.py:196
  6.3 12.2 %collective-permute-start.3 = (bf16[256,512]{1,0:T(8,128)(2,1)}, bf16[256,512]{1,0:T(8,128)(2,1)S(1)}, u32[]{:S(2)}, u32[]{:S(2)}) collective-permute-start(bf16[256,512]{1,0:T(8,128)(2,1)} %bitcast.7), channel_id=1, source_target_pairs={{0,4},{1,5},{2,6},{3,7},{4,0},{5,1},{6,2},{7,3},{8,12},{9,13},{10,... | collective-permute-start | bytes 786440 | tf_op jit(solution)/shard_map/ppermute | solution.py:196
  7.8 11.4 %collective-permute-start.1 = (bf16[256,512]{1,0:T(8,128)(2,1)}, bf16[256,512]{1,0:T(8,128)(2,1)S(1)}, u32[]{:S(2)}, u32[]{:S(2)}) collective-permute-start(bf16[256,512]{1,0:T(8,128)(2,1)} %bitcast.8), channel_id=1, source_target_pairs={{0,2},{1,3},{2,0},{3,1},{4,6},{5,7},{6,4},{7,5},{8,10},{9,11},{10,... | collective-permute-start | bytes 786440 | tf_op jit(solution)/shard_map/ppermute | solution.py:196
  9.3 11.5 %collective-permute-start = (bf16[256,512]{1,0:T(8,128)(2,1)}, bf16[256,512]{1,0:T(8,128)(2,1)S(1)}, u32[]{:S(2)}, u32[]{:S(2)}) collective-permute-start(bf16[256,512]{1,0:T(8,128)(2,1)} %bitcast.9), channel_id=1, source_target_pairs={{0,1},{1,0},{2,3},{3,2},{4,5},{5,4},{6,7},{7,6},{8,9},{9,8},{10,11... | collective-permute-start | bytes 786440 | tf_op jit(solution)/shard_map/ppermute | solution.py:196
  17.0 7.4 %collective-permute-start.20 = (bf16[256,512]{1,0:T(8,128)(2,1)S(1)}, bf16[256,512]{1,0:T(8,128)(2,1)S(1)}, u32[]{:S(2)}, u32[]{:S(2)}) collective-permute-start(bf16[256,512]{1,0:T(8,128)(2,1)S(1)} %collective-permute-done.6.refs_4_), channel_id=1, source_target_pairs={{0,2},{1,3},{2,0},{3,1},{4,6},{5,7},{6,4},{7,5},{8,10},{9,11},{10,... | collective-permute-start | bytes 786440 | tf_op jit(solution)/shard_map/ppermute | solution.py:196
  18.5 7.2 %collective-permute-start.13 = (bf16[256,512]{1,0:T(8,128)(2,1)S(1)}, bf16[256,512]{1,0:T(8,128)(2,1)S(1)}, u32[]{:S(2)}, u32[]{:S(2)}) collective-permute-start(bf16[256,512]{1,0:T(8,128)(2,1)S(1)} %collective-permute-done.6.refs_4_), channel_id=1, source_target_pairs={{0,1},{1,0},{2,3},{3,2},{4,5},{5,4},{6,7},{7,6},{8,9},{9,8},{10,11... | collective-permute-start | bytes 786440 | tf_op jit(solution)/shard_map/ppermute | solution.py:196
  18.5 8.7 %collective-permute-start.8 = (bf16[256,512]{1,0:T(8,128)(2,1)S(1)}, bf16[256,512]{1,0:T(8,128)(2,1)S(1)}, u32[]{:S(2)}, u32[]{:S(2)}) collective-permute-start(bf16[256,512]{1,0:T(8,128)(2,1)S(1)} %collective-permute-done.6.refs_4_), channel_id=1, source_target_pairs={{0,8},{1,9},{2,10},{3,11},{4,12},{5,13},{6,14},{7,15},{8,0},{9,1},... | collective-permute-start | bytes 786440 | tf_op jit(solution)/shard_map/ppermute | solution.py:196
  19.3 9.2 %collective-permute-start.7 = (bf16[256,512]{1,0:T(8,128)(2,1)S(1)}, bf16[256,512]{1,0:T(8,128)(2,1)S(1)}, u32[]{:S(2)}, u32[]{:S(2)}) collective-permute-start(bf16[256,512]{1,0:T(8,128)(2,1)S(1)} %collective-permute-done.6.refs_4_), channel_id=1, source_target_pairs={{0,4},{1,5},{2,6},{3,7},{4,0},{5,1},{6,2},{7,3},{8,12},{9,13},{10,... | collective-permute-start | bytes 786440 | tf_op jit(solution)/shard_map/ppermute | solution.py:196
  20.8 9.0 %collective-permute-start.11 = (bf16[256,512]{1,0:T(8,128)(2,1)S(1)}, bf16[256,512]{1,0:T(8,128)(2,1)S(1)}, u32[]{:S(2)}, u32[]{:S(2)}) collective-permute-start(bf16[256,512]{1,0:T(8,128)(2,1)S(1)} %collective-permute-done.4.refs_2_), channel_id=1, source_target_pairs={{0,1},{1,0},{2,3},{3,2},{4,5},{5,4},{6,7},{7,6},{8,9},{9,8},{10,11... | collective-permute-start | bytes 786440 | tf_op jit(solution)/shard_map/ppermute | solution.py:196
  24.4 8.8 %collective-permute-start.5 = (bf16[256,512]{1,0:T(8,128)(2,1)S(1)}, bf16[256,512]{1,0:T(8,128)(2,1)S(1)}, u32[]{:S(2)}, u32[]{:S(2)}) collective-permute-start(bf16[256,512]{1,0:T(8,128)(2,1)S(1)} %collective-permute-done.4.refs_2_), channel_id=1, source_target_pairs={{0,4},{1,5},{2,6},{3,7},{4,0},{5,1},{6,2},{7,3},{8,12},{9,13},{10,... | collective-permute-start | bytes 786440 | tf_op jit(solution)/shard_map/ppermute | solution.py:196
  25.7 7.6 %collective-permute-start.17 = (bf16[256,512]{1,0:T(8,128)(2,1)S(1)}, bf16[256,512]{1,0:T(8,128)(2,1)S(1)}, u32[]{:S(2)}, u32[]{:S(2)}) collective-permute-start(bf16[256,512]{1,0:T(8,128)(2,1)S(1)} %collective-permute-done.3.refs_1_), channel_id=1, source_target_pairs={{0,2},{1,3},{2,0},{3,1},{4,6},{5,7},{6,4},{7,5},{8,10},{9,11},{10,... | collective-permute-start | bytes 786440 | tf_op jit(solution)/shard_map/ppermute | solution.py:196
  27.2 7.0 %collective-permute-start.10 = (bf16[256,512]{1,0:T(8,128)(2,1)S(1)}, bf16[256,512]{1,0:T(8,128)(2,1)S(1)}, u32[]{:S(2)}, u32[]{:S(2)}) collective-permute-start(bf16[256,512]{1,0:T(8,128)(2,1)S(1)} %collective-permute-done.3.refs_1_), channel_id=1, source_target_pairs={{0,1},{1,0},{2,3},{3,2},{4,5},{5,4},{6,7},{7,6},{8,9},{9,8},{10,11... | collective-permute-start | bytes 786440 | tf_op jit(solution)/shard_map/ppermute | solution.py:196
  28.4 7.5 %collective-permute-start.18 = (bf16[256,512]{1,0:T(8,128)(2,1)S(1)}, bf16[256,512]{1,0:T(8,128)(2,1)S(1)}, u32[]{:S(2)}, u32[]{:S(2)}) collective-permute-start(bf16[256,512]{1,0:T(8,128)(2,1)S(1)} %collective-permute-done.1.refs_16_.pown2.refs_8_), channel_id=1, source_target_pairs={{0,8},{1,9},{2,10},{3,11},{4,12},{5,13},{6,14},{7,15},{8,0},{9,1},... | collective-permute-start | bytes 786440 | tf_op jit(solution)/shard_map/ppermute | solution.py:196
  29.8 7.7 %collective-permute-start.2 = (bf16[256,512]{1,0:T(8,128)(2,1)S(1)}, bf16[256,512]{1,0:T(8,128)(2,1)S(1)}, u32[]{:S(2)}, u32[]{:S(2)}) collective-permute-start(bf16[256,512]{1,0:T(8,128)(2,1)S(1)} %collective-permute-done.1.refs_16_.pown2.refs_8_), channel_id=1, source_target_pairs={{0,1},{1,0},{2,3},{3,2},{4,5},{5,4},{6,7},{7,6},{8,9},{9,8},{10,11... | collective-permute-start | bytes 786440 | tf_op jit(solution)/shard_map/ppermute | solution.py:196
  33.3 5.5 %collective-permute-start.27 = (bf16[256,512]{1,0:T(8,128)(2,1)S(1)}, bf16[256,512]{1,0:T(8,128)(2,1)S(1)}, u32[]{:S(2)}, u32[]{:S(2)}) collective-permute-start(bf16[256,512]{1,0:T(8,128)(2,1)S(1)} %collective-permute-done.20.refs_20_.refs_12_), channel_id=1, source_target_pairs={{0,1},{1,0},{2,3},{3,2},{4,5},{5,4},{6,7},{7,6},{8,9},{9,8},{10,11... | collective-permute-start | bytes 786440 | tf_op jit(solution)/shard_map/ppermute | solution.py:196
  33.3 9.2 %collective-permute-start.22 = (bf16[256,512]{1,0:T(8,128)(2,1)S(1)}, bf16[256,512]{1,0:T(8,128)(2,1)}, u32[]{:S(2)}, u32[]{:S(2)}) collective-permute-start(bf16[256,512]{1,0:T(8,128)(2,1)S(1)} %collective-permute-done.8.refs_6_), channel_id=1, source_target_pairs={{0,2},{1,3},{2,0},{3,1},{4,6},{5,7},{6,4},{7,5},{8,10},{9,11},{10,... | collective-permute-start | bytes 786440 | tf_op jit(solution)/shard_map/ppermute | solution.py:196
  34.2 8.3 %collective-permute-start.15 = (bf16[256,512]{1,0:T(8,128)(2,1)S(1)}, bf16[256,512]{1,0:T(8,128)(2,1)S(1)}, u32[]{:S(2)}, u32[]{:S(2)}) collective-permute-start(bf16[256,512]{1,0:T(8,128)(2,1)S(1)} %collective-permute-done.8.refs_6_), channel_id=1, source_target_pairs={{0,1},{1,0},{2,3},{3,2},{4,5},{5,4},{6,7},{7,6},{8,9},{9,8},{10,11... | collective-permute-start | bytes 786440 | tf_op jit(solution)/shard_map/ppermute | solution.py:196
  36.0 7.7 %collective-permute-start.9 = (bf16[256,512]{1,0:T(8,128)(2,1)S(1)}, bf16[256,512]{1,0:T(8,128)(2,1)}, u32[]{:S(2)}, u32[]{:S(2)}) collective-permute-start(bf16[256,512]{1,0:T(8,128)(2,1)S(1)} %collective-permute-done.8.refs_6_), channel_id=1, source_target_pairs={{0,4},{1,5},{2,6},{3,7},{4,0},{5,1},{6,2},{7,3},{8,12},{9,13},{10,... | collective-permute-start | bytes 786440 | tf_op jit(solution)/shard_map/ppermute | solution.py:196
  38.2 9.5 %collective-permute-start.21 = (bf16[256,512]{1,0:T(8,128)(2,1)S(1)}, bf16[256,512]{1,0:T(8,128)(2,1)}, u32[]{:S(2)}, u32[]{:S(2)}) collective-permute-start(bf16[256,512]{1,0:T(8,128)(2,1)S(1)} %collective-permute-done.7.refs_5_), channel_id=1, source_target_pairs={{0,2},{1,3},{2,0},{3,1},{4,6},{5,7},{6,4},{7,5},{8,10},{9,11},{10,... | collective-permute-start | bytes 786440 | tf_op jit(solution)/shard_map/ppermute | solution.py:196
  39.4 9.0 %collective-permute-start.14 = (bf16[256,512]{1,0:T(8,128)(2,1)S(1)}, bf16[256,512]{1,0:T(8,128)(2,1)S(1)}, u32[]{:S(2)}, u32[]{:S(2)}) collective-permute-start(bf16[256,512]{1,0:T(8,128)(2,1)S(1)} %collective-permute-done.7.refs_5_), channel_id=1, source_target_pairs={{0,1},{1,0},{2,3},{3,2},{4,5},{5,4},{6,7},{7,6},{8,9},{9,8},{10,11... | collective-permute-start | bytes 786440 | tf_op jit(solution)/shard_map/ppermute | solution.py:196
  42.5 8.2 %collective-permute-start.12 = (bf16[256,512]{1,0:T(8,128)(2,1)S(1)}, bf16[256,512]{1,0:T(8,128)(2,1)S(1)}, u32[]{:S(2)}, u32[]{:S(2)}) collective-permute-start(bf16[256,512]{1,0:T(8,128)(2,1)S(1)} %collective-permute-done.5.refs_3_), channel_id=1, source_target_pairs={{0,1},{1,0},{2,3},{3,2},{4,5},{5,4},{6,7},{7,6},{8,9},{9,8},{10,11... | collective-permute-start | bytes 786440 | tf_op jit(solution)/shard_map/ppermute | solution.py:196
  43.2 8.4 %collective-permute-start.24 = (bf16[256,512]{1,0:T(8,128)(2,1)S(1)}, bf16[256,512]{1,0:T(8,128)(2,1)S(1)}, u32[]{:S(2)}, u32[]{:S(2)}) collective-permute-start(bf16[256,512]{1,0:T(8,128)(2,1)S(1)} %collective-permute-done.17.refs_17_.refs_9_), channel_id=1, source_target_pairs={{0,1},{1,0},{2,3},{3,2},{4,5},{5,4},{6,7},{7,6},{8,9},{9,8},{10,11... | collective-permute-start | bytes 786440 | tf_op jit(solution)/shard_map/ppermute | solution.py:196
  43.7 8.9 %collective-permute-start.19 = (bf16[256,512]{1,0:T(8,128)(2,1)S(1)}, bf16[256,512]{1,0:T(8,128)(2,1)}, u32[]{:S(2)}, u32[]{:S(2)}) collective-permute-start(bf16[256,512]{1,0:T(8,128)(2,1)S(1)} %collective-permute-done.17.refs_17_.refs_9_), channel_id=1, source_target_pairs={{0,8},{1,9},{2,10},{3,11},{4,12},{5,13},{6,14},{7,15},{8,0},{9,1},... | collective-permute-start | bytes 786440 | tf_op jit(solution)/shard_map/ppermute | solution.py:196
  47.7 5.1 %collective-permute-start.25 = (bf16[256,512]{1,0:T(8,128)(2,1)S(1)}, bf16[256,512]{1,0:T(8,128)(2,1)S(1)}, u32[]{:S(2)}, u32[]{:S(2)}) collective-permute-start(bf16[256,512]{1,0:T(8,128)(2,1)S(1)} %collective-permute-done.18.refs_18_.refs_10_), channel_id=1, source_target_pairs={{0,1},{1,0},{2,3},{3,2},{4,5},{5,4},{6,7},{7,6},{8,9},{9,8},{10,11... | collective-permute-start | bytes 786440 | tf_op jit(solution)/shard_map/ppermute | solution.py:196
  49.1 9.0 %collective-permute-start.23 = (bf16[256,512]{1,0:T(8,128)(2,1)}, bf16[256,512]{1,0:T(8,128)(2,1)}, u32[]{:S(2)}, u32[]{:S(2)}) collective-permute-start(bf16[256,512]{1,0:T(8,128)(2,1)} %collective-permute-done.22.refs_22_.refs_14_), channel_id=1, source_target_pairs={{0,4},{1,5},{2,6},{3,7},{4,0},{5,1},{6,2},{7,3},{8,12},{9,13},{10,... | collective-permute-start | bytes 786440 | tf_op jit(solution)/shard_map/ppermute | solution.py:196
  51.3 11.0 %collective-permute-start.29 = (bf16[256,512]{1,0:T(8,128)(2,1)}, bf16[256,512]{1,0:T(8,128)(2,1)}, u32[]{:S(2)}, u32[]{:S(2)}) collective-permute-start(bf16[256,512]{1,0:T(8,128)(2,1)} %collective-permute-done.22.refs_22_.refs_14_), channel_id=1, source_target_pairs={{0,1},{1,0},{2,3},{3,2},{4,5},{5,4},{6,7},{7,6},{8,9},{9,8},{10,11... | collective-permute-start | bytes 786440 | tf_op jit(solution)/shard_map/ppermute | solution.py:196
  52.3 10.1 %collective-permute-start.16 = (bf16[256,512]{1,0:T(8,128)(2,1)}, bf16[256,512]{1,0:T(8,128)(2,1)}, u32[]{:S(2)}, u32[]{:S(2)}) collective-permute-start(bf16[256,512]{1,0:T(8,128)(2,1)} %collective-permute-done.9.refs_7_), channel_id=1, source_target_pairs={{0,1},{1,0},{2,3},{3,2},{4,5},{5,4},{6,7},{7,6},{8,9},{9,8},{10,11... | collective-permute-start | bytes 786440 | tf_op jit(solution)/shard_map/ppermute | solution.py:196
  52.6 9.8 %collective-permute-start.28 = (bf16[256,512]{1,0:T(8,128)(2,1)}, bf16[256,512]{1,0:T(8,128)(2,1)}, u32[]{:S(2)}, u32[]{:S(2)}) collective-permute-start(bf16[256,512]{1,0:T(8,128)(2,1)} %collective-permute-done.21.refs_21_.refs_13_), channel_id=1, source_target_pairs={{0,1},{1,0},{2,3},{3,2},{4,5},{5,4},{6,7},{7,6},{8,9},{9,8},{10,11... | collective-permute-start | bytes 786440 | tf_op jit(solution)/shard_map/ppermute | solution.py:196
  53.5 8.9 %collective-permute-start.26 = (bf16[256,512]{1,0:T(8,128)(2,1)}, bf16[256,512]{1,0:T(8,128)(2,1)}, u32[]{:S(2)}, u32[]{:S(2)}) collective-permute-start(bf16[256,512]{1,0:T(8,128)(2,1)} %collective-permute-done.19.refs_19_.refs_11_), channel_id=1, source_target_pairs={{0,1},{1,0},{2,3},{3,2},{4,5},{5,4},{6,7},{7,6},{8,9},{9,8},{10,11... | collective-permute-start | bytes 786440 | tf_op jit(solution)/shard_map/ppermute | solution.py:196
  58.2 4.3 %collective-permute-start.30 = (bf16[256,512]{1,0:T(8,128)(2,1)}, bf16[256,512]{1,0:T(8,128)(2,1)}, u32[]{:S(2)}, u32[]{:S(2)}) collective-permute-start(bf16[256,512]{1,0:T(8,128)(2,1)} %collective-permute-done.23.refs_23_.refs_15_), channel_id=1, source_target_pairs={{0,1},{1,0},{2,3},{3,2},{4,5},{5,4},{6,7},{7,6},{8,9},{9,8},{10,11... | collective-permute-start | bytes 786440 | tf_op jit(solution)/shard_map/ppermute | solution.py:196
  71.0 24.1 %copy-start.13 = (bf16[256,512]{1,0:T(8,128)(2,1)S(1)}, bf16[256,512]{1,0:T(8,128)(2,1)}, u32[]{:S(2)}) copy-start(bf16[256,512]{1,0:T(8,128)(2,1)} %copy-done.11) | copy-start | bytes 786436
  (27 other events, 208.2 us)

commit v2 on v0

v2 whole, which is shorter than its diff:
```python
import functools
CONFIG = {'route': {'a1': ('a0', 'Y'), 'a2': ('a0', 'Z'), 'a4': ('a0', 'W'), 'b0': ('a0', 'X'), 'b1': ('a1', 'X'), 'a3': ('a2', 'Y'), 'a6': ('a4', 'Z'), 'b4': ('a4', 'X'), 'a5': ('a4', 'Y'), 'b2': ('b0', 'Z'), 'b6': ('a6', 'X'), 'a7': ('a6', 'Y'), 'b3': ('b1', 'Z'), 'b5': ('a5', 'X'), 'b7': ('b6', 'Y')}, 'ties': {'a3': ['b0'], 'a6': ['b1'], 'b4': ['b1'], 'a5': ['a3'], 'b2': ['b1'], 'b6': ['b4'], 'a7': ['a5'], 'b3': ['a7'], 'b5': ['b6'], 'P4': ['b7'], 'P5': ['K1']}, 'packs': {'P1': ['a1', 'a2', 'a4', 'b0'], 'P2': ['a3', 'a6', 'b1'], 'P3': ['a5', 'b4', 'b2'], 'P0': ['a0'], 'P5': ['b6'], 'P6': ['a7'], 'P4': ['b3', 'b5'], 'P7': ['b7']}, 'kernels': {'K1': (['a0', 'a1', 'a2', 'a4', 'a3', 'a6'], ['b0', 'c0', 'c2', 'c4', 'd0']), 'K2': (['a5'], ['c6', 'b4', 'b2']), 'K3': (['a7'], ['d4', 'd2', 'b6', 'd6'])}, 'cost': {'K1': 40, 'K2': 40, 'K3': 40}, 'emit': ['a2', 'a4', 'a1', 'b0', 'b1', 'a3', 'a6', 'b4', 'a5', 'b2', 'b6', 'a7', 'b3', 'b5', 'b7']}
import math

import jax
import jax.numpy as jnp
from jax import lax
from jax.experimental import pallas as pl
from jax.experimental.pallas import tpu as pltpu
from jax.sharding import PartitionSpec as P

LOG2E = math.log2(math.e)
TILE = 256
NT = (((1,), (1,)), ((), ()))
SMEM = pl.BlockSpec(memory_space=pltpu.SMEM)
VMEM = pl.BlockSpec(memory_space=pltpu.VMEM)
LIGHT = pl.CostEstimate(flops=1000, bytes_accessed=1000, transcendentals=0)


def scores(rows, cols):
    return lax.dot_general(rows, cols, NT, preferred_element_type=jnp.float32)


def factor_kernel(pairings_ref, scale_ref, out_ref):
    mine = lax.axis_index("mod")
    for m in (1, 2, 3):
        factor = jnp.float32(0.0)
        for k in range(3):
            factor = factor + jnp.where(pairings_ref[k, mine] == (mine ^ m), scale_ref[k], 0.0)
        out_ref[m - 1] = jnp.full(out_ref.shape[1:], factor, jnp.float32)
        out_ref[m + 2] = jnp.full(out_ref.shape[1:], factor * LOG2E, jnp.float32)


def pair_factors(pairings, logit_scale, size):
    return pl.pallas_call(
        factor_kernel,
        out_shape=jax.ShapeDtypeStruct((6, 8, size), jnp.float32),
        in_specs=[SMEM] * 2,
        out_specs=VMEM,
        compiler_params=pltpu.CompilerParams(vmem_limit_bytes=1 << 20),
        cost_estimate=LIGHT,
        name="pair_factors",
    )(pairings, logit_scale)


def unique(blocks):
    arrays, places = [], []
    for array, slab in blocks:
        for i, known in enumerate(arrays):
            if known is array:
                break
        else:
            i = len(arrays)
            arrays.append(array)
        places.append((i, slab))
    return arrays, places


class Placed:
    def __init__(self, ref, slab, size):
        self.ref, self.start, self.size = ref, slab * size, size

    def all(self):
        return self.ref[pl.ds(self.start, self.size), :]

    def part(self, i):
        return self.ref[pl.ds(pl.multiple_of(self.start + i * TILE, TILE), TILE), :]


def stats_kernel(size, places, n_arrays, plan, n_rows, n_old, order, n_stack, factor_ref, *refs):
    blocks = [Placed(refs[i], slab, size) for i, slab in places]
    rows, cols, stack = blocks[:n_rows], blocks[n_rows : n_rows + len(plan)], blocks[n_rows + len(plan) :]
    refs = refs[n_arrays:]
    old = refs[:2] if n_old else None
    outs = refs[2 if n_old else 0 :]
    for i, block in enumerate(stack):
        outs[-1][i * size : (i + 1) * size, :] = block.all()
    for c, (m, members) in enumerate(plan):
        scale = factor_ref[m + 2]
        if c < n_old:
            top, total = old[0][c], old[1][c]
        else:
            top = jnp.full((8, size), -1e30, jnp.float32)
            total = jnp.zeros((8, size), jnp.float32)
        block = cols[c].all()
        for r in members:

            def chunk(i, carry, r=r, block=block, scale=scale):
                top, total = carry
                s = scores(rows[r].part(i), block)
                s = s.reshape(TILE // 8, 8, size)
                new = jnp.maximum(top, jnp.max(s, 0))
                shift = new * scale
                total = total * jnp.exp2(top * scale - shift) + jnp.sum(jnp.exp2(s * scale[None] - shift[None]), 0)
                return new, total

            if size == TILE:
                top, total = chunk(0, (top, total))
            else:
                top, total = lax.fori_loop(0, size // TILE, chunk, (top, total))
        if order:
            best = jnp.max(top, 0, keepdims=True)
            total = jnp.sum(total * jnp.exp2((top - best) * scale), 0, keepdims=True)
            outs[0][order[c]] = best * scale[:1] + jnp.log2(total)
        else:
            outs[0][c] = top
            outs[1][c] = total


def stats(info, size, rows, cols, plan, old=None, order=None, stack=(), cost=4):
    arrays, places = unique(list(rows) + list(cols) + list(stack))
    width = arrays[0].shape[1]
    n = len(plan)
    n_old = old[0].shape[0] if old else 0
    state = jax.ShapeDtypeStruct((n, 8, size), jnp.float32)
    out = [jax.ShapeDtypeStruct((n, 1, size), jnp.float32)] if order else [state, state]
    if stack:
        out.append(jax.ShapeDtypeStruct((len(stack) * size, width), jnp.bfloat16))
    tiles = sum(len(members) for _, members in plan)
    used = sum(math.prod(x.shape) * 2 for x in arrays) + len(stack) * size * width * 2
    return pl.pallas_call(
        functools.partial(
            stats_kernel, size, tuple(places), len(arrays), plan, len(rows), n_old, order, len(stack)
        ),
        out_shape=tuple(out),
        in_specs=[VMEM] * (1 + len(arrays) + (2 if old else 0)),
        out_specs=tuple([VMEM] * len(out)),
        compiler_params=pltpu.CompilerParams(vmem_limit_bytes=(6 << 20) + (used if size > TILE else 0)),
        cost_estimate=pl.CostEstimate(flops=cost * tiles * size * size * width, bytes_accessed=1000, transcendentals=0),
        name="col_stats",
    )(info, *arrays, *(old or ()))


def pack_kernel(*refs):
    size = refs[0].shape[0]
    for i, ref in enumerate(refs[:-1]):
        refs[-1][i * size : (i + 1) * size, :] = ref[...]


def pack(*blocks):
    size, width = blocks[0].shape
    return pl.pallas_call(
        pack_kernel,
        out_shape=jax.ShapeDtypeStruct((len(blocks) * size, width), blocks[0].dtype),
        in_specs=[VMEM] * len(blocks),
        out_specs=VMEM,
        compiler_params=pltpu.CompilerParams(vmem_limit_bytes=(2 << 20) + (len(blocks) * size * width * 4 if size > TILE else 0)),
        cost_estimate=LIGHT,
        name="pack",
    )(*blocks)


def own_kernel(places, n_arrays, factor_ref, own_ref, lse_ref, *refs):
    blocks = [Placed(refs[i], slab, TILE) for i, slab in places]
    cols, pown = blocks[:24], blocks[24:]
    grad_ref, loss_ref, prob, score, scratch = refs[n_arrays:]
    own = own_ref[...]
    own_float = own.astype(jnp.float32)
    n = own.shape[0]
    grad = jnp.zeros(own.shape, jnp.float32)
    loss = jnp.zeros((n, 1), jnp.float32)
    for pair in range(3):
        factor = factor_ref[pair, :1, :1]
        scale = factor_ref[pair + 3, :1]
        held = [(scratch if a % 2 == 0 else score).at[pair * 4 + a // 2] for a in range(8)]
        top = jnp.full((n, 128), -1e30, jnp.float32)
        for a in range(8):
            s = scores(own, cols[pair * 8 + a].all())
            held[a][...] = s
            top = jnp.maximum(top, jnp.maximum(s[:, :128], s[:, 128:]))
        best = jnp.max(top, 1, keepdims=True) * scale[:, :1]
        total = jnp.zeros((n, 128), jnp.float32)
        for a in range(8):
            p = jnp.exp2(held[a][...] * scale - best)
            prob[pair * 8 + a] = p
            total = total + p[:, :128] + p[:, 128:]
        total = jnp.sum(total, 1, keepdims=True)
        inverse = 1.0 / total
        product = jnp.zeros(own.shape, jnp.float32)
        for a in range(8):
            p = prob[pair * 8 + a] * inverse
            if a % 2:
                prob[pair * 8 + a] = p
                continue
            w = (p + jnp.exp2(held[a][...] * scale - lse_ref[pair * 4 + a // 2])).astype(jnp.bfloat16)
            product = product + jnp.dot(w, cols[pair * 8 + a].all(), preferred_element_type=jnp.float32)
        partner = pown[pair].all().astype(jnp.float32)
        grad = grad + factor * (product - 2.0 * partner)
        diagonal = factor * jnp.sum(own_float * partner, 1, keepdims=True)
        loss = loss + (best * (1.0 / LOG2E) + jnp.log(total) - diagonal)
    grad_ref[...] = grad
    loss_ref[...] = jnp.transpose(jnp.broadcast_to(loss, (n, 128)))[:1, :]


def own_half(info, own, lse, cols, pown):
    arrays, places = unique(cols + pown)
    n, width = own.shape
    return pl.pallas_call(
        functools.partial(own_kernel, tuple(places), len(arrays)),
        out_shape=(
            jax.ShapeDtypeStruct((n, width), jnp.float32),
            jax.ShapeDtypeStruct((1, n), jnp.float32),
            jax.ShapeDtypeStruct((24, n, TILE), jnp.float32),
            jax.ShapeDtypeStruct((12, n, TILE), jnp.float32),
        ),
        in_specs=[VMEM] * (3 + len(arrays)),
        out_specs=(VMEM,) * 4,
        scratch_shapes=[pltpu.VMEM((12, n, TILE), jnp.float32)],
        compiler_params=pltpu.CompilerParams(vmem_limit_bytes=12 * n * TILE * 4 + (6 << 20)),
        cost_estimate=LIGHT,
        name="own_half",
    )(info, own, lse, *arrays)


def other_kernel(places, n_arrays, factor_ref, half_ref, prob, score, lse_ref, *refs):
    cols = [Placed(refs[i], slab, TILE) for i, slab in places]
    grad = half_ref[...]
    for pair in range(3):
        scale = factor_ref[pair + 3, :1]
        product = jnp.zeros(half_ref.shape, jnp.float32)
        for i in range(4):
            q = jnp.exp2(score[pair * 4 + i] * scale - lse_ref[pair * 4 + i])
            w = (prob[pair * 8 + 2 * i + 1] + q).astype(jnp.bfloat16)
            product = product + jnp.dot(w, cols[pair * 4 + i].all(), preferred_element_type=jnp.float32)
        grad = grad + factor_ref[pair, :1, :1] * product
    refs[n_arrays][...] = grad


def other_half(info, half, prob, score, lse, cols):
    arrays, places = unique(cols)
    return pl.pallas_call(
        functools.partial(other_kernel, tuple(places), len(arrays)),
        out_shape=jax.ShapeDtypeStruct(half.shape, jnp.float32),
        in_specs=[VMEM] * (5 + len(arrays)),
        out_specs=VMEM,
        compiler_params=pltpu.CompilerParams(vmem_limit_bytes=8 << 20),
        cost_estimate=LIGHT,
        name="other_half",
    )(info, half, prob, score, lse, *arrays)


def whole_kernel(size, places, n_arrays, factor_ref, own_ref, *refs):
    cols = [Placed(refs[i], slab, size) for i, slab in places]
    pown = refs[n_arrays : n_arrays + 3]
    lses = refs[n_arrays + 3 : n_arrays + 5]
    grad_ref, loss_ref, prob, colprob = refs[n_arrays + 5 :]
    groups = size // TILE
    own = own_ref[...]
    own_float = own.astype(jnp.float32)
    n = own.shape[0]
    grad = jnp.zeros(own.shape, jnp.float32)
    loss = jnp.zeros((n, 1), jnp.float32)

    def loop(f, carry):
        for a in range(8):
            carry = lax.fori_loop(0, groups, functools.partial(f, a), carry)
        return carry

    for pair in range(3):
        factor = factor_ref[pair, :1, :1]
        scale = factor_ref[pair + 3, :1, :TILE]

        def first(a, g, top, pair=pair):
            s = scores(own, cols[pair * 8 + a].part(g))
            prob[a * groups + g] = s
            return jnp.maximum(top, jnp.maximum(s[:, :128], s[:, 128:]))

        top = loop(first, jnp.full((n, 128), -1e30, jnp.float32))
        best = jnp.max(top, 1, keepdims=True) * scale[:, :1]

        def second(a, g, total, pair=pair, best=best, scale=scale):
            j = a * groups + g
            s = prob[j] * scale
            p = jnp.exp2(s - best)
            prob[j] = p
            lse = lses[a % 2][pair * 4 + a // 2, :, pl.ds(pl.multiple_of(g * TILE, TILE), TILE)]
            colprob[j] = jnp.exp2(s - lse)
            return total + p[:, :128] + p[:, 128:]

        total = jnp.sum(loop(second, jnp.zeros((n, 128), jnp.float32)), 1, keepdims=True)
        inverse = 1.0 / total

        def third(a, g, acc, pair=pair, inverse=inverse):
            j = a * groups + g
            w = (prob[j] * inverse + colprob[j]).astype(jnp.bfloat16)
            return acc + jnp.dot(w, cols[pair * 8 + a].part(g), preferred_element_type=jnp.float32)

        product = loop(third, jnp.zeros(own.shape, jnp.float32))
        partner = pown[pair][...].astype(jnp.float32)
        grad = grad + factor * (product - 2.0 * partner)
        diagonal = factor * jnp.sum(own_float * partner, 1, keepdims=True)
        loss = loss + (best * (1.0 / LOG2E) + jnp.log(total) - diagonal)
    grad_ref[...] = grad
    loss_ref[...] = jnp.transpose(jnp.broadcast_to(loss, (n, 128)))[:1, :]


def whole(info, size, own, pown, lse, lse_other, cols):
    arrays, places = unique(cols)
    n, width = own.shape
    slots = 8 * size // TILE
    scratch = pltpu.VMEM((slots, n, TILE), jnp.float32)
    need = 24 * size * width * 2 + slots * n * TILE * 8
    return pl.pallas_call(
        functools.partial(whole_kernel, size, tuple(places), len(arrays)),
        out_shape=(jax.ShapeDtypeStruct((n, width), jnp.float32), jax.ShapeDtypeStruct((1, n), jnp.float32)),
        in_specs=[VMEM] * (7 + len(arrays)),
        out_specs=(VMEM, VMEM),
        scratch_shapes=[scratch, scratch],
        compiler_params=pltpu.CompilerParams(vmem_limit_bytes=need + (6 << 20)),
        cost_estimate=LIGHT,
        name="weights_and_gradient",
    )(info, own, *arrays, *pown, lse, lse_other)


def after(x, *others):
    return lax.optimization_barrier((x, *others))[0]


def shards(n_dp, embeddings, pairings, logit_scale):
    own = embeddings[0]
    n = own.shape[0]
    group = n_dp // 8
    size = n * group
    info = pair_factors(pairings, logit_scale, size)

    def send(block, dp_xor, mod_xor):
        pairs = [(d * 4 + m, (d ^ (dp_xor * group)) * 4 + (m ^ mod_xor)) for d in range(n_dp) for m in range(4)]
        return lax.ppermute(block, ("dp", "mod"), pairs)

    def to_y(block):
        return send(block, 1, 0)

    def to_z(block):
        return send(block, 2, 0)

    def to_far(block):
        return send(block, 4, 0)

    def to_x(block):
        return send(block, 0, 2)

    def to_core(block):
        return send(block, 0, 1)

    block = own
    if group > 1:
        members = [[g * group + i for i in range(group)] for g in range(8)]
        block = lax.all_gather(own, "dp", axis=0, tiled=True, axis_index_groups=members)

    made = {}
    busy = set()
    AX = {"X": to_x, "Y": to_y, "Z": to_z, "W": to_far}

    def one(x):
        return (x, 0)

    ROUTE = CONFIG["route"]
    TIES = CONFIG["ties"]
    COST = CONFIG["cost"]

    def tied(name, x):
        t = [first(get(o)) for o in TIES.get(name, ())]
        return after(x, *t) if t else x

    def first(v):
        return v[0] if isinstance(v, (list, tuple)) else v

    def slab(v):
        return (get(v), 0)

    def get(name):
        if name in made:
            return made[name]
        assert name not in busy, "cycle"
        busy.add(name)
        if name == "a0":
            v = block
        elif name == "own":
            v = pack(get("a0"))
        elif name in ROUTE:
            parent, ax = ROUTE[name]
            v = AX[ax](tied(name, get(parent)))
        elif name in CONFIG["packs"]:
            blocks = [get(x) for x in CONFIG["packs"][name]]
            blocks[0] = tied(name, blocks[0])
            v = to_core(pack(*blocks) if len(blocks) > 1 else blocks[0])
        elif name in CONFIG["kernels"]:
            v = kernel(name)
        elif name == "lse_other":
            v = to_y(get("K3")[0])
        busy.discard(name)
        made[name] = v
        return v

    where = {}
    for pname, members in CONFIG["packs"].items():
        for i, x in enumerate(members):
            where[("c" if x[0] == "a" else "d") + x[1]] = (pname, i)

    def handle(x):
        if x in where:
            pname, i = where[x]
            return (get(pname), i)
        return (get("own" if x == "a0" else x), 0)

    KROWS, KCOLS = {}, {}
    rr, cc = [], []
    seq = list(CONFIG["kernels"])
    prevk = {}
    for k in seq:
        nr, nc = CONFIG["kernels"][k]
        prevk[k] = (list(rr), list(cc))
        rr = rr + list(nr)
        cc = cc + list(nc)
        KROWS[k], KCOLS[k] = list(rr), list(cc)
    PAIR = {"c": 1, "b": 2, "d": 3}

    def kernel(k):
        i = seq.index(k)
        old = get(seq[i - 1]) if i else None
        oldr, oldc = prevk[k]
        rows = [handle(x) for x in KROWS[k]]
        cols = [handle(x) for x in KCOLS[k]]
        rows[0] = (tied(k, rows[0][0]), rows[0][1])
        new_rows = tuple(range(len(oldr), len(KROWS[k])))
        every = tuple(range(len(KROWS[k])))
        plan = [(PAIR[x[0]], new_rows if n < len(oldc) else every) for n, x in enumerate(KCOLS[k])]
        order = None
        if i == len(seq) - 1:
            order = tuple((PAIR[x[0]] - 1) * 4 + int(x[1]) // 2 for x in KCOLS[k])
        return stats(info, size, rows, cols, plan, old, order=order, cost=COST.get(k, 4))

    for name in CONFIG["emit"]:
        get(name)
    own_block = get("own")
    lse = get(seq[-1])[0]
    lse_other = to_y(lse)
    b, c, d = ([handle(p + str(i)) for i in range(8)] for p in "bcd")

    partners = c + b + d
    pown = [c[0], b[0], d[0]]
    if group > 1:
        start = (lax.axis_index("dp") % group) * n
        pown = [lax.dynamic_slice_in_dim(x, slab * size + start, n, 0) for x, slab in pown]
        gradient, losses = whole(info, size, own, pown, lse, lse_other, partners)
    else:
        half, losses, prob, score = own_half(info, own_block, lse, partners, pown)
        odd = [x[i] for x in (c, b, d) for i in (1, 3, 5, 7)]
        gradient = other_half(info, half, prob, score, lse_other, odd)
    return gradient[None], losses


def solution(mesh):
    return jax.shard_map(
        functools.partial(shards, mesh.shape["dp"]),
        mesh=mesh,
        in_specs=(P("mod", "dp", None), P(), P()),
        out_specs=(P("mod", "dp", None), P("mod", "dp")),
        check_vma=False,
    )
```

time: 276 us -> 66.1 us (0.24)
  waiting for transfers between devices: 155 us -> 25.6 us
  blocking collectives: 67.7 us -> 0 us
  matrix products: 21.9 us -> 0 us
  starting transfers between devices: 0.16 us -> 20.8 us
  between operations: 19.9 us -> 0.75 us
  Pallas kernels: 0 us -> 16.5 us
  other arithmetic: 7.43 us -> 0 us
    all_gather x4 -> x0, waiting for transfers between devices: 154 us -> none  [the longest x3 141 us: shards(): partner = lax.all_gather(own_rows, 'dp', axis=0, tiled=True)]
    pmax x1 -> x0, blocking collectives: 34.6 us -> none  [shards(): lax.pmax(jnp.max(scores, 0).astype(jnp.bfloat16), 'dp').astype(jnp.float32)]
    psum x1 -> x0, blocking collectives: 33.1 us -> none  [shards(): col_sum = lax.psum(jnp.sum(jnp.exp(scores - col_max[None, :]), 0), 'dp')]
    ppermute x0 -> x24, waiting for transfers between devices: none -> 25.6 us  [send(): return lax.ppermute(block, ('dp', 'mod'), pairs)]
    dot_general x6 -> x0, matrix products: 21.9 us -> none  [the longest x3 11.7 us: shards(): lax.dot_general(anchor, partner, (((1,), (1,)), ((), ())), preferred_elem...]
    ppermute x0 -> x24, starting transfers between devices: none -> 20.8 us  [send(): return lax.ppermute(block, ('dp', 'mod'), pairs)]
    pallas_call x0 -> x11, Pallas kernels: none -> 16.5 us  [the longest x3 8.21 us: stats(): pl.pallas_call(functools.partial(stats_kernel, size, tuple(places), len(a...]
    reduce_sum x4 -> x0, other arithmetic: 4.99 us -> none  [the longest x3 2.84 us: shards(): row_lse = row_max[:, 0] + jnp.log(jnp.sum(jnp.exp(scores - row_max), 1))]
  transfers between devices with their start and end apart: 4 -> 24, of which waited for: 4 -> 11; matrix products, arithmetic and copies ran while one was open for 4% -> 0% of each run, Pallas kernels for 0% -> 22%
where the time goes in v2:
time: 66.1 us; the launch traced here: 65.9 us
  waiting for transfers between devices  25.6 us (39%)
  starting transfers between devices  20.8 us (31%)
  Pallas kernels  16.5 us (25%)
  local copies, waits for them, and re-layouts  2.27 us (3%)
  between operations  0.75 us (1%)
    ppermute x24, waiting for transfers between devices, send(): return lax.ppermute(block, ('dp', 'mod'), pairs)  25.6 us
    ppermute x24, starting transfers between devices, send(): return lax.ppermute(block, ('dp', 'mod'), pairs)  20.8 us
    pallas_call x3, Pallas kernels, stats(): pl.pallas_call(functools.partial(stats_kernel, size, tuple(places), len(a...  8.21 us
    pallas_call x1, Pallas kernels, own_half(): pl.pallas_call(functools.partial(own_kernel, tuple(places), len(arrays)),...  5.63 us
    unnamed x6, local copies, waits for them, and re-layouts  2.27 us
    pallas_call x1, Pallas kernels, other_half(): pl.pallas_call(functools.partial(other_kernel, tuple(places), len(arrays)...  1.88 us
  transfers between devices with their start and end apart: 24, of which 11 were waited for; matrix products, arithmetic and copies ran while one was open for 0% of the time, Pallas kernels for 22%

profile of v2, /device:TPU:0, one launch (start us, length us, event | category | flops | bytes accessed | tf_op | source)
XLA Modules:
  0.0 65.9 jit_solution(12187350733492343543)
XLA Ops:
  0.6 3.0 %collective-permute-start.3 = (bf16[256,512]{1,0:T(8,128)(2,1)}, bf16[256,512]{1,0:T(8,128)(2,1)S(1)}, u32[]{:S(2)}, u32[]{:S(2)}) collective-permute-start(bf16[256,512]{1,0:T(8,128)(2,1)} %bitcast.2), channel_id=1, source_target_pairs={{0,2},{1,3},{2,0},{3,1},{4,6},{5,7},{6,4},{7,5},{8,10},{9,11},{10,... | collective-permute-start | bytes 786440 | tf_op jit(solution)/shard_map/ppermute | solution.py:328
  3.6 1.6 %collective-permute-start.1 = (bf16[256,512]{1,0:T(8,128)(2,1)}, bf16[256,512]{1,0:T(8,128)(2,1)S(1)}, u32[]{:S(2)}, u32[]{:S(2)}) collective-permute-start(bf16[256,512]{1,0:T(8,128)(2,1)} %bitcast.3), channel_id=1, source_target_pairs={{0,8},{1,9},{2,10},{3,11},{4,12},{5,13},{6,14},{7,15},{8,0},{9,1},... | collective-permute-start | bytes 786440 | tf_op jit(solution)/shard_map/ppermute | solution.py:328
  5.2 1.5 %collective-permute-start = (bf16[256,512]{1,0:T(8,128)(2,1)}, bf16[256,512]{1,0:T(8,128)(2,1)S(1)}, u32[]{:S(2)}, u32[]{:S(2)}) collective-permute-start(bf16[256,512]{1,0:T(8,128)(2,1)} %bitcast.4), channel_id=1, source_target_pairs={{0,4},{1,5},{2,6},{3,7},{4,0},{5,1},{6,2},{7,3},{8,12},{9,13},{10,... | collective-permute-start | bytes 786440 | tf_op jit(solution)/shard_map/ppermute | solution.py:328
  6.7 2.6 %collective-permute-start.2 = (bf16[256,512]{1,0:T(8,128)(2,1)}, bf16[256,512]{1,0:T(8,128)(2,1)S(1)}, u32[]{:S(2)}, u32[]{:S(2)}) collective-permute-start(bf16[256,512]{1,0:T(8,128)(2,1)} %bitcast.5), channel_id=1, source_target_pairs={{0,16},{1,17},{2,18},{3,19},{4,20},{5,21},{6,22},{7,23},{8,24},{9,... | collective-permute-start | bytes 786440 | tf_op jit(solution)/shard_map/ppermute | solution.py:328
  9.3 0.8 %collective-permute-done.3.refs_3_.refs_6_.refs_7_.refs_8_.refs_5_ = bf16[256,512]{1,0:T(8,128)(2,1)S(1)} collective-permute-done((bf16[256,512]{1,0:T(8,128)(2,1)}, bf16[256,512]{1,0:T(8,128)(2,1)S(1)}, u32[]{:S(2)}, u32[]{:S(2)}) %collective-permute-start.3) | collective-permute-done | bytes 262176 | tf_op jit(solution)/shard_map/ppermute | solution.py:328
  10.2 5.7 %collective-permute-done.1.refs_1_.refs_2_ = bf16[256,512]{1,0:T(8,128)(2,1)S(1)} collective-permute-done((bf16[256,512]{1,0:T(8,128)(2,1)}, bf16[256,512]{1,0:T(8,128)(2,1)S(1)}, u32[]{:S(2)}, u32[]{:S(2)}) %collective-permute-start.1) | collective-permute-done | bytes 262176 | tf_op jit(solution)/shard_map/ppermute | solution.py:328
  15.9 2.5 %collective-permute-start.4 = (bf16[256,512]{1,0:T(8,128)(2,1)S(1)}, bf16[256,512]{1,0:T(8,128)(2,1)S(1)}, u32[]{:S(2)}, u32[]{:S(2)}) collective-permute-start(bf16[256,512]{1,0:T(8,128)(2,1)S(1)} %collective-permute-done.1.refs_1_.refs_2_), channel_id=1, source_target_pairs={{0,4},{1,5},{2,6},{3,7},{4,0},{5,1},{6,2},{7,3},{8,12},{9,13},{10,... | collective-permute-start | bytes 786440 | tf_op jit(solution)/shard_map/ppermute | solution.py:328
  18.4 0.5 collective-permute-start.5
  18.9 1.8 %collective-permute-done.2.refs_2_.refs_3_ = bf16[256,512]{1,0:T(8,128)(2,1)S(1)} collective-permute-done((bf16[256,512]{1,0:T(8,128)(2,1)}, bf16[256,512]{1,0:T(8,128)(2,1)S(1)}, u32[]{:S(2)}, u32[]{:S(2)}) %collective-permute-start.2) | collective-permute-done | bytes 262176 | tf_op jit(solution)/shard_map/ppermute | solution.py:328
  20.9 2.6 %collective-permute-done.4.refs_0_.refs_4_ = bf16[256,512]{1,0:T(8,128)(2,1)S(1)} collective-permute-done((bf16[256,512]{1,0:T(8,128)(2,1)S(1)}, bf16[256,512]{1,0:T(8,128)(2,1)S(1)}, u32[]{:S(2)}, u32[]{:S(2)}) %collective-permute-start.4) | collective-permute-done | bytes 262176 | tf_op jit(solution)/shard_map/ppermute | solution.py:328
  23.5 1.7 %collective-permute-start.7 = (bf16[256,512]{1,0:T(8,128)(2,1)S(1)}, bf16[256,512]{1,0:T(8,128)(2,1)S(1)}, u32[]{:S(2)}, u32[]{:S(2)}) collective-permute-start(bf16[256,512]{1,0:T(8,128)(2,1)S(1)} %collective-permute-done.2.refs_2_.refs_3_), channel_id=1, source_target_pairs={{0,4},{1,5},{2,6},{3,7},{4,0},{5,1},{6,2},{7,3},{8,12},{9,13},{10,... | collective-permute-start | bytes 786440 | tf_op jit(solution)/shard_map/ppermute | solution.py:328
  25.3 0.5 collective-permute-start.12
  25.8 4.1 %collective-permute-done.7.refs_0_.refs_6_ = bf16[256,512]{1,0:T(8,128)(2,1)S(1)} collective-permute-done((bf16[256,512]{1,0:T(8,128)(2,1)S(1)}, bf16[256,512]{1,0:T(8,128)(2,1)S(1)}, u32[]{:S(2)}, u32[]{:S(2)}) %collective-permute-start.7) | collective-permute-done | bytes 262176 | tf_op jit(solution)/shard_map/ppermute | solution.py:328
  29.9 2.2 %collective-permute-done.6.refs_1_.refs_5_ = bf16[256,512]{1,0:T(8,128)(2,1)S(1)} collective-permute-done((bf16[256,512]{1,0:T(8,128)(2,1)S(1)}, bf16[256,512]{1,0:T(8,128)(2,1)S(1)}, u32[]{:S(2)}, u32[]{:S(2)}) %collective-permute-start.6) | collective-permute-done | bytes 262176 | tf_op jit(solution)/shard_map/ppermute | solution.py:328
  32.4 0.5 collective-permute-start.15
  32.9 2.3 %collective-permute-start.13 = (bf16[256,512]{1,0:T(8,128)(2,1)S(1)}, bf16[256,512]{1,0:T(8,128)(2,1)S(1)}, u32[]{:S(2)}, u32[]{:S(2)}) collective-permute-start(bf16[256,512]{1,0:T(8,128)(2,1)S(1)} %collective-permute-done.3.refs_3_.refs_6_.refs_7_.refs_8_.refs_5_), channel_id=1, source_target_pairs={{0,8},{1,9},{2,10},{3,11},{4,12},{5,13},{6,14},{7,15},{8,0},{9,1},... | collective-permute-start | bytes 786440 | tf_op jit(solution)/shard_map/ppermute | solution.py:328
  35.2 4.9 %collective-permute-done.8.refs_7_ = bf16[256,512]{1,0:T(8,128)(2,1)S(1)} collective-permute-done((bf16[256,512]{1,0:T(8,128)(2,1)S(1)}, bf16[256,512]{1,0:T(8,128)(2,1)S(1)}, u32[]{:S(2)}, u32[]{:S(2)}) %collective-permute-start.8) | collective-permute-done | bytes 262176 | tf_op jit(solution)/shard_map/ppermute | solution.py:328
  40.1 2.3 %collective-permute-start.20 = (bf16[256,512]{1,0:T(8,128)(2,1)S(1)}, bf16[256,512]{1,0:T(8,128)(2,1)S(1)}, u32[]{:S(2)}, u32[]{:S(2)}) collective-permute-start(bf16[256,512]{1,0:T(8,128)(2,1)S(1)} %collective-permute-done.15.refs_15_.refs_11_), channel_id=1, source_target_pairs={{0,4},{1,5},{2,6},{3,7},{4,0},{5,1},{6,2},{7,3},{8,12},{9,13},{10,... | collective-permute-start | bytes 786440 | tf_op jit(solution)/shard_map/ppermute | solution.py:328
  42.5 0.9 %copy-done = bf16[1,256,512]{2,1,0:T(8,128)(2,1)S(1)} copy-done((bf16[1,256,512]{2,1,0:T(8,128)(2,1)S(1)}, bf16[1,256,512]{2,1,0:T(8,128)(2,1)}, u32[]{:S(2)}) %copy-start) | copy-done | bytes 262168
  43.4 0.7 %copy-done.1 = s32[3,4]{1,0:T(4,128)S(1)} copy-done((s32[3,4]{1,0:T(4,128)S(1)}, s32[3,4]{1,0:T(4,128)}, u32[]{:S(2)}) %copy-start.1) | copy-done | bytes 72
  44.1 0.7 copy-done.2
  44.8 0.6 pair_factors.1.factor_ref
  45.5 1.0 %collective-permute-done.18.refs_0_.refs_8_.refs_5_ = bf16[256,512]{1,0:T(8,128)(2,1)S(1)} collective-permute-done((bf16[256,512]{1,0:T(8,128)(2,1)S(1)}, bf16[256,512]{1,0:T(8,128)(2,1)S(1)}, u32[]{:S(2)}, u32[]{:S(2)}) %collective-permute-start.18) | collective-permute-done | bytes 262176 | tf_op jit(solution)/shard_map/ppermute | solution.py:328
  46.5 0.3 collective-permute-done.20.refs_12_.refs_7_
  47.0 1.8 %collective-permute-done.19.refs_1_.refs_10_.refs_6_ = bf16[256,512]{1,0:T(8,128)(2,1)S(1)} collective-permute-done((bf16[256,512]{1,0:T(8,128)(2,1)S(1)}, bf16[256,512]{1,0:T(8,128)(2,1)S(1)}, u32[]{:S(2)}, u32[]{:S(2)}) %collective-permute-start.19) | collective-permute-done | bytes 262176 | tf_op jit(solution)/shard_map/ppermute | solution.py:328
  48.9 0.6 collective-permute-start.21
  49.4 2.6 %col_stats.3 = (f32[5,8,256]{2,1,0:T(8,128)S(1)}, f32[5,8,256]{2,1,0:T(8,128)S(1)}) custom-call(f32[6,8,256]{2,1,0:T(8,128)S(1)} %pair_factors.1.factor_ref, bf16[256,512]{1,0:T(8,128)(2,1)S(1)} %pack.5.refs_0_.own_ref, bf16[256,512]{1,0:T(8,128)(2,1)S(1)} %collective-permute-done.refs_0_.refs_1_, ...), custom_call_target="tpu_custom_call" | custom-call | flops 40265318400 | bytes 1000 | tf_op jit(solution)/shard_map/col_stats/pallas_call | solution.py:121
  52.1 0.5 collective-permute-start.22
  52.6 2.2 %col_stats.4 = (f32[8,8,256]{2,1,0:T(8,128)S(1)}, f32[8,8,256]{2,1,0:T(8,128)S(1)}) custom-call(f32[6,8,256]{2,1,0:T(8,128)S(1)} %pair_factors.1.factor_ref, bf16[256,512]{1,0:T(8,128)(2,1)S(1)} %pack.5.refs_0_.own_ref, bf16[256,512]{1,0:T(8,128)(2,1)S(1)} %collective-permute-done.refs_0_.refs_1_, ...), custom_call_target="tpu_custom_call" | custom-call | flops 34896609280 | bytes 1000 | tf_op jit(solution)/shard_map/col_stats/pallas_call | solution.py:121
  54.9 3.4 %col_stats.5.lse_ref = f32[12,1,256]{2,1,0:T(1,128)S(1)} custom-call(f32[6,8,256]{2,1,0:T(8,128)S(1)} %pair_factors.1.factor_ref, bf16[256,512]{1,0:T(8,128)(2,1)S(1)} %pack.5.refs_0_.own_ref, bf16[256,512]{1,0:T(8,128)(2,1)S(1)} %collective-permute-done.refs_0_.refs_1_, bf16[256,512]{1,0:T(8,128)(2,1)S(1)} %collective-permute-done.1.refs_1_.refs_2_, ...), custom_call_target="tpu_custom_call" | custom-call | flops 53687091200 | bytes 1000 | tf_op jit(solution)/shard_map/col_stats/pallas_call | solution.py:121
  58.4 5.6 %own_half.1 = (f32[256,512]{1,0:T(8,128)S(1)}, f32[1,256]{1,0:T(1,128)}, f32[24,256,256]{2,1,0:T(8,128)S(1)}, f32[12,256,256]{2,1,0:T(8,128)S(1)}) custom-call(f32[6,8,256]{2,1,0:T(8,128)S(1)} %pair_factors.1.factor_ref, bf16[256,512]{1,0:T(8,128)(2,1)S(1)} %pack.5.refs_0_.own_ref, f32[12,1,256]{2,1,0:T(1,128)S(1)} %col_stats.5.lse_ref, ...), custom_call_target="tpu_custom_call" | custom-call | flops 1000 | bytes 1000 | tf_op jit(solution)/shard_map/own_half/pallas_call | solution.py:198
  64.1 1.9 %other_half.1 = f32[256,512]{1,0:T(8,128)} custom-call(f32[6,8,256]{2,1,0:T(8,128)S(1)} %pair_factors.1.factor_ref, f32[256,512]{1,0:T(8,128)S(1)} %get-tuple-element.34.half_ref, f32[24,256,256]{2,1,0:T(8,128)S(1)} %get-tuple-element.35.prob, f32[12,256,256]{2,1,0:T(8,128)S(1)} %get-tuple-element.36.score, ...), custom_call_target="tpu_custom_call" | custom-call | flops 1000 | bytes 1000 | tf_op jit(solution)/shard_map/other_half/pallas_call | solution.py:231
  (33 shorter events, 1.0 us)
Async XLA Ops:
  0.6 9.5 %collective-permute-start.3 = (bf16[256,512]{1,0:T(8,128)(2,1)}, bf16[256,512]{1,0:T(8,128)(2,1)S(1)}, u32[]{:S(2)}, u32[]{:S(2)}) collective-permute-start(bf16[256,512]{1,0:T(8,128)(2,1)} %bitcast.2), channel_id=1, source_target_pairs={{0,2},{1,3},{2,0},{3,1},{4,6},{5,7},{6,4},{7,5},{8,10},{9,11},{10,... | collective-permute-start | bytes 786440 | tf_op jit(solution)/shard_map/ppermute | solution.py:328
  3.6 12.2 %collective-permute-start.1 = (bf16[256,512]{1,0:T(8,128)(2,1)}, bf16[256,512]{1,0:T(8,128)(2,1)S(1)}, u32[]{:S(2)}, u32[]{:S(2)}) collective-permute-start(bf16[256,512]{1,0:T(8,128)(2,1)} %bitcast.3), channel_id=1, source_target_pairs={{0,8},{1,9},{2,10},{3,11},{4,12},{5,13},{6,14},{7,15},{8,0},{9,1},... | collective-permute-start | bytes 786440 | tf_op jit(solution)/shard_map/ppermute | solution.py:328
  5.2 13.2 %collective-permute-start = (bf16[256,512]{1,0:T(8,128)(2,1)}, bf16[256,512]{1,0:T(8,128)(2,1)S(1)}, u32[]{:S(2)}, u32[]{:S(2)}) collective-permute-start(bf16[256,512]{1,0:T(8,128)(2,1)} %bitcast.4), channel_id=1, source_target_pairs={{0,4},{1,5},{2,6},{3,7},{4,0},{5,1},{6,2},{7,3},{8,12},{9,13},{10,... | collective-permute-start | bytes 786440 | tf_op jit(solution)/shard_map/ppermute | solution.py:328
  6.7 14.0 %collective-permute-start.2 = (bf16[256,512]{1,0:T(8,128)(2,1)}, bf16[256,512]{1,0:T(8,128)(2,1)S(1)}, u32[]{:S(2)}, u32[]{:S(2)}) collective-permute-start(bf16[256,512]{1,0:T(8,128)(2,1)} %bitcast.5), channel_id=1, source_target_pairs={{0,16},{1,17},{2,18},{3,19},{4,20},{5,21},{6,22},{7,23},{8,24},{9,... | collective-permute-start | bytes 786440 | tf_op jit(solution)/shard_map/ppermute | solution.py:328
  15.9 7.6 %collective-permute-start.4 = (bf16[256,512]{1,0:T(8,128)(2,1)S(1)}, bf16[256,512]{1,0:T(8,128)(2,1)S(1)}, u32[]{:S(2)}, u32[]{:S(2)}) collective-permute-start(bf16[256,512]{1,0:T(8,128)(2,1)S(1)} %collective-permute-done.1.refs_1_.refs_2_), channel_id=1, source_target_pairs={{0,4},{1,5},{2,6},{3,7},{4,0},{5,1},{6,2},{7,3},{8,12},{9,13},{10,... | collective-permute-start | bytes 786440 | tf_op jit(solution)/shard_map/ppermute | solution.py:328
  18.4 6.9 %collective-permute-start.5 = (bf16[256,512]{1,0:T(8,128)(2,1)S(1)}, bf16[256,512]{1,0:T(8,128)(2,1)S(1)}, u32[]{:S(2)}, u32[]{:S(2)}) collective-permute-start(bf16[256,512]{1,0:T(8,128)(2,1)S(1)} %collective-permute-done.refs_0_.refs_1_), channel_id=1, source_target_pairs={{0,2},{1,3},{2,0},{3,1},{4,6},{5,7},{6,4},{7,5},{8,10},{9,11},{10,... | collective-permute-start | bytes 786440 | tf_op jit(solution)/shard_map/ppermute | solution.py:328
  20.8 28.6 %collective-permute-start.10 = (bf16[1024,512]{1,0:T(8,128)(2,1)S(1)}, bf16[1024,512]{1,0:T(8,128)(2,1)S(1)}, u32[]{:S(2)}, u32[]{:S(2)}) collective-permute-start(bf16[1024,512]{1,0:T(8,128)(2,1)S(1)} %pack.6), channel_id=1, source_target_pairs={{0,1},{1,0},{2,3},{3,2},{4,5},{5,4},{6,7},{7,6},{8,9},{9,8},{10,11... | collective-permute-start | bytes 3145736 | tf_op jit(solution)/shard_map/ppermute | solution.py:328
  23.5 6.4 %collective-permute-start.7 = (bf16[256,512]{1,0:T(8,128)(2,1)S(1)}, bf16[256,512]{1,0:T(8,128)(2,1)S(1)}, u32[]{:S(2)}, u32[]{:S(2)}) collective-permute-start(bf16[256,512]{1,0:T(8,128)(2,1)S(1)} %collective-permute-done.2.refs_2_.refs_3_), channel_id=1, source_target_pairs={{0,4},{1,5},{2,6},{3,7},{4,0},{5,1},{6,2},{7,3},{8,12},{9,13},{10,... | collective-permute-start | bytes 786440 | tf_op jit(solution)/shard_map/ppermute | solution.py:328
  25.3 6.9 %collective-permute-start.6 = (bf16[256,512]{1,0:T(8,128)(2,1)S(1)}, bf16[256,512]{1,0:T(8,128)(2,1)S(1)}, u32[]{:S(2)}, u32[]{:S(2)}) collective-permute-start(bf16[256,512]{1,0:T(8,128)(2,1)S(1)} %collective-permute-done.2.refs_2_.refs_3_), channel_id=1, source_target_pairs={{0,8},{1,9},{2,10},{3,11},{4,12},{5,13},{6,14},{7,15},{8,0},{9,1},... | collective-permute-start | bytes 786440 | tf_op jit(solution)/shard_map/ppermute | solution.py:328
  25.3 7.1 %collective-permute-start.12 = (bf16[256,512]{1,0:T(8,128)(2,1)S(1)}, bf16[256,512]{1,0:T(8,128)(2,1)S(1)}, u32[]{:S(2)}, u32[]{:S(2)}) collective-permute-start(bf16[256,512]{1,0:T(8,128)(2,1)S(1)} %collective-permute-done.2.refs_2_.refs_3_), channel_id=1, source_target_pairs={{0,2},{1,3},{2,0},{3,1},{4,6},{5,7},{6,4},{7,5},{8,10},{9,11},{10,... | collective-permute-start | bytes 786440 | tf_op jit(solution)/shard_map/ppermute | solution.py:328
  32.1 8.0 %collective-permute-start.8 = (bf16[256,512]{1,0:T(8,128)(2,1)S(1)}, bf16[256,512]{1,0:T(8,128)(2,1)S(1)}, u32[]{:S(2)}, u32[]{:S(2)}) collective-permute-start(bf16[256,512]{1,0:T(8,128)(2,1)S(1)} %collective-permute-done.6.refs_1_.refs_5_), channel_id=1, source_target_pairs={{0,4},{1,5},{2,6},{3,7},{4,0},{5,1},{6,2},{7,3},{8,12},{9,13},{10,... | collective-permute-start | bytes 786440 | tf_op jit(solution)/shard_map/ppermute | solution.py:328
  32.4 7.7 %collective-permute-start.15 = (bf16[256,512]{1,0:T(8,128)(2,1)S(1)}, bf16[256,512]{1,0:T(8,128)(2,1)S(1)}, u32[]{:S(2)}, u32[]{:S(2)}) collective-permute-start(bf16[256,512]{1,0:T(8,128)(2,1)S(1)} %collective-permute-done.6.refs_1_.refs_5_), channel_id=1, source_target_pairs={{0,2},{1,3},{2,0},{3,1},{4,6},{5,7},{6,4},{7,5},{8,10},{9,11},{10,... | collective-permute-start | bytes 786440 | tf_op jit(solution)/shard_map/ppermute | solution.py:328
  32.9 9.5 %collective-permute-start.13 = (bf16[256,512]{1,0:T(8,128)(2,1)S(1)}, bf16[256,512]{1,0:T(8,128)(2,1)S(1)}, u32[]{:S(2)}, u32[]{:S(2)}) collective-permute-start(bf16[256,512]{1,0:T(8,128)(2,1)S(1)} %collective-permute-done.3.refs_3_.refs_6_.refs_7_.refs_8_.refs_5_), channel_id=1, source_target_pairs={{0,8},{1,9},{2,10},{3,11},{4,12},{5,13},{6,14},{7,15},{8,0},{9,1},... | collective-permute-start | bytes 786440 | tf_op jit(solution)/shard_map/ppermute | solution.py:328
  40.1 6.4 %collective-permute-start.18 = (bf16[256,512]{1,0:T(8,128)(2,1)S(1)}, bf16[256,512]{1,0:T(8,128)(2,1)S(1)}, u32[]{:S(2)}, u32[]{:S(2)}) collective-permute-start(bf16[256,512]{1,0:T(8,128)(2,1)S(1)} %collective-permute-done.5.refs_2_.refs_6_.refs_4_), channel_id=1, source_target_pairs={{0,8},{1,9},{2,10},{3,11},{4,12},{5,13},{6,14},{7,15},{8,0},{9,1},... | collective-permute-start | bytes 786440 | tf_op jit(solution)/shard_map/ppermute | solution.py:328
  40.1 6.7 %collective-permute-start.20 = (bf16[256,512]{1,0:T(8,128)(2,1)S(1)}, bf16[256,512]{1,0:T(8,128)(2,1)S(1)}, u32[]{:S(2)}, u32[]{:S(2)}) collective-permute-start(bf16[256,512]{1,0:T(8,128)(2,1)S(1)} %collective-permute-done.15.refs_15_.refs_11_), channel_id=1, source_target_pairs={{0,4},{1,5},{2,6},{3,7},{4,0},{5,1},{6,2},{7,3},{8,12},{9,13},{10,... | collective-permute-start | bytes 786440 | tf_op jit(solution)/shard_map/ppermute | solution.py:328
  42.4 6.4 %collective-permute-start.19 = (bf16[256,512]{1,0:T(8,128)(2,1)S(1)}, bf16[256,512]{1,0:T(8,128)(2,1)S(1)}, u32[]{:S(2)}, u32[]{:S(2)}) collective-permute-start(bf16[256,512]{1,0:T(8,128)(2,1)S(1)} %collective-permute-done.7.refs_0_.refs_6_), channel_id=1, source_target_pairs={{0,2},{1,3},{2,0},{3,1},{4,6},{5,7},{6,4},{7,5},{8,10},{9,11},{10,... | collective-permute-start | bytes 786440 | tf_op jit(solution)/shard_map/ppermute | solution.py:328
  42.5 6.4 %collective-permute-start.9 = (bf16[256,512]{1,0:T(8,128)(2,1)}, bf16[256,512]{1,0:T(8,128)(2,1)S(1)}, u32[]{:S(2)}, u32[]{:S(2)}) collective-permute-start(bf16[256,512]{1,0:T(8,128)(2,1)} %bitcast.6), channel_id=1, source_target_pairs={{0,1},{1,0},{2,3},{3,2},{4,5},{5,4},{6,7},{7,6},{8,9},{9,8},{10,11... | collective-permute-start | bytes 786440 | tf_op jit(solution)/shard_map/ppermute | solution.py:328
  42.5 1.0 %copy-start = (bf16[1,256,512]{2,1,0:T(8,128)(2,1)S(1)}, bf16[1,256,512]{2,1,0:T(8,128)(2,1)}, u32[]{:S(2)}) copy-start(bf16[1,256,512]{2,1,0:T(8,128)(2,1)} %param.3) | copy-start | bytes 786436
  43.4 0.7 %copy-start.1 = (s32[3,4]{1,0:T(4,128)S(1)}, s32[3,4]{1,0:T(4,128)}, u32[]{:S(2)}) copy-start(s32[3,4]{1,0:T(4,128)} %pairings_ref.1) | copy-start | bytes 148
  44.1 0.7 copy-start.2
  46.5 5.7 %collective-permute-start.11 = (bf16[768,512]{1,0:T(8,128)(2,1)S(1)}, bf16[768,512]{1,0:T(8,128)(2,1)S(1)}, u32[]{:S(2)}, u32[]{:S(2)}) collective-permute-start(bf16[768,512]{1,0:T(8,128)(2,1)S(1)} %pack.7), channel_id=1, source_target_pairs={{0,1},{1,0},{2,3},{3,2},{4,5},{5,4},{6,7},{7,6},{8,9},{9,8},{10,11... | collective-permute-start | bytes 2359304 | tf_op jit(solution)/shard_map/ppermute | solution.py:328
  46.8 8.0 %collective-permute-start.14 = (bf16[768,512]{1,0:T(8,128)(2,1)S(1)}, bf16[768,512]{1,0:T(8,128)(2,1)S(1)}, u32[]{:S(2)}, u32[]{:S(2)}) collective-permute-start(bf16[768,512]{1,0:T(8,128)(2,1)S(1)} %pack.8), channel_id=1, source_target_pairs={{0,1},{1,0},{2,3},{3,2},{4,5},{5,4},{6,7},{7,6},{8,9},{9,8},{10,11... | collective-permute-start | bytes 2359304 | tf_op jit(solution)/shard_map/ppermute | solution.py:328
  48.8 9.6 %collective-permute-start.17 = (bf16[256,512]{1,0:T(8,128)(2,1)S(1)}, bf16[256,512]{1,0:T(8,128)(2,1)S(1)}, u32[]{:S(2)}, u32[]{:S(2)}) collective-permute-start(bf16[256,512]{1,0:T(8,128)(2,1)S(1)} %collective-permute-done.8.refs_7_), channel_id=1, source_target_pairs={{0,1},{1,0},{2,3},{3,2},{4,5},{5,4},{6,7},{7,6},{8,9},{9,8},{10,11... | collective-permute-start | bytes 786440 | tf_op jit(solution)/shard_map/ppermute | solution.py:328
  48.9 9.6 %collective-permute-start.21 = (bf16[512,512]{1,0:T(8,128)(2,1)S(1)}, bf16[512,512]{1,0:T(8,128)(2,1)S(1)}, u32[]{:S(2)}, u32[]{:S(2)}) collective-permute-start(bf16[512,512]{1,0:T(8,128)(2,1)S(1)} %pack.9), channel_id=1, source_target_pairs={{0,1},{1,0},{2,3},{3,2},{4,5},{5,4},{6,7},{7,6},{8,9},{9,8},{10,11... | collective-permute-start | bytes 1572872 | tf_op jit(solution)/shard_map/ppermute | solution.py:328
  52.0 2.8 %collective-permute-start.16 = (bf16[256,512]{1,0:T(8,128)(2,1)S(1)}, bf16[256,512]{1,0:T(8,128)(2,1)S(1)}, u32[]{:S(2)}, u32[]{:S(2)}) collective-permute-start(bf16[256,512]{1,0:T(8,128)(2,1)S(1)} %collective-permute-done.15.refs_15_.refs_11_), channel_id=1, source_target_pairs={{0,1},{1,0},{2,3},{3,2},{4,5},{5,4},{6,7},{7,6},{8,9},{9,8},{10,11... | collective-permute-start | bytes 786440 | tf_op jit(solution)/shard_map/ppermute | solution.py:328
  52.1 6.3 %collective-permute-start.22 = (bf16[256,512]{1,0:T(8,128)(2,1)S(1)}, bf16[256,512]{1,0:T(8,128)(2,1)S(1)}, u32[]{:S(2)}, u32[]{:S(2)}) collective-permute-start(bf16[256,512]{1,0:T(8,128)(2,1)S(1)} %collective-permute-done.20.refs_12_.refs_7_), channel_id=1, source_target_pairs={{0,1},{1,0},{2,3},{3,2},{4,5},{5,4},{6,7},{7,6},{8,9},{9,8},{10,11... | collective-permute-start | bytes 786440 | tf_op jit(solution)/shard_map/ppermute | solution.py:328
  58.3 5.8 %collective-permute-start.23 = (f32[12,1,256]{2,1,0:T(1,128)S(1)}, f32[12,1,256]{2,1,0:T(1,128)S(1)}, u32[]{:S(2)}, u32[]{:S(2)}) collective-permute-start(f32[12,1,256]{2,1,0:T(1,128)S(1)} %col_stats.5.lse_ref), channel_id=1, source_target_pairs={{0,4},{1,5},{2,6},{3,7},{4,0},{5,1},{6,2},{7,3},{8,12},{9,13},{10,... | collective-permute-start | bytes 36872 | tf_op jit(solution)/shard_map/ppermute | solution.py:328

commit v3 on v2

--- a/solution.py
+++ b/solution.py
@@ -1,5 +1,4 @@
 import functools
-CONFIG = {'route': {'a1': ('a0', 'Y'), 'a2': ('a0', 'Z'), 'a4': ('a0', 'W'), 'b0': ('a0', 'X'), 'b1': ('a1', 'X'), 'a3': ('a2', 'Y'), 'a6': ('a4', 'Z'), 'b4': ('a4', 'X'), 'a5': ('a4', 'Y'), 'b2': ('b0', 'Z'), 'b6': ('a6', 'X'), 'a7': ('a6', 'Y'), 'b3': ('b1', 'Z'), 'b5': ('a5', 'X'), 'b7': ('b6', 'Y')}, 'ties': {'a3': ['b0'], 'a6': ['b1'], 'b4': ['b1'], 'a5': ['a3'], 'b2': ['b1'], 'b6': ['b4'], 'a7': ['a5'], 'b3': ['a7'], 'b5': ['b6'], 'P4': ['b7'], 'P5': ['K1']}, 'packs': {'P1': ['a1', 'a2', 'a4', 'b0'], 'P2': ['a3', 'a6', 'b1'], 'P3': ['a5', 'b4', 'b2'], 'P0': ['a0'], 'P5': ['b6'], 'P6': ['a7'], 'P4': ['b3', 'b5'], 'P7': ['b7']}, 'kernels': {'K1': (['a0', 'a1', 'a2', 'a4', 'a3', 'a6'], ['b0', 'c0', 'c2', 'c4', 'd0']), 'K2': (['a5'], ['c6', 'b4', 'b2']), 'K3': (['a7'], ['d4', 'd2', 'b6', 'd6'])}, 'cost': {'K1': 40, 'K2': 40, 'K3': 40}, 'emit': ['a2', 'a4', 'a1', 'b0', 'b1', 'a3', 'a6', 'b4', 'a5', 'b2', 'b6', 'a7', 'b3', 'b5', 'b7']}
 import math
 
 import jax
@@ -14,6 +13,59 @@
 NT = (((1,), (1,)), ((), ()))
 SMEM = pl.BlockSpec(memory_space=pltpu.SMEM)
 VMEM = pl.BlockSpec(memory_space=pltpu.VMEM)
+ROUTE = {
+    "a2": ("a0", "Z"),
+    "a4": ("a0", "W"),
+    "a1": ("a0", "Y"),
+    "b0": ("a0", "X"),
+    "b1": ("a1", "X"),
+    "a3": ("a2", "Y"),
+    "a6": ("a4", "Z"),
+    "b4": ("a4", "X"),
+    "a5": ("a4", "Y"),
+    "b2": ("b0", "Z"),
+    "b6": ("a6", "X"),
+    "a7": ("a6", "Y"),
+    "b3": ("b1", "Z"),
+    "b5": ("a5", "X"),
+    "b7": ("b6", "Y"),
+}
+AFTER = {
+    "a6": ("b1", "b0"),
+    "a5": ("a3",),
+    "b2": ("a6", "b4"),
+    "a7": ("a4",),
+    "b3": ("b6",),
+    "b5": ("b6",),
+    "P4": ("b0", "b5"),
+    "P1": ("a1",),
+    "P3": ("b4",),
+    "K2": ("b7", "b1", "a4"),
+    "K1": ("a3",),
+    "P5": ("a6",),
+    "b1": ("own", "info"),
+}
+PACKS = {
+    "P1": ("a2", "a4", "b0"),
+    "P2": ("a6", "b1", "a7"),
+    "P3": ("a5", "b4", "b2"),
+    "P4": ("b3", "b5", "a3", "a1"),
+    "P7": ("b6",),
+    "P11": ("a0",),
+    "P9": ("b7",),
+}
+KERNELS = {
+    "K1": (("a0", "a1", "a2", "a4", "a3", "a6", "a5", "a7"), ("b0", "c0", "c2", "c4", "d0", "b6", "b2", "b4")),
+    "K2": ((), ("c6", "d2")),
+    "K3": ((), ("d4", "d6")),
+}
+COST = {
+    "K1": 40,
+    "K2": 40,
+    "K3": 10,
+}
+PAIR = {"c": 1, "b": 2, "d": 3}
+
 LIGHT = pl.CostEstimate(flops=1000, bytes_accessed=1000, transcendentals=0)
 
 
@@ -157,37 +209,69 @@
     own = own_ref[...]
     own_float = own.astype(jnp.float32)
     n = own.shape[0]
+    tops, bests, totals, inverses, products = ([None] * 3 for _ in range(5))
+
+    def held(pair, a):
+        return (score if a % 2 else scratch).at[pair * 4 + a // 2]
+
+    def score_step(pair, a):
+        s = scores(own, cols[pair * 8 + a].all()) * factor_ref[pair + 3, :1]
+        held(pair, a)[...] = s
+        top = jnp.maximum(s[:, :128], s[:, 128:])
+        tops[pair] = top if a == 0 else jnp.maximum(tops[pair], top)
+
+    def close_scores(pair):
+        bests[pair] = jnp.max(tops[pair], 1, keepdims=True)
+        totals[pair] = jnp.zeros((n, 128), jnp.float32)
+
+    def prob_step(pair, a):
+        p = jnp.exp2(held(pair, a)[...] - bests[pair])
+        prob[pair * 8 + a] = p
+        totals[pair] = totals[pair] + p[:, :128] + p[:, 128:]
+
+    def close_probs(pair):
+        totals[pair] = jnp.sum(totals[pair], 1, keepdims=True)
+        inverses[pair] = 1.0 / totals[pair]
+        products[pair] = jnp.zeros(own.shape, jnp.float32)
+
+    def weight_step(pair, a):
+        p = prob[pair * 8 + a] * inverses[pair]
+        if a % 2:
+            prob[pair * 8 + a] = p
+            return
+        w = (p + jnp.exp2(held(pair, a)[...] - lse_ref[pair * 4 + a // 2])).astype(jnp.bfloat16)
+        products[pair] = products[pair] + jnp.dot(
+            w, cols[pair * 8 + a].all(), preferred_element_type=jnp.float32
+        )
+
+    for a in range(8):
+        score_step(0, a)
+    close_scores(0)
+    for a in range(8):
+        score_step(1, a)
+        prob_step(0, a)
+    close_probs(0)
+    close_scores(1)
+    for a in range(8):
+        score_step(2, a)
+        prob_step(1, a)
+    close_probs(1)
+    close_scores(2)
+    for a in range(8):
+        weight_step(0, a)
+        prob_step(2, a)
+    close_probs(2)
+    for a in range(8):
+        weight_step(1, a)
+        weight_step(2, a)
     grad = jnp.zeros(own.shape, jnp.float32)
     loss = jnp.zeros((n, 1), jnp.float32)
     for pair in range(3):
         factor = factor_ref[pair, :1, :1]
-        scale = factor_ref[pair + 3, :1]
-        held = [(scratch if a % 2 == 0 else score).at[pair * 4 + a // 2] for a in range(8)]
-        top = jnp.full((n, 128), -1e30, jnp.float32)
-        for a in range(8):
-            s = scores(own, cols[pair * 8 + a].all())
-            held[a][...] = s
-            top = jnp.maximum(top, jnp.maximum(s[:, :128], s[:, 128:]))
-        best = jnp.max(top, 1, keepdims=True) * scale[:, :1]
-        total = jnp.zeros((n, 128), jnp.float32)
-        for a in range(8):
-            p = jnp.exp2(held[a][...] * scale - best)
-            prob[pair * 8 + a] = p
-            total = total + p[:, :128] + p[:, 128:]
-        total = jnp.sum(total, 1, keepdims=True)
-        inverse = 1.0 / total
-        product = jnp.zeros(own.shape, jnp.float32)
-        for a in range(8):
-            p = prob[pair * 8 + a] * inverse
-            if a % 2:
-                prob[pair * 8 + a] = p
-                continue
-            w = (p + jnp.exp2(held[a][...] * scale - lse_ref[pair * 4 + a // 2])).astype(jnp.bfloat16)
-            product = product + jnp.dot(w, cols[pair * 8 + a].all(), preferred_element_type=jnp.float32)
         partner = pown[pair].all().astype(jnp.float32)
-        grad = grad + factor * (product - 2.0 * partner)
+        grad = grad + factor * (products[pair] - 2.0 * partner)
         diagonal = factor * jnp.sum(own_float * partner, 1, keepdims=True)
-        loss = loss + (best * (1.0 / LOG2E) + jnp.log(total) - diagonal)
+        loss = loss + (bests[pair] * (1.0 / LOG2E) + jnp.log(totals[pair]) - diagonal)
     grad_ref[...] = grad
     loss_ref[...] = jnp.transpose(jnp.broadcast_to(loss, (n, 128)))[:1, :]
 
@@ -216,10 +300,9 @@
     cols = [Placed(refs[i], slab, TILE) for i, slab in places]
     grad = half_ref[...]
     for pair in range(3):
-        scale = factor_ref[pair + 3, :1]
         product = jnp.zeros(half_ref.shape, jnp.float32)
         for i in range(4):
-            q = jnp.exp2(score[pair * 4 + i] * scale - lse_ref[pair * 4 + i])
+            q = jnp.exp2(score[pair * 4 + i] - lse_ref[pair * 4 + i])
             w = (prob[pair * 8 + 2 * i + 1] + q).astype(jnp.bfloat16)
             product = product + jnp.dot(w, cols[pair * 4 + i].all(), preferred_element_type=jnp.float32)
         grad = grad + factor_ref[pair, :1, :1] * product
@@ -347,101 +430,70 @@
         members = [[g * group + i for i in range(group)] for g in range(8)]
         block = lax.all_gather(own, "dp", axis=0, tiled=True, axis_index_groups=members)
 
-    made = {}
-    busy = set()
-    AX = {"X": to_x, "Y": to_y, "Z": to_z, "W": to_far}
-
-    def one(x):
-        return (x, 0)
-
-    ROUTE = CONFIG["route"]
-    TIES = CONFIG["ties"]
-    COST = CONFIG["cost"]
-
-    def tied(name, x):
-        t = [first(get(o)) for o in TIES.get(name, ())]
-        return after(x, *t) if t else x
-
-    def first(v):
-        return v[0] if isinstance(v, (list, tuple)) else v
-
-    def slab(v):
-        return (get(v), 0)
+    axes = {"X": to_x, "Y": to_y, "Z": to_z, "W": to_far}
+    places = {}
+    for pack_name, members in PACKS.items():
+        for i, x in enumerate(members):
+            places[("c" if x[0] == "a" else "d") + x[1]] = (pack_name, i)
+    sequence = list(KERNELS)
+    made = {"a0": block, "info": info}
+
+    def released(name, x):
+        waits = [get(other) for other in AFTER.get(name, ())]
+        return after(x, *(w[0] if isinstance(w, tuple) else w for w in waits)) if waits else x
 
     def get(name):
-        if name in made:
-            return made[name]
-        assert name not in busy, "cycle"
-        busy.add(name)
-        if name == "a0":
-            v = block
-        elif name == "own":
-            v = pack(get("a0"))
-        elif name in ROUTE:
-            parent, ax = ROUTE[name]
-            v = AX[ax](tied(name, get(parent)))
-        elif name in CONFIG["packs"]:
-            blocks = [get(x) for x in CONFIG["packs"][name]]
-            blocks[0] = tied(name, blocks[0])
-            v = to_core(pack(*blocks) if len(blocks) > 1 else blocks[0])
-        elif name in CONFIG["kernels"]:
-            v = kernel(name)
-        elif name == "lse_other":
-            v = to_y(get("K3")[0])
-        busy.discard(name)
-        made[name] = v
-        return v
-
-    where = {}
-    for pname, members in CONFIG["packs"].items():
-        for i, x in enumerate(members):
-            where[("c" if x[0] == "a" else "d") + x[1]] = (pname, i)
-
-    def handle(x):
-        if x in where:
-            pname, i = where[x]
-            return (get(pname), i)
-        return (get("own" if x == "a0" else x), 0)
-
-    KROWS, KCOLS = {}, {}
-    rr, cc = [], []
-    seq = list(CONFIG["kernels"])
-    prevk = {}
-    for k in seq:
-        nr, nc = CONFIG["kernels"][k]
-        prevk[k] = (list(rr), list(cc))
-        rr = rr + list(nr)
-        cc = cc + list(nc)
-        KROWS[k], KCOLS[k] = list(rr), list(cc)
-    PAIR = {"c": 1, "b": 2, "d": 3}
-
-    def kernel(k):
-        i = seq.index(k)
-        old = get(seq[i - 1]) if i else None
-        oldr, oldc = prevk[k]
-        rows = [handle(x) for x in KROWS[k]]
-        cols = [handle(x) for x in KCOLS[k]]
-        rows[0] = (tied(k, rows[0][0]), rows[0][1])
-        new_rows = tuple(range(len(oldr), len(KROWS[k])))
-        every = tuple(range(len(KROWS[k])))
-        plan = [(PAIR[x[0]], new_rows if n < len(oldc) else every) for n, x in enumerate(KCOLS[k])]
+        if name not in made:
+            made[name] = make(name)
+        return made[name]
+
+    def make(name):
+        if name == "own":
+            return pack(get("a0"))
+        if name in ROUTE:
+            parent, axis = ROUTE[name]
+            return axes[axis](released(name, get(parent)))
+        if name in PACKS:
+            blocks = [get(x) for x in PACKS[name]]
+            blocks[0] = released(name, blocks[0])
+            return to_core(pack(*blocks) if len(blocks) > 1 else blocks[0])
+        return column_sums(name)
+
+    def slab(x):
+        if x in places:
+            pack_name, i = places[x]
+            return get(pack_name), i
+        return get("own" if x == "a0" else x), 0
+
+    def column_sums(name):
+        step = sequence.index(name)
+        old = get(sequence[step - 1]) if step else None
+        rows = [x for k in sequence[: step + 1] for x in KERNELS[k][0]]
+        cols = [x for k in sequence[: step + 1] for x in KERNELS[k][1]]
+        every = tuple(range(len(rows)))
+        new_rows = every[len(rows) - len(KERNELS[name][0]) :]
+        n_old = len(cols) - len(KERNELS[name][1])
+        plan = [(PAIR[x[0]], new_rows if i < n_old else every) for i, x in enumerate(cols)]
         order = None
-        if i == len(seq) - 1:
-            order = tuple((PAIR[x[0]] - 1) * 4 + int(x[1]) // 2 for x in KCOLS[k])
-        return stats(info, size, rows, cols, plan, old, order=order, cost=COST.get(k, 4))
-
-    for name in CONFIG["emit"]:
+        if step == len(sequence) - 1:
+            order = tuple((PAIR[x[0]] - 1) * 4 + int(x[1]) // 2 for x in cols)
+        row_slabs = [slab(x) for x in rows]
+        col_slabs = [slab(x) for x in cols]
+        row_slabs[0] = (released(name, row_slabs[0][0]), row_slabs[0][1])
+        return tuple(stats(info, size, row_slabs, col_slabs, plan, old, order=order, cost=COST[name]))
+
+    for name in ROUTE:
         get(name)
     own_block = get("own")
-    lse = get(seq[-1])[0]
+    (lse,) = get(sequence[-1])
     lse_other = to_y(lse)
-    b, c, d = ([handle(p + str(i)) for i in range(8)] for p in "bcd")
+    b, c, d = ([slab(p + str(i)) for i in range(8)] for p in "bcd")
 
     partners = c + b + d
     pown = [c[0], b[0], d[0]]
     if group > 1:
         start = (lax.axis_index("dp") % group) * n
-        pown = [lax.dynamic_slice_in_dim(x, slab * size + start, n, 0) for x, slab in pown]
+        pown = [lax.dynamic_slice_in_dim(x, i * size + start, n, 0) for x, i in pown]
         gradient, losses = whole(info, size, own, pown, lse, lse_other, partners)
     else:
         half, losses, prob, score = own_half(info, own_block, lse, partners, pown)

time: 66.1 us -> 56.2 us (0.85)
  waiting for transfers between devices: 25.6 us -> 18.6 us
  Pallas kernels: 16.5 us -> 14.8 us
  starting transfers between devices: 20.8 us -> 19.5 us
    ppermute x24 -> x23, waiting for transfers between devices: 25.6 us -> 18.6 us  [send(): return lax.ppermute(block, ('dp', 'mod'), pairs)]
    ppermute x24 -> x23, starting transfers between devices: 20.8 us -> 19.5 us  [send(): return lax.ppermute(block, ('dp', 'mod'), pairs)]
    pallas_call x1, Pallas kernels: 5.63 us -> 4.38 us  [own_half(): pl.pallas_call(functools.partial(own_kernel, tuple(places), len(arrays)),...]
  transfers between devices with their start and end apart: 24 -> 23, of which waited for: 11 -> 7; matrix products, arithmetic and copies ran while one was open for 0% -> 0% of each run, Pallas kernels for 22% -> 23%
where the time goes in v3:
time: 56.2 us; the launch traced here: 56.1 us
  starting transfers between devices  19.5 us (35%)
  waiting for transfers between devices  18.6 us (33%)
  Pallas kernels  14.8 us (26%)
  local copies, waits for them, and re-layouts  2.31 us (4%)
  between operations  0.77 us (1%)
    ppermute x23, starting transfers between devices, send(): return lax.ppermute(block, ('dp', 'mod'), pairs)  19.5 us
    ppermute x23, waiting for transfers between devices, send(): return lax.ppermute(block, ('dp', 'mod'), pairs)  18.6 us
    pallas_call x3, Pallas kernels, stats(): pl.pallas_call(functools.partial(stats_kernel, size, tuple(places), len(a...  7.84 us
    pallas_call x1, Pallas kernels, own_half(): pl.pallas_call(functools.partial(own_kernel, tuple(places), len(arrays)),...  4.38 us
    unnamed x6, local copies, waits for them, and re-layouts  2.31 us
    pallas_call x1, Pallas kernels, other_half(): pl.pallas_call(functools.partial(other_kernel, tuple(places), len(arrays)...  1.8 us
  transfers between devices with their start and end apart: 23, of which 7 were waited for; matrix products, arithmetic and copies ran while one was open for 0% of the time, Pallas kernels for 23%

profile of v3, /device:TPU:0, one launch (start us, length us, event | category | flops | bytes accessed | tf_op | source)
XLA Modules:
  0.0 56.1 jit_solution(9533398747842523626)
XLA Ops:
  0.6 3.0 %collective-permute-start = (bf16[256,512]{1,0:T(8,128)(2,1)}, bf16[256,512]{1,0:T(8,128)(2,1)S(1)}, u32[]{:S(2)}, u32[]{:S(2)}) collective-permute-start(bf16[256,512]{1,0:T(8,128)(2,1)} %bitcast.2), channel_id=1, source_target_pairs={{0,4},{1,5},{2,6},{3,7},{4,0},{5,1},{6,2},{7,3},{8,12},{9,13},{10,... | collective-permute-start | bytes 786440 | tf_op jit(solution)/shard_map/ppermute | solution.py:411
  3.7 1.6 %collective-permute-start.1 = (bf16[256,512]{1,0:T(8,128)(2,1)}, bf16[256,512]{1,0:T(8,128)(2,1)S(1)}, u32[]{:S(2)}, u32[]{:S(2)}) collective-permute-start(bf16[256,512]{1,0:T(8,128)(2,1)} %bitcast.3), channel_id=1, source_target_pairs={{0,8},{1,9},{2,10},{3,11},{4,12},{5,13},{6,14},{7,15},{8,0},{9,1},... | collective-permute-start | bytes 786440 | tf_op jit(solution)/shard_map/ppermute | solution.py:411
  5.2 2.6 %collective-permute-start.2 = (bf16[256,512]{1,0:T(8,128)(2,1)}, bf16[256,512]{1,0:T(8,128)(2,1)S(1)}, u32[]{:S(2)}, u32[]{:S(2)}) collective-permute-start(bf16[256,512]{1,0:T(8,128)(2,1)} %bitcast.4), channel_id=1, source_target_pairs={{0,16},{1,17},{2,18},{3,19},{4,20},{5,21},{6,22},{7,23},{8,24},{9,... | collective-permute-start | bytes 786440 | tf_op jit(solution)/shard_map/ppermute | solution.py:411
  7.8 1.5 %collective-permute-start.5 = (bf16[256,512]{1,0:T(8,128)(2,1)}, bf16[256,512]{1,0:T(8,128)(2,1)S(1)}, u32[]{:S(2)}, u32[]{:S(2)}) collective-permute-start(bf16[256,512]{1,0:T(8,128)(2,1)} %bitcast.5), channel_id=1, source_target_pairs={{0,2},{1,3},{2,0},{3,1},{4,6},{5,7},{6,4},{7,5},{8,10},{9,11},{10,... | collective-permute-start | bytes 786440 | tf_op jit(solution)/shard_map/ppermute | solution.py:411
  9.3 1.0 %copy-done = bf16[1,256,512]{2,1,0:T(8,128)(2,1)S(1)} copy-done((bf16[1,256,512]{2,1,0:T(8,128)(2,1)S(1)}, bf16[1,256,512]{2,1,0:T(8,128)(2,1)}, u32[]{:S(2)}) %copy-start) | copy-done | bytes 262168
  10.3 0.7 %copy-done.1 = s32[3,4]{1,0:T(4,128)S(1)} copy-done((s32[3,4]{1,0:T(4,128)S(1)}, s32[3,4]{1,0:T(4,128)}, u32[]{:S(2)}) %copy-start.1) | copy-done | bytes 72
  11.0 0.7 %copy-done.2 = f32[3]{0:T(128)S(1)} copy-done((f32[3]{0:T(128)S(1)}, f32[3]{0:T(128)}, u32[]{:S(2)}) %copy-start.2) | copy-done | bytes 36
  11.7 0.6 %pair_factors.1.factor_ref = f32[6,8,256]{2,1,0:T(8,128)S(1)} custom-call(s32[3,4]{1,0:T(4,128)S(1)} %copy-done.1, f32[3]{0:T(128)S(1)} %copy-done.2), custom_call_target="tpu_custom_call" | custom-call | flops 1000 | bytes 1000 | tf_op jit(solution)/shard_map/pair_factors/pallas_call | solution.py:87
  12.3 0.6 %collective-permute-start.4 = (bf16[256,512]{1,0:T(8,128)(2,1)S(1)}, bf16[256,512]{1,0:T(8,128)(2,1)S(1)}, u32[]{:S(2)}, u32[]{:S(2)}) collective-permute-start(bf16[256,512]{1,0:T(8,128)(2,1)S(1)} %collective-permute-done.refs_1_.refs_3_), channel_id=1, source_target_pairs={{0,2},{1,3},{2,0},{3,1},{4,6},{5,7},{6,4},{7,5},{8,10},{9,11},{10,... | collective-permute-start | bytes 786440 | tf_op jit(solution)/shard_map/ppermute | solution.py:411
  12.9 4.2 %collective-permute-done.1.refs_0_.refs_2_ = bf16[256,512]{1,0:T(8,128)(2,1)S(1)} collective-permute-done((bf16[256,512]{1,0:T(8,128)(2,1)}, bf16[256,512]{1,0:T(8,128)(2,1)S(1)}, u32[]{:S(2)}, u32[]{:S(2)}) %collective-permute-start.1) | collective-permute-done | bytes 262176 | tf_op jit(solution)/shard_map/ppermute | solution.py:411
  17.5 2.0 %collective-permute-done.2.refs_1_.refs_3_ = bf16[256,512]{1,0:T(8,128)(2,1)S(1)} collective-permute-done((bf16[256,512]{1,0:T(8,128)(2,1)}, bf16[256,512]{1,0:T(8,128)(2,1)S(1)}, u32[]{:S(2)}, u32[]{:S(2)}) %collective-permute-start.2) | collective-permute-done | bytes 262176 | tf_op jit(solution)/shard_map/ppermute | solution.py:411
  19.7 1.2 %collective-permute-done.4.refs_1_.refs_6_.refs_3_ = bf16[256,512]{1,0:T(8,128)(2,1)S(1)} collective-permute-done((bf16[256,512]{1,0:T(8,128)(2,1)S(1)}, bf16[256,512]{1,0:T(8,128)(2,1)S(1)}, u32[]{:S(2)}, u32[]{:S(2)}) %collective-permute-start.4) | collective-permute-done | bytes 262176 | tf_op jit(solution)/shard_map/ppermute | solution.py:411
  21.3 1.5 %collective-permute-start.12 = (bf16[256,512]{1,0:T(8,128)(2,1)S(1)}, bf16[256,512]{1,0:T(8,128)(2,1)S(1)}, u32[]{:S(2)}, u32[]{:S(2)}) collective-permute-start(bf16[256,512]{1,0:T(8,128)(2,1)S(1)} %collective-permute-done.2.refs_1_.refs_3_), channel_id=1, source_target_pairs={{0,2},{1,3},{2,0},{3,1},{4,6},{5,7},{6,4},{7,5},{8,10},{9,11},{10,... | collective-permute-start | bytes 786440 | tf_op jit(solution)/shard_map/ppermute | solution.py:411
  22.8 1.2 %collective-permute-done.3.refs_4_.refs_2_ = bf16[256,512]{1,0:T(8,128)(2,1)S(1)} collective-permute-done((bf16[256,512]{1,0:T(8,128)(2,1)S(1)}, bf16[256,512]{1,0:T(8,128)(2,1)S(1)}, u32[]{:S(2)}, u32[]{:S(2)}) %collective-permute-start.3) | collective-permute-done | bytes 262176 | tf_op jit(solution)/shard_map/ppermute | solution.py:411
  24.0 0.7 %collective-permute-start.7 = (bf16[256,512]{1,0:T(8,128)(2,1)S(1)}, bf16[256,512]{1,0:T(8,128)(2,1)S(1)}, u32[]{:S(2)}, u32[]{:S(2)}) collective-permute-start(bf16[256,512]{1,0:T(8,128)(2,1)S(1)} %collective-permute-done.2.refs_1_.refs_3_), channel_id=1, source_target_pairs={{0,4},{1,5},{2,6},{3,7},{4,0},{5,1},{6,2},{7,3},{8,12},{9,13},{10,... | collective-permute-start | bytes 786440 | tf_op jit(solution)/shard_map/ppermute | solution.py:411
  24.7 3.7 %collective-permute-done.6.refs_0_.refs_5_ = bf16[256,512]{1,0:T(8,128)(2,1)S(1)} collective-permute-done((bf16[256,512]{1,0:T(8,128)(2,1)S(1)}, bf16[256,512]{1,0:T(8,128)(2,1)S(1)}, u32[]{:S(2)}, u32[]{:S(2)}) %collective-permute-start.6) | collective-permute-done | bytes 262176 | tf_op jit(solution)/shard_map/ppermute | solution.py:411
  28.4 1.5 %collective-permute-start.11 = (bf16[256,512]{1,0:T(8,128)(2,1)S(1)}, bf16[256,512]{1,0:T(8,128)(2,1)S(1)}, u32[]{:S(2)}, u32[]{:S(2)}) collective-permute-start(bf16[256,512]{1,0:T(8,128)(2,1)S(1)} %collective-permute-done.6.refs_0_.refs_5_), channel_id=1, source_target_pairs={{0,2},{1,3},{2,0},{3,1},{4,6},{5,7},{6,4},{7,5},{8,10},{9,11},{10,... | collective-permute-start | bytes 786440 | tf_op jit(solution)/shard_map/ppermute | solution.py:411
  29.9 0.6 collective-permute-start.13
  30.4 0.5 collective-permute-start.8
  30.9 4.0 %collective-permute-done.11.refs_11_ = bf16[256,512]{1,0:T(8,128)(2,1)S(1)} collective-permute-done((bf16[256,512]{1,0:T(8,128)(2,1)S(1)}, bf16[256,512]{1,0:T(8,128)(2,1)S(1)}, u32[]{:S(2)}, u32[]{:S(2)}) %collective-permute-start.11) | collective-permute-done | bytes 262176 | tf_op jit(solution)/shard_map/ppermute | solution.py:411
  34.9 1.5 %collective-permute-start.19 = (bf16[256,512]{1,0:T(8,128)(2,1)S(1)}, bf16[256,512]{1,0:T(8,128)(2,1)S(1)}, u32[]{:S(2)}, u32[]{:S(2)}) collective-permute-start(bf16[256,512]{1,0:T(8,128)(2,1)S(1)} %collective-permute-done.7.refs_0_.refs_6_), channel_id=1, source_target_pairs={{0,2},{1,3},{2,0},{3,1},{4,6},{5,7},{6,4},{7,5},{8,10},{9,11},{10,... | collective-permute-start | bytes 786440 | tf_op jit(solution)/shard_map/ppermute | solution.py:411
  36.4 0.8 %collective-permute-start.18 = (bf16[256,512]{1,0:T(8,128)(2,1)S(1)}, bf16[256,512]{1,0:T(8,128)(2,1)S(1)}, u32[]{:S(2)}, u32[]{:S(2)}) collective-permute-start(bf16[256,512]{1,0:T(8,128)(2,1)S(1)} %collective-permute-done.4.refs_1_.refs_6_.refs_3_), channel_id=1, source_target_pairs={{0,8},{1,9},{2,10},{3,11},{4,12},{5,13},{6,14},{7,15},{8,0},{9,1},... | collective-permute-start | bytes 786440 | tf_op jit(solution)/shard_map/ppermute | solution.py:411
  37.4 0.6 collective-permute-start.14
  38.0 0.5 collective-permute-start.17
  38.5 4.8 %col_stats.3 = (f32[8,8,256]{2,1,0:T(8,128)S(1)}, f32[8,8,256]{2,1,0:T(8,128)S(1)}) custom-call(f32[6,8,256]{2,1,0:T(8,128)S(1)} %pair_factors.1.factor_ref, bf16[256,512]{1,0:T(8,128)(2,1)S(1)} %pack.5.refs_0_.own_ref, bf16[256,512]{1,0:T(8,128)(2,1)S(1)} %collective-permute-done.refs_1_.refs_3_, ...), custom_call_target="tpu_custom_call" | custom-call | flops 85899345920 | bytes 1000 | tf_op jit(solution)/shard_map/col_stats/pallas_call | solution.py:173
  43.5 0.5 collective-permute-start.20
  44.1 2.2 %collective-permute-done.17.refs_12_.refs_6_ = bf16[256,512]{1,0:T(8,128)(2,1)S(1)} collective-permute-done((bf16[256,512]{1,0:T(8,128)(2,1)S(1)}, bf16[256,512]{1,0:T(8,128)(2,1)S(1)}, u32[]{:S(2)}, u32[]{:S(2)}) %collective-permute-start.17) | collective-permute-done | bytes 262176 | tf_op jit(solution)/shard_map/ppermute | solution.py:411
  46.3 1.4 %col_stats.4 = (f32[10,8,256]{2,1,0:T(8,128)S(1)}, f32[10,8,256]{2,1,0:T(8,128)S(1)}) custom-call(f32[6,8,256]{2,1,0:T(8,128)S(1)} %pair_factors.1.factor_ref, bf16[256,512]{1,0:T(8,128)(2,1)S(1)} %pack.5.refs_0_.own_ref, bf16[256,512]{1,0:T(8,128)(2,1)S(1)} %collective-permute-done.refs_1_.refs_3_, ...), custom_call_target="tpu_custom_call" | custom-call | flops 21474836480 | bytes 1000 | tf_op jit(solution)/shard_map/col_stats/pallas_call | solution.py:173
  47.8 1.5 %col_stats.5.lse_ref = f32[12,1,256]{2,1,0:T(1,128)S(1)} custom-call(f32[6,8,256]{2,1,0:T(8,128)S(1)} %pair_factors.1.factor_ref, bf16[256,512]{1,0:T(8,128)(2,1)S(1)} %pack.5.refs_0_.own_ref, bf16[256,512]{1,0:T(8,128)(2,1)S(1)} %collective-permute-done.refs_1_.refs_3_, bf16[256,512]{1,0:T(8,128)(2,1)S(1)} %collective-permute-done.1.refs_0_.refs_2_, ...), custom_call_target="tpu_custom_call" | custom-call | flops 5368709120 | bytes 1000 | tf_op jit(solution)/shard_map/col_stats/pallas_call | solution.py:173
  49.3 0.6 collective-permute-start.22
  49.9 4.4 %own_half.1 = (f32[256,512]{1,0:T(8,128)S(1)}, f32[1,256]{1,0:T(1,128)}, f32[24,256,256]{2,1,0:T(8,128)S(1)}, f32[12,256,256]{2,1,0:T(8,128)S(1)}) custom-call(f32[6,8,256]{2,1,0:T(8,128)S(1)} %pair_factors.1.factor_ref, bf16[256,512]{1,0:T(8,128)(2,1)S(1)} %pack.5.refs_0_.own_ref, f32[12,1,256]{2,1,0:T(1,128)S(1)} %col_stats.5.lse_ref, ...), custom_call_target="tpu_custom_call" | custom-call | flops 1000 | bytes 1000 | tf_op jit(solution)/shard_map/own_half/pallas_call | solution.py:282
  54.3 1.8 %other_half.1 = f32[256,512]{1,0:T(8,128)} custom-call(f32[6,8,256]{2,1,0:T(8,128)S(1)} %pair_factors.1.factor_ref, f32[256,512]{1,0:T(8,128)S(1)} %get-tuple-element.38.half_ref, f32[24,256,256]{2,1,0:T(8,128)S(1)} %get-tuple-element.39.prob, f32[12,256,256]{2,1,0:T(8,128)S(1)} %get-tuple-element.40.score, ...), custom_call_target="tpu_custom_call" | custom-call | flops 1000 | bytes 1000 | tf_op jit(solution)/shard_map/other_half/pallas_call | solution.py:314
  (31 shorter events, 1.3 us)
Async XLA Ops:
  0.6 11.6 %collective-permute-start = (bf16[256,512]{1,0:T(8,128)(2,1)}, bf16[256,512]{1,0:T(8,128)(2,1)S(1)}, u32[]{:S(2)}, u32[]{:S(2)}) collective-permute-start(bf16[256,512]{1,0:T(8,128)(2,1)} %bitcast.2), channel_id=1, source_target_pairs={{0,4},{1,5},{2,6},{3,7},{4,0},{5,1},{6,2},{7,3},{8,12},{9,13},{10,... | collective-permute-start | bytes 786440 | tf_op jit(solution)/shard_map/ppermute | solution.py:411
  3.7 13.5 %collective-permute-start.1 = (bf16[256,512]{1,0:T(8,128)(2,1)}, bf16[256,512]{1,0:T(8,128)(2,1)S(1)}, u32[]{:S(2)}, u32[]{:S(2)}) collective-permute-start(bf16[256,512]{1,0:T(8,128)(2,1)} %bitcast.3), channel_id=1, source_target_pairs={{0,8},{1,9},{2,10},{3,11},{4,12},{5,13},{6,14},{7,15},{8,0},{9,1},... | collective-permute-start | bytes 786440 | tf_op jit(solution)/shard_map/ppermute | solution.py:411
  5.2 14.3 %collective-permute-start.2 = (bf16[256,512]{1,0:T(8,128)(2,1)}, bf16[256,512]{1,0:T(8,128)(2,1)S(1)}, u32[]{:S(2)}, u32[]{:S(2)}) collective-permute-start(bf16[256,512]{1,0:T(8,128)(2,1)} %bitcast.4), channel_id=1, source_target_pairs={{0,16},{1,17},{2,18},{3,19},{4,20},{5,21},{6,22},{7,23},{8,24},{9,... | collective-permute-start | bytes 786440 | tf_op jit(solution)/shard_map/ppermute | solution.py:411
  7.8 11.7 %collective-permute-start.5 = (bf16[256,512]{1,0:T(8,128)(2,1)}, bf16[256,512]{1,0:T(8,128)(2,1)S(1)}, u32[]{:S(2)}, u32[]{:S(2)}) collective-permute-start(bf16[256,512]{1,0:T(8,128)(2,1)} %bitcast.5), channel_id=1, source_target_pairs={{0,2},{1,3},{2,0},{3,1},{4,6},{5,7},{6,4},{7,5},{8,10},{9,11},{10,... | collective-permute-start | bytes 786440 | tf_op jit(solution)/shard_map/ppermute | solution.py:411
  9.3 1.0 %copy-start = (bf16[1,256,512]{2,1,0:T(8,128)(2,1)S(1)}, bf16[1,256,512]{2,1,0:T(8,128)(2,1)}, u32[]{:S(2)}) copy-start(bf16[1,256,512]{2,1,0:T(8,128)(2,1)} %param.3) | copy-start | bytes 786436
  10.3 0.7 %copy-start.1 = (s32[3,4]{1,0:T(4,128)S(1)}, s32[3,4]{1,0:T(4,128)}, u32[]{:S(2)}) copy-start(s32[3,4]{1,0:T(4,128)} %pairings_ref.1) | copy-start | bytes 148
  11.0 0.7 %copy-start.2 = (f32[3]{0:T(128)S(1)}, f32[3]{0:T(128)}, u32[]{:S(2)}) copy-start(f32[3]{0:T(128)} %scale_ref.1) | copy-start | bytes 40
  12.3 8.6 %collective-permute-start.4 = (bf16[256,512]{1,0:T(8,128)(2,1)S(1)}, bf16[256,512]{1,0:T(8,128)(2,1)S(1)}, u32[]{:S(2)}, u32[]{:S(2)}) collective-permute-start(bf16[256,512]{1,0:T(8,128)(2,1)S(1)} %collective-permute-done.refs_1_.refs_3_), channel_id=1, source_target_pairs={{0,2},{1,3},{2,0},{3,1},{4,6},{5,7},{6,4},{7,5},{8,10},{9,11},{10,... | collective-permute-start | bytes 786440 | tf_op jit(solution)/shard_map/ppermute | solution.py:411
  17.1 6.9 %collective-permute-start.3 = (bf16[256,512]{1,0:T(8,128)(2,1)S(1)}, bf16[256,512]{1,0:T(8,128)(2,1)S(1)}, u32[]{:S(2)}, u32[]{:S(2)}) collective-permute-start(bf16[256,512]{1,0:T(8,128)(2,1)S(1)} %collective-permute-done.1.refs_0_.refs_2_), channel_id=1, source_target_pairs={{0,4},{1,5},{2,6},{3,7},{4,0},{5,1},{6,2},{7,3},{8,12},{9,13},{10,... | collective-permute-start | bytes 786440 | tf_op jit(solution)/shard_map/ppermute | solution.py:411
  19.6 18.4 %collective-permute-start.10 = (bf16[768,512]{1,0:T(8,128)(2,1)S(1)}, bf16[768,512]{1,0:T(8,128)(2,1)S(1)}, u32[]{:S(2)}, u32[]{:S(2)}) collective-permute-start(bf16[768,512]{1,0:T(8,128)(2,1)S(1)} %pack.6), channel_id=1, source_target_pairs={{0,1},{1,0},{2,3},{3,2},{4,5},{5,4},{6,7},{7,6},{8,9},{9,8},{10,11... | collective-permute-start | bytes 2359304 | tf_op jit(solution)/shard_map/ppermute | solution.py:411
  20.9 7.5 %collective-permute-start.6 = (bf16[256,512]{1,0:T(8,128)(2,1)S(1)}, bf16[256,512]{1,0:T(8,128)(2,1)S(1)}, u32[]{:S(2)}, u32[]{:S(2)}) collective-permute-start(bf16[256,512]{1,0:T(8,128)(2,1)S(1)} %collective-permute-done.2.refs_1_.refs_3_), channel_id=1, source_target_pairs={{0,8},{1,9},{2,10},{3,11},{4,12},{5,13},{6,14},{7,15},{8,0},{9,1},... | collective-permute-start | bytes 786440 | tf_op jit(solution)/shard_map/ppermute | solution.py:411
  21.3 8.5 %collective-permute-start.12 = (bf16[256,512]{1,0:T(8,128)(2,1)S(1)}, bf16[256,512]{1,0:T(8,128)(2,1)S(1)}, u32[]{:S(2)}, u32[]{:S(2)}) collective-permute-start(bf16[256,512]{1,0:T(8,128)(2,1)S(1)} %collective-permute-done.2.refs_1_.refs_3_), channel_id=1, source_target_pairs={{0,2},{1,3},{2,0},{3,1},{4,6},{5,7},{6,4},{7,5},{8,10},{9,11},{10,... | collective-permute-start | bytes 786440 | tf_op jit(solution)/shard_map/ppermute | solution.py:411
  24.0 6.9 %collective-permute-start.7 = (bf16[256,512]{1,0:T(8,128)(2,1)S(1)}, bf16[256,512]{1,0:T(8,128)(2,1)S(1)}, u32[]{:S(2)}, u32[]{:S(2)}) collective-permute-start(bf16[256,512]{1,0:T(8,128)(2,1)S(1)} %collective-permute-done.2.refs_1_.refs_3_), channel_id=1, source_target_pairs={{0,4},{1,5},{2,6},{3,7},{4,0},{5,1},{6,2},{7,3},{8,12},{9,13},{10,... | collective-permute-start | bytes 786440 | tf_op jit(solution)/shard_map/ppermute | solution.py:411
  28.4 6.6 %collective-permute-start.11 = (bf16[256,512]{1,0:T(8,128)(2,1)S(1)}, bf16[256,512]{1,0:T(8,128)(2,1)S(1)}, u32[]{:S(2)}, u32[]{:S(2)}) collective-permute-start(bf16[256,512]{1,0:T(8,128)(2,1)S(1)} %collective-permute-done.6.refs_0_.refs_5_), channel_id=1, source_target_pairs={{0,2},{1,3},{2,0},{3,1},{4,6},{5,7},{6,4},{7,5},{8,10},{9,11},{10,... | collective-permute-start | bytes 786440 | tf_op jit(solution)/shard_map/ppermute | solution.py:411
  29.9 6.6 %collective-permute-start.13 = (bf16[256,512]{1,0:T(8,128)(2,1)S(1)}, bf16[256,512]{1,0:T(8,128)(2,1)S(1)}, u32[]{:S(2)}, u32[]{:S(2)}) collective-permute-start(bf16[256,512]{1,0:T(8,128)(2,1)S(1)} %collective-permute-done.5.refs_2_.refs_8_.refs_5_), channel_id=1, source_target_pairs={{0,8},{1,9},{2,10},{3,11},{4,12},{5,13},{6,14},{7,15},{8,0},{9,1},... | collective-permute-start | bytes 786440 | tf_op jit(solution)/shard_map/ppermute | solution.py:411
  30.4 6.9 %collective-permute-start.8 = (bf16[256,512]{1,0:T(8,128)(2,1)S(1)}, bf16[256,512]{1,0:T(8,128)(2,1)S(1)}, u32[]{:S(2)}, u32[]{:S(2)}) collective-permute-start(bf16[256,512]{1,0:T(8,128)(2,1)S(1)} %collective-permute-done.6.refs_0_.refs_5_), channel_id=1, source_target_pairs={{0,4},{1,5},{2,6},{3,7},{4,0},{5,1},{6,2},{7,3},{8,12},{9,13},{10,... | collective-permute-start | bytes 786440 | tf_op jit(solution)/shard_map/ppermute | solution.py:411
  30.9 6.5 %collective-permute-start.9 = (bf16[256,512]{1,0:T(8,128)(2,1)}, bf16[256,512]{1,0:T(8,128)(2,1)S(1)}, u32[]{:S(2)}, u32[]{:S(2)}) collective-permute-start(bf16[256,512]{1,0:T(8,128)(2,1)} %bitcast.6), channel_id=1, source_target_pairs={{0,1},{1,0},{2,3},{3,2},{4,5},{5,4},{6,7},{7,6},{8,9},{9,8},{10,11... | collective-permute-start | bytes 786440 | tf_op jit(solution)/shard_map/ppermute | solution.py:411
  34.9 8.4 %collective-permute-start.19 = (bf16[256,512]{1,0:T(8,128)(2,1)S(1)}, bf16[256,512]{1,0:T(8,128)(2,1)S(1)}, u32[]{:S(2)}, u32[]{:S(2)}) collective-permute-start(bf16[256,512]{1,0:T(8,128)(2,1)S(1)} %collective-permute-done.7.refs_0_.refs_6_), channel_id=1, source_target_pairs={{0,2},{1,3},{2,0},{3,1},{4,6},{5,7},{6,4},{7,5},{8,10},{9,11},{10,... | collective-permute-start | bytes 786440 | tf_op jit(solution)/shard_map/ppermute | solution.py:411
  36.4 7.0 %collective-permute-start.18 = (bf16[256,512]{1,0:T(8,128)(2,1)S(1)}, bf16[256,512]{1,0:T(8,128)(2,1)S(1)}, u32[]{:S(2)}, u32[]{:S(2)}) collective-permute-start(bf16[256,512]{1,0:T(8,128)(2,1)S(1)} %collective-permute-done.4.refs_1_.refs_6_.refs_3_), channel_id=1, source_target_pairs={{0,8},{1,9},{2,10},{3,11},{4,12},{5,13},{6,14},{7,15},{8,0},{9,1},... | collective-permute-start | bytes 786440 | tf_op jit(solution)/shard_map/ppermute | solution.py:411
  37.3 9.0 %collective-permute-start.15 = (bf16[768,512]{1,0:T(8,128)(2,1)S(1)}, bf16[768,512]{1,0:T(8,128)(2,1)S(1)}, u32[]{:S(2)}, u32[]{:S(2)}) collective-permute-start(bf16[768,512]{1,0:T(8,128)(2,1)S(1)} %pack.8), channel_id=1, source_target_pairs={{0,1},{1,0},{2,3},{3,2},{4,5},{5,4},{6,7},{7,6},{8,9},{9,8},{10,11... | collective-permute-start | bytes 2359304 | tf_op jit(solution)/shard_map/ppermute | solution.py:411
  37.4 8.9 %collective-permute-start.14 = (bf16[768,512]{1,0:T(8,128)(2,1)S(1)}, bf16[768,512]{1,0:T(8,128)(2,1)S(1)}, u32[]{:S(2)}, u32[]{:S(2)}) collective-permute-start(bf16[768,512]{1,0:T(8,128)(2,1)S(1)} %pack.7), channel_id=1, source_target_pairs={{0,1},{1,0},{2,3},{3,2},{4,5},{5,4},{6,7},{7,6},{8,9},{9,8},{10,11... | collective-permute-start | bytes 2359304 | tf_op jit(solution)/shard_map/ppermute | solution.py:411
  38.0 8.3 %collective-permute-start.17 = (bf16[256,512]{1,0:T(8,128)(2,1)S(1)}, bf16[256,512]{1,0:T(8,128)(2,1)S(1)}, u32[]{:S(2)}, u32[]{:S(2)}) collective-permute-start(bf16[256,512]{1,0:T(8,128)(2,1)S(1)} %collective-permute-done.11.refs_11_), channel_id=1, source_target_pairs={{0,4},{1,5},{2,6},{3,7},{4,0},{5,1},{6,2},{7,3},{8,12},{9,13},{10,... | collective-permute-start | bytes 786440 | tf_op jit(solution)/shard_map/ppermute | solution.py:411
  43.4 4.4 %collective-permute-start.16 = (bf16[256,512]{1,0:T(8,128)(2,1)S(1)}, bf16[256,512]{1,0:T(8,128)(2,1)S(1)}, u32[]{:S(2)}, u32[]{:S(2)}) collective-permute-start(bf16[256,512]{1,0:T(8,128)(2,1)S(1)} %collective-permute-done.11.refs_11_), channel_id=1, source_target_pairs={{0,1},{1,0},{2,3},{3,2},{4,5},{5,4},{6,7},{7,6},{8,9},{9,8},{10,11... | collective-permute-start | bytes 786440 | tf_op jit(solution)/shard_map/ppermute | solution.py:411
  43.5 6.3 %collective-permute-start.20 = (bf16[1024,512]{1,0:T(8,128)(2,1)S(1)}, bf16[1024,512]{1,0:T(8,128)(2,1)S(1)}, u32[]{:S(2)}, u32[]{:S(2)}) collective-permute-start(bf16[1024,512]{1,0:T(8,128)(2,1)S(1)} %pack.9), channel_id=1, source_target_pairs={{0,1},{1,0},{2,3},{3,2},{4,5},{5,4},{6,7},{7,6},{8,9},{9,8},{10,11... | collective-permute-start | bytes 3145736 | tf_op jit(solution)/shard_map/ppermute | solution.py:411
  46.3 3.6 %collective-permute-start.21 = (bf16[256,512]{1,0:T(8,128)(2,1)S(1)}, bf16[256,512]{1,0:T(8,128)(2,1)S(1)}, u32[]{:S(2)}, u32[]{:S(2)}) collective-permute-start(bf16[256,512]{1,0:T(8,128)(2,1)S(1)} %collective-permute-done.17.refs_12_.refs_6_), channel_id=1, source_target_pairs={{0,1},{1,0},{2,3},{3,2},{4,5},{5,4},{6,7},{7,6},{8,9},{9,8},{10,11... | collective-permute-start | bytes 786440 | tf_op jit(solution)/shard_map/ppermute | solution.py:411
  49.3 4.9 %collective-permute-start.22 = (f32[12,1,256]{2,1,0:T(1,128)S(1)}, f32[12,1,256]{2,1,0:T(1,128)S(1)}, u32[]{:S(2)}, u32[]{:S(2)}) collective-permute-start(f32[12,1,256]{2,1,0:T(1,128)S(1)} %col_stats.5.lse_ref), channel_id=1, source_target_pairs={{0,4},{1,5},{2,6},{3,7},{4,0},{5,1},{6,2},{7,3},{8,12},{9,13},{10,... | collective-permute-start | bytes 36872 | tf_op jit(solution)/shard_map/ppermute | solution.py:411

commit v4 on v3

--- a/solution.py
+++ b/solution.py
@@ -17,12 +17,12 @@
     "a2": ("a0", "Z"),
     "a4": ("a0", "W"),
     "a1": ("a0", "Y"),
-    "b0": ("a0", "X"),
+    "a5": ("a4", "Y"),
     "b1": ("a1", "X"),
     "a3": ("a2", "Y"),
     "a6": ("a4", "Z"),
     "b4": ("a4", "X"),
-    "a5": ("a4", "Y"),
+    "b0": ("a0", "X"),
     "b2": ("b0", "Z"),
     "b6": ("a6", "X"),
     "a7": ("a6", "Y"),
@@ -39,30 +39,26 @@
     "b5": ("b6",),
     "P4": ("b0", "b5"),
     "P1": ("a1",),
-    "P3": ("b4",),
-    "K2": ("b7", "b1", "a4"),
     "K1": ("a3",),
     "P5": ("a6",),
     "b1": ("own", "info"),
+    "P9": ("K3",),
+    "P3": ("a4", "info"),
 }
 PACKS = {
     "P1": ("a2", "a4", "b0"),
-    "P2": ("a6", "b1", "a7"),
-    "P3": ("a5", "b4", "b2"),
+    "P2": ("a6", "b1", "a7", "b6", "a5", "b4", "b2"),
     "P4": ("b3", "b5", "a3", "a1"),
-    "P7": ("b6",),
     "P11": ("a0",),
     "P9": ("b7",),
 }
 KERNELS = {
     "K1": (("a0", "a1", "a2", "a4", "a3", "a6", "a5", "a7"), ("b0", "c0", "c2", "c4", "d0", "b6", "b2", "b4")),
-    "K2": ((), ("c6", "d2")),
-    "K3": ((), ("d4", "d6")),
+    "K3": ((), ("c6", "d2", "d4", "d6")),
 }
 COST = {
     "K1": 40,
-    "K2": 40,
-    "K3": 10,
+    "K3": 20,
 }
 PAIR = {"c": 1, "b": 2, "d": 3}
 

time: 56.2 us -> 54.2 us (0.964)
  waiting for transfers between devices: 18.6 us -> 16.7 us
    ppermute x23 -> x21, waiting for transfers between devices: 18.6 us -> 16.7 us  [send(): return lax.ppermute(block, ('dp', 'mod'), pairs)]
    pallas_call x3 -> x2, Pallas kernels: 7.84 us -> 7.53 us  [stats(): pl.pallas_call(functools.partial(stats_kernel, size, tuple(places), len(a...]
    ppermute x23 -> x21, starting transfers between devices: 19.5 us -> 19.7 us  [send(): return lax.ppermute(block, ('dp', 'mod'), pairs)]
  transfers between devices with their start and end apart: 23 -> 21, of which waited for: 7 -> 7; matrix products, arithmetic and copies ran while one was open for 0% -> 0% of each run, Pallas kernels for 23% -> 24%
where the time goes in v4:
time: 54.2 us; the launch traced here: 54 us
  starting transfers between devices  19.7 us (36%)
  waiting for transfers between devices  16.7 us (31%)
  Pallas kernels  14.6 us (27%)
  local copies, waits for them, and re-layouts  2.31 us (4%)
  between operations  0.74 us (1%)
    ppermute x21, starting transfers between devices, send(): return lax.ppermute(block, ('dp', 'mod'), pairs)  19.7 us
    ppermute x21, waiting for transfers between devices, send(): return lax.ppermute(block, ('dp', 'mod'), pairs)  16.7 us
    pallas_call x2, Pallas kernels, stats(): pl.pallas_call(functools.partial(stats_kernel, size, tuple(places), len(a...  7.53 us
    pallas_call x1, Pallas kernels, own_half(): pl.pallas_call(functools.partial(own_kernel, tuple(places), len(arrays)),...  4.39 us
    unnamed x6, local copies, waits for them, and re-layouts  2.31 us
    pallas_call x1, Pallas kernels, other_half(): pl.pallas_call(functools.partial(other_kernel, tuple(places), len(arrays)...  1.8 us
  transfers between devices with their start and end apart: 21, of which 7 were waited for; matrix products, arithmetic and copies ran while one was open for 0% of the time, Pallas kernels for 24%

profile of v4, /device:TPU:0, one launch (start us, length us, event | category | flops | bytes accessed | tf_op | source)
XLA Modules:
  0.0 54.0 jit_solution(235906503855878969)
XLA Ops:
  0.6 3.0 %collective-permute-start = (bf16[256,512]{1,0:T(8,128)(2,1)}, bf16[256,512]{1,0:T(8,128)(2,1)S(1)}, u32[]{:S(2)}, u32[]{:S(2)}) collective-permute-start(bf16[256,512]{1,0:T(8,128)(2,1)} %bitcast.2), channel_id=1, source_target_pairs={{0,4},{1,5},{2,6},{3,7},{4,0},{5,1},{6,2},{7,3},{8,12},{9,13},{10,... | collective-permute-start | bytes 786440 | tf_op jit(solution)/shard_map/ppermute | solution.py:407
  3.7 1.6 %collective-permute-start.1 = (bf16[256,512]{1,0:T(8,128)(2,1)}, bf16[256,512]{1,0:T(8,128)(2,1)S(1)}, u32[]{:S(2)}, u32[]{:S(2)}) collective-permute-start(bf16[256,512]{1,0:T(8,128)(2,1)} %bitcast.3), channel_id=1, source_target_pairs={{0,8},{1,9},{2,10},{3,11},{4,12},{5,13},{6,14},{7,15},{8,0},{9,1},... | collective-permute-start | bytes 786440 | tf_op jit(solution)/shard_map/ppermute | solution.py:407
  5.2 2.6 %collective-permute-start.2 = (bf16[256,512]{1,0:T(8,128)(2,1)}, bf16[256,512]{1,0:T(8,128)(2,1)S(1)}, u32[]{:S(2)}, u32[]{:S(2)}) collective-permute-start(bf16[256,512]{1,0:T(8,128)(2,1)} %bitcast.4), channel_id=1, source_target_pairs={{0,16},{1,17},{2,18},{3,19},{4,20},{5,21},{6,22},{7,23},{8,24},{9,... | collective-permute-start | bytes 786440 | tf_op jit(solution)/shard_map/ppermute | solution.py:407
  7.8 1.5 %collective-permute-start.5 = (bf16[256,512]{1,0:T(8,128)(2,1)}, bf16[256,512]{1,0:T(8,128)(2,1)S(1)}, u32[]{:S(2)}, u32[]{:S(2)}) collective-permute-start(bf16[256,512]{1,0:T(8,128)(2,1)} %bitcast.5), channel_id=1, source_target_pairs={{0,2},{1,3},{2,0},{3,1},{4,6},{5,7},{6,4},{7,5},{8,10},{9,11},{10,... | collective-permute-start | bytes 786440 | tf_op jit(solution)/shard_map/ppermute | solution.py:407
  9.3 1.0 %copy-done = bf16[1,256,512]{2,1,0:T(8,128)(2,1)S(1)} copy-done((bf16[1,256,512]{2,1,0:T(8,128)(2,1)S(1)}, bf16[1,256,512]{2,1,0:T(8,128)(2,1)}, u32[]{:S(2)}) %copy-start) | copy-done | bytes 262168
  10.3 0.7 %copy-done.1 = s32[3,4]{1,0:T(4,128)S(1)} copy-done((s32[3,4]{1,0:T(4,128)S(1)}, s32[3,4]{1,0:T(4,128)}, u32[]{:S(2)}) %copy-start.1) | copy-done | bytes 72
  11.0 0.7 %copy-done.2 = f32[3]{0:T(128)S(1)} copy-done((f32[3]{0:T(128)S(1)}, f32[3]{0:T(128)}, u32[]{:S(2)}) %copy-start.2) | copy-done | bytes 36
  11.7 0.6 %pair_factors.1.factor_ref = f32[6,8,256]{2,1,0:T(8,128)S(1)} custom-call(s32[3,4]{1,0:T(4,128)S(1)} %copy-done.1, f32[3]{0:T(128)S(1)} %copy-done.2), custom_call_target="tpu_custom_call" | custom-call | flops 1000 | bytes 1000 | tf_op jit(solution)/shard_map/pair_factors/pallas_call | solution.py:83
  12.3 0.6 %collective-permute-start.4 = (bf16[256,512]{1,0:T(8,128)(2,1)S(1)}, bf16[256,512]{1,0:T(8,128)(2,1)S(1)}, u32[]{:S(2)}, u32[]{:S(2)}) collective-permute-start(bf16[256,512]{1,0:T(8,128)(2,1)S(1)} %collective-permute-done.refs_1_.refs_3_), channel_id=1, source_target_pairs={{0,2},{1,3},{2,0},{3,1},{4,6},{5,7},{6,4},{7,5},{8,10},{9,11},{10,... | collective-permute-start | bytes 786440 | tf_op jit(solution)/shard_map/ppermute | solution.py:407
  12.9 4.2 %collective-permute-done.1.refs_0_.refs_2_ = bf16[256,512]{1,0:T(8,128)(2,1)S(1)} collective-permute-done((bf16[256,512]{1,0:T(8,128)(2,1)}, bf16[256,512]{1,0:T(8,128)(2,1)S(1)}, u32[]{:S(2)}, u32[]{:S(2)}) %collective-permute-start.1) | collective-permute-done | bytes 262176 | tf_op jit(solution)/shard_map/ppermute | solution.py:407
  17.1 0.4 collective-permute-start.3
  17.5 2.0 %collective-permute-done.2.refs_1_.refs_3_ = bf16[256,512]{1,0:T(8,128)(2,1)S(1)} collective-permute-done((bf16[256,512]{1,0:T(8,128)(2,1)}, bf16[256,512]{1,0:T(8,128)(2,1)S(1)}, u32[]{:S(2)}, u32[]{:S(2)}) %collective-permute-start.2) | collective-permute-done | bytes 262176 | tf_op jit(solution)/shard_map/ppermute | solution.py:407
  19.7 1.2 %collective-permute-done.4.refs_1_.refs_5_.refs_2_ = bf16[256,512]{1,0:T(8,128)(2,1)S(1)} collective-permute-done((bf16[256,512]{1,0:T(8,128)(2,1)S(1)}, bf16[256,512]{1,0:T(8,128)(2,1)S(1)}, u32[]{:S(2)}, u32[]{:S(2)}) %collective-permute-start.4) | collective-permute-done | bytes 262176 | tf_op jit(solution)/shard_map/ppermute | solution.py:407
  20.9 0.4 collective-permute-start.6
  21.3 1.5 %collective-permute-start.12 = (bf16[256,512]{1,0:T(8,128)(2,1)S(1)}, bf16[256,512]{1,0:T(8,128)(2,1)S(1)}, u32[]{:S(2)}, u32[]{:S(2)}) collective-permute-start(bf16[256,512]{1,0:T(8,128)(2,1)S(1)} %collective-permute-done.2.refs_1_.refs_3_), channel_id=1, source_target_pairs={{0,2},{1,3},{2,0},{3,1},{4,6},{5,7},{6,4},{7,5},{8,10},{9,11},{10,... | collective-permute-start | bytes 786440 | tf_op jit(solution)/shard_map/ppermute | solution.py:407
  22.8 1.2 %collective-permute-done.3.refs_4_.refs_2_ = bf16[256,512]{1,0:T(8,128)(2,1)S(1)} collective-permute-done((bf16[256,512]{1,0:T(8,128)(2,1)S(1)}, bf16[256,512]{1,0:T(8,128)(2,1)S(1)}, u32[]{:S(2)}, u32[]{:S(2)}) %collective-permute-start.3) | collective-permute-done | bytes 262176 | tf_op jit(solution)/shard_map/ppermute | solution.py:407
  24.0 0.7 %collective-permute-start.7 = (bf16[256,512]{1,0:T(8,128)(2,1)S(1)}, bf16[256,512]{1,0:T(8,128)(2,1)S(1)}, u32[]{:S(2)}, u32[]{:S(2)}) collective-permute-start(bf16[256,512]{1,0:T(8,128)(2,1)S(1)} %collective-permute-done.2.refs_1_.refs_3_), channel_id=1, source_target_pairs={{0,4},{1,5},{2,6},{3,7},{4,0},{5,1},{6,2},{7,3},{8,12},{9,13},{10,... | collective-permute-start | bytes 786440 | tf_op jit(solution)/shard_map/ppermute | solution.py:407
  24.7 3.7 %collective-permute-done.6.refs_0_.refs_5_ = bf16[256,512]{1,0:T(8,128)(2,1)S(1)} collective-permute-done((bf16[256,512]{1,0:T(8,128)(2,1)S(1)}, bf16[256,512]{1,0:T(8,128)(2,1)S(1)}, u32[]{:S(2)}, u32[]{:S(2)}) %collective-permute-start.6) | collective-permute-done | bytes 262176 | tf_op jit(solution)/shard_map/ppermute | solution.py:407
  28.4 1.5 %collective-permute-start.11 = (bf16[256,512]{1,0:T(8,128)(2,1)S(1)}, bf16[256,512]{1,0:T(8,128)(2,1)S(1)}, u32[]{:S(2)}, u32[]{:S(2)}) collective-permute-start(bf16[256,512]{1,0:T(8,128)(2,1)S(1)} %collective-permute-done.6.refs_0_.refs_5_), channel_id=1, source_target_pairs={{0,2},{1,3},{2,0},{3,1},{4,6},{5,7},{6,4},{7,5},{8,10},{9,11},{10,... | collective-permute-start | bytes 786440 | tf_op jit(solution)/shard_map/ppermute | solution.py:407
  29.9 0.6 %collective-permute-start.13 = (bf16[256,512]{1,0:T(8,128)(2,1)S(1)}, bf16[256,512]{1,0:T(8,128)(2,1)S(1)}, u32[]{:S(2)}, u32[]{:S(2)}) collective-permute-start(bf16[256,512]{1,0:T(8,128)(2,1)S(1)} %collective-permute-done.5.refs_2_.refs_8_.refs_4_), channel_id=1, source_target_pairs={{0,8},{1,9},{2,10},{3,11},{4,12},{5,13},{6,14},{7,15},{8,0},{9,1},... | collective-permute-start | bytes 786440 | tf_op jit(solution)/shard_map/ppermute | solution.py:407
  30.4 0.5 collective-permute-start.8
  30.9 4.0 %collective-permute-done.11.refs_3_.refs_11_.refs_10_ = bf16[256,512]{1,0:T(8,128)(2,1)S(1)} collective-permute-done((bf16[256,512]{1,0:T(8,128)(2,1)S(1)}, bf16[256,512]{1,0:T(8,128)(2,1)S(1)}, u32[]{:S(2)}, u32[]{:S(2)}) %collective-permute-start.11) | collective-permute-done | bytes 262176 | tf_op jit(solution)/shard_map/ppermute | solution.py:407
  34.9 1.5 %collective-permute-start.16 = (bf16[256,512]{1,0:T(8,128)(2,1)S(1)}, bf16[256,512]{1,0:T(8,128)(2,1)S(1)}, u32[]{:S(2)}, u32[]{:S(2)}) collective-permute-start(bf16[256,512]{1,0:T(8,128)(2,1)S(1)} %collective-permute-done.7.refs_4_.refs_6_), channel_id=1, source_target_pairs={{0,2},{1,3},{2,0},{3,1},{4,6},{5,7},{6,4},{7,5},{8,10},{9,11},{10,... | collective-permute-start | bytes 786440 | tf_op jit(solution)/shard_map/ppermute | solution.py:407
  36.4 0.8 %collective-permute-start.15 = (bf16[256,512]{1,0:T(8,128)(2,1)S(1)}, bf16[256,512]{1,0:T(8,128)(2,1)S(1)}, u32[]{:S(2)}, u32[]{:S(2)}) collective-permute-start(bf16[256,512]{1,0:T(8,128)(2,1)S(1)} %collective-permute-done.4.refs_1_.refs_5_.refs_2_), channel_id=1, source_target_pairs={{0,8},{1,9},{2,10},{3,11},{4,12},{5,13},{6,14},{7,15},{8,0},{9,1},... | collective-permute-start | bytes 786440 | tf_op jit(solution)/shard_map/ppermute | solution.py:407
  37.4 0.6 %collective-permute-start.18 = (bf16[256,512]{1,0:T(8,128)(2,1)S(1)}, bf16[256,512]{1,0:T(8,128)(2,1)S(1)}, u32[]{:S(2)}, u32[]{:S(2)}) collective-permute-start(bf16[256,512]{1,0:T(8,128)(2,1)S(1)} %collective-permute-done.11.refs_3_.refs_11_.refs_10_), channel_id=1, source_target_pairs={{0,4},{1,5},{2,6},{3,7},{4,0},{5,1},{6,2},{7,3},{8,12},{9,13},{10,... | collective-permute-start | bytes 786440 | tf_op jit(solution)/shard_map/ppermute | solution.py:407
  38.0 4.8 %col_stats.2 = (f32[8,8,256]{2,1,0:T(8,128)S(1)}, f32[8,8,256]{2,1,0:T(8,128)S(1)}) custom-call(f32[6,8,256]{2,1,0:T(8,128)S(1)} %pair_factors.1.factor_ref, bf16[256,512]{1,0:T(8,128)(2,1)S(1)} %pack.4.refs_0_.own_ref, bf16[256,512]{1,0:T(8,128)(2,1)S(1)} %collective-permute-done.refs_1_.refs_3_, ...), custom_call_target="tpu_custom_call" | custom-call | flops 85899345920 | bytes 1000 | tf_op jit(solution)/shard_map/col_stats/pallas_call | solution.py:169
  43.0 0.2 collective-permute-start.17
  43.2 2.7 %col_stats.3.lse_ref = f32[12,1,256]{2,1,0:T(1,128)S(1)} custom-call(f32[6,8,256]{2,1,0:T(8,128)S(1)} %pair_factors.1.factor_ref, bf16[256,512]{1,0:T(8,128)(2,1)S(1)} %pack.4.refs_0_.own_ref, bf16[256,512]{1,0:T(8,128)(2,1)S(1)} %collective-permute-done.refs_1_.refs_3_, bf16[256,512]{1,0:T(8,128)(2,1)S(1)} %collective-permute-done.1.refs_0_.refs_2_, ...), custom_call_target="tpu_custom_call" | custom-call | flops 21474836480 | bytes 1000 | tf_op jit(solution)/shard_map/col_stats/pallas_call | solution.py:169
  45.9 0.3 collective-permute-done.18.refs_11_.refs_5_
  46.3 1.5 %collective-permute-start.20 = (f32[12,1,256]{2,1,0:T(1,128)S(1)}, f32[12,1,256]{2,1,0:T(1,128)S(1)}, u32[]{:S(2)}, u32[]{:S(2)}) collective-permute-start(f32[12,1,256]{2,1,0:T(1,128)S(1)} %col_stats.3.lse_ref), channel_id=1, source_target_pairs={{0,4},{1,5},{2,6},{3,7},{4,0},{5,1},{6,2},{7,3},{8,12},{9,13},{10,... | collective-permute-start | bytes 36872 | tf_op jit(solution)/shard_map/ppermute | solution.py:407
  47.9 4.4 %own_half.1 = (f32[256,512]{1,0:T(8,128)S(1)}, f32[1,256]{1,0:T(1,128)}, f32[24,256,256]{2,1,0:T(8,128)S(1)}, f32[12,256,256]{2,1,0:T(8,128)S(1)}) custom-call(f32[6,8,256]{2,1,0:T(8,128)S(1)} %pair_factors.1.factor_ref, bf16[256,512]{1,0:T(8,128)(2,1)S(1)} %pack.4.refs_0_.own_ref, f32[12,1,256]{2,1,0:T(1,128)S(1)} %col_stats.3.lse_ref, ...), custom_call_target="tpu_custom_call" | custom-call | flops 1000 | bytes 1000 | tf_op jit(solution)/shard_map/own_half/pallas_call | solution.py:278
  52.2 1.8 %other_half.1 = f32[256,512]{1,0:T(8,128)} custom-call(f32[6,8,256]{2,1,0:T(8,128)S(1)} %pair_factors.1.factor_ref, f32[256,512]{1,0:T(8,128)S(1)} %get-tuple-element.32.half_ref, f32[24,256,256]{2,1,0:T(8,128)S(1)} %get-tuple-element.33.prob, f32[12,256,256]{2,1,0:T(8,128)S(1)} %get-tuple-element.34.score, ...), custom_call_target="tpu_custom_call" | custom-call | flops 1000 | bytes 1000 | tf_op jit(solution)/shard_map/other_half/pallas_call | solution.py:310
  (25 shorter events, 0.6 us)
Async XLA Ops:
  0.6 11.6 %collective-permute-start = (bf16[256,512]{1,0:T(8,128)(2,1)}, bf16[256,512]{1,0:T(8,128)(2,1)S(1)}, u32[]{:S(2)}, u32[]{:S(2)}) collective-permute-start(bf16[256,512]{1,0:T(8,128)(2,1)} %bitcast.2), channel_id=1, source_target_pairs={{0,4},{1,5},{2,6},{3,7},{4,0},{5,1},{6,2},{7,3},{8,12},{9,13},{10,... | collective-permute-start | bytes 786440 | tf_op jit(solution)/shard_map/ppermute | solution.py:407
  3.7 13.5 %collective-permute-start.1 = (bf16[256,512]{1,0:T(8,128)(2,1)}, bf16[256,512]{1,0:T(8,128)(2,1)S(1)}, u32[]{:S(2)}, u32[]{:S(2)}) collective-permute-start(bf16[256,512]{1,0:T(8,128)(2,1)} %bitcast.3), channel_id=1, source_target_pairs={{0,8},{1,9},{2,10},{3,11},{4,12},{5,13},{6,14},{7,15},{8,0},{9,1},... | collective-permute-start | bytes 786440 | tf_op jit(solution)/shard_map/ppermute | solution.py:407
  5.2 14.3 %collective-permute-start.2 = (bf16[256,512]{1,0:T(8,128)(2,1)}, bf16[256,512]{1,0:T(8,128)(2,1)S(1)}, u32[]{:S(2)}, u32[]{:S(2)}) collective-permute-start(bf16[256,512]{1,0:T(8,128)(2,1)} %bitcast.4), channel_id=1, source_target_pairs={{0,16},{1,17},{2,18},{3,19},{4,20},{5,21},{6,22},{7,23},{8,24},{9,... | collective-permute-start | bytes 786440 | tf_op jit(solution)/shard_map/ppermute | solution.py:407
  7.8 11.7 %collective-permute-start.5 = (bf16[256,512]{1,0:T(8,128)(2,1)}, bf16[256,512]{1,0:T(8,128)(2,1)S(1)}, u32[]{:S(2)}, u32[]{:S(2)}) collective-permute-start(bf16[256,512]{1,0:T(8,128)(2,1)} %bitcast.5), channel_id=1, source_target_pairs={{0,2},{1,3},{2,0},{3,1},{4,6},{5,7},{6,4},{7,5},{8,10},{9,11},{10,... | collective-permute-start | bytes 786440 | tf_op jit(solution)/shard_map/ppermute | solution.py:407
  9.3 1.0 %copy-start = (bf16[1,256,512]{2,1,0:T(8,128)(2,1)S(1)}, bf16[1,256,512]{2,1,0:T(8,128)(2,1)}, u32[]{:S(2)}) copy-start(bf16[1,256,512]{2,1,0:T(8,128)(2,1)} %param.3) | copy-start | bytes 786436
  10.3 0.7 %copy-start.1 = (s32[3,4]{1,0:T(4,128)S(1)}, s32[3,4]{1,0:T(4,128)}, u32[]{:S(2)}) copy-start(s32[3,4]{1,0:T(4,128)} %pairings_ref.1) | copy-start | bytes 148
  11.0 0.7 %copy-start.2 = (f32[3]{0:T(128)S(1)}, f32[3]{0:T(128)}, u32[]{:S(2)}) copy-start(f32[3]{0:T(128)} %scale_ref.1) | copy-start | bytes 40
  12.3 8.6 %collective-permute-start.4 = (bf16[256,512]{1,0:T(8,128)(2,1)S(1)}, bf16[256,512]{1,0:T(8,128)(2,1)S(1)}, u32[]{:S(2)}, u32[]{:S(2)}) collective-permute-start(bf16[256,512]{1,0:T(8,128)(2,1)S(1)} %collective-permute-done.refs_1_.refs_3_), channel_id=1, source_target_pairs={{0,2},{1,3},{2,0},{3,1},{4,6},{5,7},{6,4},{7,5},{8,10},{9,11},{10,... | collective-permute-start | bytes 786440 | tf_op jit(solution)/shard_map/ppermute | solution.py:407
  17.1 6.9 %collective-permute-start.3 = (bf16[256,512]{1,0:T(8,128)(2,1)S(1)}, bf16[256,512]{1,0:T(8,128)(2,1)S(1)}, u32[]{:S(2)}, u32[]{:S(2)}) collective-permute-start(bf16[256,512]{1,0:T(8,128)(2,1)S(1)} %collective-permute-done.1.refs_0_.refs_2_), channel_id=1, source_target_pairs={{0,4},{1,5},{2,6},{3,7},{4,0},{5,1},{6,2},{7,3},{8,12},{9,13},{10,... | collective-permute-start | bytes 786440 | tf_op jit(solution)/shard_map/ppermute | solution.py:407
  19.6 18.4 %collective-permute-start.10 = (bf16[768,512]{1,0:T(8,128)(2,1)S(1)}, bf16[768,512]{1,0:T(8,128)(2,1)S(1)}, u32[]{:S(2)}, u32[]{:S(2)}) collective-permute-start(bf16[768,512]{1,0:T(8,128)(2,1)S(1)} %pack.5), channel_id=1, source_target_pairs={{0,1},{1,0},{2,3},{3,2},{4,5},{5,4},{6,7},{7,6},{8,9},{9,8},{10,11... | collective-permute-start | bytes 2359304 | tf_op jit(solution)/shard_map/ppermute | solution.py:407
  20.9 7.5 %collective-permute-start.6 = (bf16[256,512]{1,0:T(8,128)(2,1)S(1)}, bf16[256,512]{1,0:T(8,128)(2,1)S(1)}, u32[]{:S(2)}, u32[]{:S(2)}) collective-permute-start(bf16[256,512]{1,0:T(8,128)(2,1)S(1)} %collective-permute-done.2.refs_1_.refs_3_), channel_id=1, source_target_pairs={{0,8},{1,9},{2,10},{3,11},{4,12},{5,13},{6,14},{7,15},{8,0},{9,1},... | collective-permute-start | bytes 786440 | tf_op jit(solution)/shard_map/ppermute | solution.py:407
  21.3 8.5 %collective-permute-start.12 = (bf16[256,512]{1,0:T(8,128)(2,1)S(1)}, bf16[256,512]{1,0:T(8,128)(2,1)S(1)}, u32[]{:S(2)}, u32[]{:S(2)}) collective-permute-start(bf16[256,512]{1,0:T(8,128)(2,1)S(1)} %collective-permute-done.2.refs_1_.refs_3_), channel_id=1, source_target_pairs={{0,2},{1,3},{2,0},{3,1},{4,6},{5,7},{6,4},{7,5},{8,10},{9,11},{10,... | collective-permute-start | bytes 786440 | tf_op jit(solution)/shard_map/ppermute | solution.py:407
  24.0 6.9 %collective-permute-start.7 = (bf16[256,512]{1,0:T(8,128)(2,1)S(1)}, bf16[256,512]{1,0:T(8,128)(2,1)S(1)}, u32[]{:S(2)}, u32[]{:S(2)}) collective-permute-start(bf16[256,512]{1,0:T(8,128)(2,1)S(1)} %collective-permute-done.2.refs_1_.refs_3_), channel_id=1, source_target_pairs={{0,4},{1,5},{2,6},{3,7},{4,0},{5,1},{6,2},{7,3},{8,12},{9,13},{10,... | collective-permute-start | bytes 786440 | tf_op jit(solution)/shard_map/ppermute | solution.py:407
  28.4 6.6 %collective-permute-start.11 = (bf16[256,512]{1,0:T(8,128)(2,1)S(1)}, bf16[256,512]{1,0:T(8,128)(2,1)S(1)}, u32[]{:S(2)}, u32[]{:S(2)}) collective-permute-start(bf16[256,512]{1,0:T(8,128)(2,1)S(1)} %collective-permute-done.6.refs_0_.refs_5_), channel_id=1, source_target_pairs={{0,2},{1,3},{2,0},{3,1},{4,6},{5,7},{6,4},{7,5},{8,10},{9,11},{10,... | collective-permute-start | bytes 786440 | tf_op jit(solution)/shard_map/ppermute | solution.py:407
  29.9 6.6 %collective-permute-start.13 = (bf16[256,512]{1,0:T(8,128)(2,1)S(1)}, bf16[256,512]{1,0:T(8,128)(2,1)S(1)}, u32[]{:S(2)}, u32[]{:S(2)}) collective-permute-start(bf16[256,512]{1,0:T(8,128)(2,1)S(1)} %collective-permute-done.5.refs_2_.refs_8_.refs_4_), channel_id=1, source_target_pairs={{0,8},{1,9},{2,10},{3,11},{4,12},{5,13},{6,14},{7,15},{8,0},{9,1},... | collective-permute-start | bytes 786440 | tf_op jit(solution)/shard_map/ppermute | solution.py:407
  30.4 6.8 %collective-permute-start.8 = (bf16[256,512]{1,0:T(8,128)(2,1)S(1)}, bf16[256,512]{1,0:T(8,128)(2,1)S(1)}, u32[]{:S(2)}, u32[]{:S(2)}) collective-permute-start(bf16[256,512]{1,0:T(8,128)(2,1)S(1)} %collective-permute-done.6.refs_0_.refs_5_), channel_id=1, source_target_pairs={{0,4},{1,5},{2,6},{3,7},{4,0},{5,1},{6,2},{7,3},{8,12},{9,13},{10,... | collective-permute-start | bytes 786440 | tf_op jit(solution)/shard_map/ppermute | solution.py:407
  30.9 6.5 %collective-permute-start.9 = (bf16[256,512]{1,0:T(8,128)(2,1)}, bf16[256,512]{1,0:T(8,128)(2,1)S(1)}, u32[]{:S(2)}, u32[]{:S(2)}) collective-permute-start(bf16[256,512]{1,0:T(8,128)(2,1)} %bitcast.6), channel_id=1, source_target_pairs={{0,1},{1,0},{2,3},{3,2},{4,5},{5,4},{6,7},{7,6},{8,9},{9,8},{10,11... | collective-permute-start | bytes 786440 | tf_op jit(solution)/shard_map/ppermute | solution.py:407
  34.9 7.9 %collective-permute-start.16 = (bf16[256,512]{1,0:T(8,128)(2,1)S(1)}, bf16[256,512]{1,0:T(8,128)(2,1)S(1)}, u32[]{:S(2)}, u32[]{:S(2)}) collective-permute-start(bf16[256,512]{1,0:T(8,128)(2,1)S(1)} %collective-permute-done.7.refs_4_.refs_6_), channel_id=1, source_target_pairs={{0,2},{1,3},{2,0},{3,1},{4,6},{5,7},{6,4},{7,5},{8,10},{9,11},{10,... | collective-permute-start | bytes 786440 | tf_op jit(solution)/shard_map/ppermute | solution.py:407
  36.4 6.4 %collective-permute-start.15 = (bf16[256,512]{1,0:T(8,128)(2,1)S(1)}, bf16[256,512]{1,0:T(8,128)(2,1)S(1)}, u32[]{:S(2)}, u32[]{:S(2)}) collective-permute-start(bf16[256,512]{1,0:T(8,128)(2,1)S(1)} %collective-permute-done.4.refs_1_.refs_5_.refs_2_), channel_id=1, source_target_pairs={{0,8},{1,9},{2,10},{3,11},{4,12},{5,13},{6,14},{7,15},{8,0},{9,1},... | collective-permute-start | bytes 786440 | tf_op jit(solution)/shard_map/ppermute | solution.py:407
  37.4 5.8 %collective-permute-start.14 = (bf16[1792,512]{1,0:T(8,128)(2,1)S(1)}, bf16[1792,512]{1,0:T(8,128)(2,1)S(1)}, u32[]{:S(2)}, u32[]{:S(2)}) collective-permute-start(bf16[1792,512]{1,0:T(8,128)(2,1)S(1)} %pack.6), channel_id=1, source_target_pairs={{0,1},{1,0},{2,3},{3,2},{4,5},{5,4},{6,7},{7,6},{8,9},{9,8},{10,11... | collective-permute-start | bytes 5505032 | tf_op jit(solution)/shard_map/ppermute | solution.py:407
  37.4 8.7 %collective-permute-start.18 = (bf16[256,512]{1,0:T(8,128)(2,1)S(1)}, bf16[256,512]{1,0:T(8,128)(2,1)S(1)}, u32[]{:S(2)}, u32[]{:S(2)}) collective-permute-start(bf16[256,512]{1,0:T(8,128)(2,1)S(1)} %collective-permute-done.11.refs_3_.refs_11_.refs_10_), channel_id=1, source_target_pairs={{0,4},{1,5},{2,6},{3,7},{4,0},{5,1},{6,2},{7,3},{8,12},{9,13},{10,... | collective-permute-start | bytes 786440 | tf_op jit(solution)/shard_map/ppermute | solution.py:407
  43.0 4.9 %collective-permute-start.17 = (bf16[1024,512]{1,0:T(8,128)(2,1)S(1)}, bf16[1024,512]{1,0:T(8,128)(2,1)S(1)}, u32[]{:S(2)}, u32[]{:S(2)}) collective-permute-start(bf16[1024,512]{1,0:T(8,128)(2,1)S(1)} %pack.7), channel_id=1, source_target_pairs={{0,1},{1,0},{2,3},{3,2},{4,5},{5,4},{6,7},{7,6},{8,9},{9,8},{10,11... | collective-permute-start | bytes 3145736 | tf_op jit(solution)/shard_map/ppermute | solution.py:407
  46.2 1.7 %collective-permute-start.19 = (bf16[256,512]{1,0:T(8,128)(2,1)S(1)}, bf16[256,512]{1,0:T(8,128)(2,1)S(1)}, u32[]{:S(2)}, u32[]{:S(2)}) collective-permute-start(bf16[256,512]{1,0:T(8,128)(2,1)S(1)} %collective-permute-done.18.refs_11_.refs_5_), channel_id=1, source_target_pairs={{0,1},{1,0},{2,3},{3,2},{4,5},{5,4},{6,7},{7,6},{8,9},{9,8},{10,11... | collective-permute-start | bytes 786440 | tf_op jit(solution)/shard_map/ppermute | solution.py:407
  46.3 5.9 %collective-permute-start.20 = (f32[12,1,256]{2,1,0:T(1,128)S(1)}, f32[12,1,256]{2,1,0:T(1,128)S(1)}, u32[]{:S(2)}, u32[]{:S(2)}) collective-permute-start(f32[12,1,256]{2,1,0:T(1,128)S(1)} %col_stats.3.lse_ref), channel_id=1, source_target_pairs={{0,4},{1,5},{2,6},{3,7},{4,0},{5,1},{6,2},{7,3},{8,12},{9,13},{10,... | collective-permute-start | bytes 36872 | tf_op jit(solution)/shard_map/ppermute | solution.py:407
